TPU v7x, 32 devices: a whole 2x2x4 slice. The times are simulated.
32 devices in a mesh: pitch: 8 (over z, x), span: 4 (over y, core).
Axes of the slice: x: 2, y: 2, z: 4, core: 2. Of those that a mesh axis runs over, the one named last changes fastest.
Arguments:
- stator_state: float32 [5, 16, 256, 2048], P(None, None, 'span', 'pitch'), may hold values from -6 to 6
- rotor_state: float32 [5, 16, 256, 2048], P(None, None, 'span', 'pitch'), may hold values from -6 to 6
- jacobians: float32 [3, 5, 5], replicated, may hold values from -2.5 to 2.5
- field_mix: float32 [5, 5], replicated, may hold values from -2.5 to 2.5
- mode_blend: float32 [5, 2048], replicated, may hold values from 0.1 to 0.9
- rotor_offset: int32 [1], replicated, may hold values from 0 to 2047
Outputs:
- stator_next: float32 [5, 16, 256, 2048], P(None, None, 'span', 'pitch')
- rotor_next: float32 [5, 16, 256, 2048], P(None, None, 'span', 'pitch')
Inputs may be any that keep to these rules, and one draw needn't show every extreme that they name: `rotor_offset`: the rotor's rotation against the stator, in whole pitch cells.
All inputs are finite; a program needn't handle non-finite values.
Results may differ from a plain program's by a relative error of at most 0.0001.
Values sent between devices are 32-bit elements; how exact they have to be, the bound alone decides.
No kernel may reach another device: no remote copies, remote signals or barrier semaphores. Data moves between devices by JAX's collectives and lax.ppermute only.
A program may use at most 192 MiB of HBM per device.

v0:
```python
import math

import jax
import jax.numpy as jnp
from jax import lax
from jax.sharding import PartitionSpec as P

NP = 2048


time_step = 0.5
damping = 1.0 / 32.0
highest = lax.Precision.HIGHEST


def padded_2(block, sides, width):
    for axis, dim in sides:
        count = lax.axis_size(axis)
        forward = [(i, i + 1) for i in range(count - 1)]
        forward.append((count - 1, 0))
        backward = [(target, source) for source, target in forward]
        low = lax.ppermute(
            lax.slice_in_dim(block, block.shape[dim] - width, None, axis=dim), axis, forward
        )
        high = lax.ppermute(lax.slice_in_dim(block, 0, width, axis=dim), axis, backward)
        block = jnp.concatenate([low, block, high], axis=dim)
    return block


def hartley_table(row_ids, col_ids, offset):
    products = (row_ids[:, None] + offset) % NP * col_ids[None, :] % NP
    angles = products.astype(jnp.float32) * (2.0 * math.pi / NP)
    return jnp.cos(angles) + jnp.sin(angles)


def contract_last(left, right):
    return lax.dot_general(
        left, right, (((1,), (1,)), ((), ())), precision=highest, preferred_element_type=jnp.float32
    )


def close_span(padded):
    span_pos = lax.axis_index("span")
    last_span = lax.axis_size("span") - 1
    lower_keep = jnp.where(span_pos == 0, 0.0, 1.0)
    upper_keep = jnp.where(span_pos == last_span, 0.0, 1.0)
    extent = padded.shape[2]
    indices = jnp.arange(extent, dtype=jnp.int32)
    rim_scale = jnp.where(
        indices < 2, lower_keep, jnp.where(indices >= extent - 2, upper_keep, 1.0)
    )
    return padded * rim_scale[None, None, :, None]


def update_block(state, extended, jacobians):
    centre = extended[:, 2:-2, 2:-2, 2:-2]
    neighbours = (
        (
            extended[:, 3:-1, 2:-2, 2:-2],
            extended[:, 1:-3, 2:-2, 2:-2],
            extended[:, 4:, 2:-2, 2:-2],
            extended[:, :-4, 2:-2, 2:-2],
        ),
        (
            extended[:, 2:-2, 3:-1, 2:-2],
            extended[:, 2:-2, 1:-3, 2:-2],
            extended[:, 2:-2, 4:, 2:-2],
            extended[:, 2:-2, :-4, 2:-2],
        ),
        (
            extended[:, 2:-2, 2:-2, 3:-1],
            extended[:, 2:-2, 2:-2, 1:-3],
            extended[:, 2:-2, 2:-2, 4:],
            extended[:, 2:-2, 2:-2, :-4],
        ),
    )
    slopes = []
    smoothing = jnp.zeros_like(centre)
    for plus_one, minus_one, plus_two, minus_two in neighbours:
        slopes.append(0.5 * (plus_one - minus_one))
        smoothing = smoothing + (
            plus_two - 4.0 * plus_one + 6.0 * centre - 4.0 * minus_one + minus_two
        )
    changes = []
    for target in range(state.shape[0]):
        totals = -damping * smoothing[target]
        for course in range(3):
            for source in range(state.shape[0]):
                totals = totals - jacobians[course, target, source] * slopes[course][source]
        changes.append(totals)
    return state + time_step * jnp.stack(changes)


def shards(stator_state, rotor_state, jacobians, field_mix, mode_blend, rotor_offset):
    fields, axial_cells, span_rows, pitch_cells = stator_state.shape
    offset = rotor_offset[0]
    position = lax.axis_index("pitch")
    stator_planes = jnp.stack(
        [stator_state[:, axial_cells - 1], stator_state[:, axial_cells - 2]], axis=0
    )
    rotor_planes = jnp.stack([rotor_state[:, 0], rotor_state[:, 1]], axis=0)
    planes = jnp.stack([stator_planes, rotor_planes], axis=0)
    plane_rows = 2 * fields * span_rows
    stacked = planes.reshape(2, plane_rows, pitch_cells)
    mode_index = jnp.arange(NP, dtype=jnp.int32)
    my_range = position * pitch_cells + jnp.arange(pitch_cells, dtype=jnp.int32)
    piece_rows = lax.all_gather(stacked, "pitch", axis=2, tiled=True)
    amount = piece_rows.shape[2]
    angles = jnp.arange(amount, dtype=jnp.int32)
    stator_matrix = hartley_table(angles, mode_index, 0)
    rotor_matrix = hartley_table(angles, mode_index, offset)
    stator_modes = jnp.dot(
        piece_rows[0], stator_matrix, precision=highest, preferred_element_type=jnp.float32
    )
    rotor_modes = jnp.dot(
        piece_rows[1], rotor_matrix, precision=highest, preferred_element_type=jnp.float32
    )
    blend = mode_blend[None, :, None, :]
    stator_modes = stator_modes.reshape(2, fields, span_rows, NP)
    rotor_modes = rotor_modes.reshape(2, fields, span_rows, NP)
    stator_blend = (blend * rotor_modes + (1.0 - blend) * stator_modes).reshape(plane_rows, NP)
    rotor_blend = (blend * stator_modes + (1.0 - blend) * rotor_modes).reshape(plane_rows, NP)
    stator_back = contract_last(stator_blend, hartley_table(my_range, mode_index, 0)) / NP
    rotor_back = contract_last(rotor_blend, hartley_table(my_range, mode_index, offset)) / NP
    inverse = jnp.stack([stator_back, rotor_back]).reshape(2, 2, fields, span_rows, pitch_cells)
    ghosts = jnp.einsum("fg,slgrp->slfrp", field_mix, inverse, precision=highest)
    stator_ghost = jnp.moveaxis(ghosts[0], 0, 1)
    rotor_ghost = jnp.moveaxis(ghosts[1], 0, 1)[:, ::-1]
    ghost_pads = ((0, 0), (0, 0), (2, 2), (2, 2))
    no_inflow = jnp.zeros((fields, 2, span_rows + 4, pitch_cells + 4), jnp.float32)
    stator_padded = close_span(padded_2(stator_state, (("pitch", 3), ("span", 2)), 2))
    rotor_padded = close_span(padded_2(rotor_state, (("pitch", 3), ("span", 2)), 2))
    stator_ext = jnp.concatenate(
        [no_inflow, stator_padded, jnp.pad(stator_ghost, ghost_pads)], axis=1
    )
    rotor_ext = jnp.concatenate([jnp.pad(rotor_ghost, ghost_pads), rotor_padded, no_inflow], axis=1)
    return (
        update_block(stator_state, stator_ext, jacobians),
        update_block(rotor_state, rotor_ext, jacobians),
    )


def solution(mesh):
    in_specs = (P(None, None, "span", "pitch"), P(None, None, "span", "pitch"), P(), P(), P(), P())
    out_specs = (P(None, None, "span", "pitch"), P(None, None, "span", "pitch"))
    return jax.shard_map(shards, mesh=mesh, in_specs=in_specs, out_specs=out_specs, check_vma=False)
```

profile of v0, /device:TPU:0, one launch (start us, length us, event | category | flops | bytes accessed | tf_op | source)
XLA Modules:
  0.0 647.2 jit_solution(8685880434663515810)
XLA Ops:
  7.2 1.1 slice_bitcast_fusion.5
  9.6 1.2 pad_maximum_fusion
  10.8 4.9 fusion.293
  15.6 2.6 copy.37
  18.2 3.0 collective-permute-start
  22.0 3.1 collective-permute-start.1
  25.1 5.0 fusion.292
  30.1 2.6 copy.41
  33.6 4.7 collective-permute-start.5
  41.2 69.5 %fusion.306 = f32[2048,2048,1,1]{1,0,3,2:T(8,128)} fusion(s32[2048]{0:T(1024)S(1)} %add_select_fusion.5), kind=kLoop, calls=%fused_computation.15.clone.1 | loop fusion | flops 62914560 | bytes 16785408 | tf_op jit(solution)/shard_map/dot_general | solution.py:115
  110.8 69.8 %fusion.7.clone.4 = f32[2048,2048,1,1]{1,0,3,2:T(8,128)} fusion(s32[2048]{0:T(1024)S(1)} %add_select_fusion.4), kind=kLoop, calls=%fused_computation.13.clone.clone.clone.1 | loop fusion | flops 62914560 | bytes 16785408 | tf_op jit(solution)/shard_map/add | solution.py:121
  180.6 5.3 copy.24
  186.0 5.3 copy.31
  191.3 1.2 copy.16
  192.5 2.5 copy.18
  195.1 1.3 pad_maximum_fusion.8
  196.5 1.7 collective-permute-start.3
  198.2 2.5 copy.27
  200.7 3.5 copy.29
  204.2 1.5 pad_maximum_fusion.5
  205.9 1.7 collective-permute-start.7
  208.3 3.7 collective-permute-done.6
  212.0 1.3 collective-permute-done.7
  213.3 14.6 %maximum_multiply_fusion.1 = (f32[5,16,68,260]{3,1,2,0:T(8,128)}, f32[5,16,68,260]{3,1,2,0:T(8,128)}) fusion(f32[5,16,2,260]{3,1,2,0:T(8,128)S(1)} %collective-permute-done.7, f32[5,16,64,2]{3,1,2,0:T(8,128)} %copy.29, f32[5,16,64,256]{3,1,2,0:T(8,128)} %copy.31, f32[5,16,64,2]{3,1,2,0:T(8,128)} %copy.27, f32[5,16,2,260]{3,1,2,0:T(8,128)S(1)} %collective-permute-done.6, ...), kind=kLoop, calls=%fused_computation.47 | loop fusion | flops 14144000 | bytes 22630672 | tf_op jit(solution)/shard_map/mul | solution.py:52
  227.9 7.7 %fusion.291 = (f32[1,640,2048]{2,1,0:T(8,128)S(1)}, f32[1,640,2048]{2,1,0:T(8,128)}) fusion(f32[2,640,2048]{2,1,0:T(8,128)} %all-gather.2.cloned.1.call-done), kind=kLoop, calls=%fused_computation.358 | loop fusion | bytes 20971520 | tf_op jit(solution)/shard_map/slice | solution.py:113
  235.6 39.4 %fusion.8 = f32[2,5,64,2048]{3,2,1,0:T(8,128)} fusion(f32[2,5,64,2048]{3,2,1,0:T(8,128)} %bitcast.160, f32[2048,2048,1,1]{1,0,3,2:T(8,128)} %fusion.306), kind=kOutput, calls=%fused_computation.14 | convolution fusion | flops 32212254720 | bytes 27262976 | tf_op jit(solution)/shard_map/dot_general | solution.py:115
  275.0 37.6 %multiply_add_fusion.3 = (f32[2,5,64,2048]{3,2,1,0:T(8,128)}, f32[2,5,64,2048]{3,2,1,0:T(8,128)}) fusion(f32[2,5,64,2048]{3,2,1,0:T(8,128)} %fusion.8, f32[5,2048]{1,0:T(8,128)S(1)} %broadcast_subtract_fusion, f32[5,2048]{1,0:T(8,128)S(1)} %copy-done.12, f32[2,5,64,2048]{3,2,1,0:T(8,128)S(1)} %bitcast.153, f32[2048,2048,1,1]{1,0,3,2:T(8,128)S(1)} %bitcast.142), kind=kOutput, calls=%fused_computation.87 | convolution fusion | flops 32220119040 | bytes 37830656 | tf_op jit(solution)/shard_map/dot_general | solution.py:112
  312.6 15.6 %fusion.88 = f32[640,256]{1,0:T(8,128)S(1)} fusion(f32[640,2048]{1,0:T(8,128)} %bitcast.159, s32[256]{0:T(256)S(1)} %get-tuple-element.108), kind=kOutput, calls=%fused_computation.120 | convolution fusion | flops 4034560000 | bytes 5899264 | tf_op jit(solution)/shard_map/dot_general | solution.py:37
  328.5 12.7 %fusion.91 = f32[640,256]{1,0:T(8,128)S(1)} fusion(f32[640,2048]{1,0:T(8,128)S(1)} %bitcast.158, s32[256]{0:T(256)S(1)} %get-tuple-element.107), kind=kOutput, calls=%fused_computation.121 | convolution fusion | flops 4034560000 | bytes 5899264 | tf_op jit(solution)/shard_map/dot_general | solution.py:37
  341.7 2.0 fusion.85
  344.4 9.5 %select_maximum_fusion = f32[5,18,68,260]{3,1,2,0:T(8,128)} fusion(f32[5,2,64,256]{3,1,2,0:T(2,128)S(1)} %copy.44, f32[5,16,68,260]{3,1,2,0:T(8,128)} %get-tuple-element.105), kind=kLoop, calls=%fused_computation.32 | loop fusion | flops 4773600 | bytes 12677760 | tf_op jit(solution)/shard_map/concatenate | solution.py:136
  353.8 57.2 %subtract_multiply_fusion.2 = (f32[5,16,64,256]{3,1,2,0:T(8,128)}, f32[5,16,64,256]{3,1,2,0:T(8,128)}, f32[5,16,64,256]{3,1,2,0:T(8,128)}, f32[5,16,64,256]{3,1,2,0:T(8,128)}) fusion(f32[5,18,68,260]{3,1,2,0:T(8,128)} %select_maximum_fusion, f32[5,16,68,260]{3,1,2,0:T(8,128)} %get-tuple-element.105), kind=kLoop, calls=%fused_computation.81 | loop fusion | flops 35389440 | bytes 86999040 | tf_op jit(solution)/shard_map/mul | solution.py:80
  411.1 20.2 %fusion.173 = f32[5,16,64,256]{3,1,2,0:T(8,128)} fusion(f32[5,16,64,256]{3,1,2,0:T(8,128)} %get-tuple-element.5, f32[5,16,64,256]{3,1,2,0:T(8,128)} %get-tuple-element.17, f32[5,16,64,256]{3,1,2,0:T(8,128)} %get-tuple-element.16, f32[5,16,64,256]{3,1,2,0:T(8,128)} %get-tuple-element.4, f32[]{:T(128)} %bitcast.36, f32[]{:T(128)} %bitcast.35, f32[]{:T(128)} %bitcast.34, ...), kind=kLoop, calls=%fused_computation.206 | loop fusion | flops 8126463 | bytes 17825852
  431.3 13.4 %fusion.157 = f32[5,16,64,256]{3,1,2,0:T(8,128)} fusion(f32[5,16,64,256]{3,1,2,0:T(8,128)} %fusion.173, f32[5,16,64,256]{3,1,2,0:T(8,128)} %get-tuple-element.5, f32[5,16,64,256]{3,1,2,0:T(8,128)S(1)} %copy-done.7, f32[5,16,64,256]{3,1,2,0:T(8,128)S(1)} %copy-done.6, f32[5,16,64,256]{3,1,2,0:T(8,128)S(1)} %copy-done.5, f32[]{:T(128)} %bitcast.51, ...), kind=kLoop, calls=%fused_computation.189 | loop fusion | flops 8126464 | bytes 17833472
  444.7 12.3 %fusion.141 = f32[5,16,64,256]{3,1,2,0:T(8,128)} fusion(f32[5,16,64,256]{3,1,2,0:T(8,128)} %fusion.157, f32[5,16,64,256]{3,1,2,0:T(8,128)S(1)} %bitcast.157, f32[5,16,64,256]{3,1,2,0:T(8,128)S(1)} %copy-done.7, f32[5,16,64,256]{3,1,2,0:T(8,128)S(1)} %copy-done.6, f32[5,16,64,256]{3,1,2,0:T(8,128)S(1)} %copy-done.5, f32[]{:T(128)} %bitcast.66, f32[]{:T(128)} %bitcast.65, ...), kind=kLoop, calls=%fused_computation.172 | loop fusion | flops 8126464 | bytes 17833472
  457.0 12.8 %fusion.125 = f32[5,16,64,256]{3,1,2,0:T(8,128)} fusion(f32[5,16,64,256]{3,1,2,0:T(8,128)} %fusion.141, f32[5,16,64,256]{3,1,2,0:T(8,128)S(1)} %bitcast.157, f32[5,16,64,256]{3,1,2,0:T(8,128)S(1)} %copy-done.7, f32[5,16,64,256]{3,1,2,0:T(8,128)S(1)} %copy-done.6, f32[5,16,64,256]{3,1,2,0:T(8,128)S(1)} %copy-done.5, f32[]{:T(128)} %bitcast.81, f32[]{:T(128)} %bitcast.80, ...), kind=kLoop, calls=%fused_computation.155 | loop fusion | flops 8126464 | bytes 17833472
  469.8 13.1 %fusion.109 = f32[5,16,64,256]{3,1,2,0:T(8,128)} fusion(f32[5,16,64,256]{3,1,2,0:T(8,128)} %fusion.125, f32[5,16,64,256]{3,1,2,0:T(8,128)S(1)} %bitcast.157, f32[5,16,64,256]{3,1,2,0:T(8,128)S(1)} %copy-done.7, f32[5,16,64,256]{3,1,2,0:T(8,128)S(1)} %copy-done.6, f32[5,16,64,256]{3,1,2,0:T(8,128)S(1)} %copy-done.5, f32[]{:T(128)} %bitcast.96, f32[]{:T(128)} %bitcast.95, ...), kind=kLoop, calls=%fused_computation.138 | loop fusion | flops 8126464 | bytes 17833472 | tf_op jit(solution)/shard_map/stack | solution.py:91
  483.0 8.5 %multiply_add_fusion = f32[5,16,64,256]{3,1,2,0:T(8,128)} fusion(f32[5,16,64,256]{3,1,2,0:T(8,128)} %fusion.109, f32[5,16,64,256]{3,2,1,0:T(8,128)S(1)} %bitcast.146), kind=kLoop, calls=%fused_computation.78 | loop fusion | flops 2621440 | bytes 15728640 | tf_op jit(solution)/shard_map/add | solution.py:91
  491.5 7.8 %copy.33 = f32[5,16,64,256]{3,2,1,0:T(8,128)} copy(f32[5,16,64,256]{3,1,2,0:T(8,128)} %multiply_add_fusion) | data formatting | bytes 10485760
  499.9 6.3 select_maximum_fusion.1
  506.1 57.8 %subtract_multiply_fusion.5 = (f32[5,16,64,256]{3,1,2,0:T(8,128)}, f32[5,16,64,256]{3,1,2,0:T(8,128)}, f32[5,16,64,256]{3,1,2,0:T(8,128)}, f32[5,16,64,256]{3,1,2,0:T(8,128)}) fusion(f32[5,18,68,260]{3,1,2,0:T(8,128)} %select_maximum_fusion.1, f32[5,16,68,260]{3,1,2,0:T(8,128)} %get-tuple-element.106), kind=kLoop, calls=%fused_computation.85 | loop fusion | flops 35389440 | bytes 86999040 | tf_op jit(solution)/shard_map/mul | solution.py:80
  563.9 19.0 %fusion.253 = f32[5,16,64,256]{3,1,2,0:T(8,128)S(1)} fusion(f32[5,16,64,256]{3,1,2,0:T(8,128)} %get-tuple-element.7, f32[5,16,64,256]{3,1,2,0:T(8,128)} %get-tuple-element.19, f32[5,16,64,256]{3,1,2,0:T(8,128)} %get-tuple-element.18, f32[5,16,64,256]{3,1,2,0:T(8,128)} %get-tuple-element.6, f32[]{:T(128)} %bitcast.36, f32[]{:T(128)} %bitcast.35, ...), kind=kLoop, calls=%fused_computation.292 | loop fusion | flops 8126463 | bytes 17825852
  583.0 12.7 %fusion.237 = f32[5,16,64,256]{3,1,2,0:T(8,128)S(1)} fusion(f32[5,16,64,256]{3,1,2,0:T(8,128)S(1)} %fusion.253, f32[5,16,64,256]{3,1,2,0:T(8,128)} %get-tuple-element.7, f32[5,16,64,256]{3,1,2,0:T(8,128)S(1)} %copy-done.4, f32[5,16,64,256]{3,1,2,0:T(8,128)S(1)} %copy-done.3, f32[5,16,64,256]{3,1,2,0:T(8,128)S(1)} %copy-done.2, f32[]{:T(128)} %bitcast.51, ...), kind=kLoop, calls=%fused_computation.275 | loop fusion | flops 8126464 | bytes 17825852
  595.7 11.6 %fusion.221 = f32[5,16,64,256]{3,1,2,0:T(8,128)S(1)} fusion(f32[5,16,64,256]{3,1,2,0:T(8,128)S(1)} %fusion.237, f32[5,16,64,256]{3,1,2,0:T(8,128)S(1)} %bitcast.155, f32[5,16,64,256]{3,1,2,0:T(8,128)S(1)} %copy-done.4, f32[5,16,64,256]{3,1,2,0:T(8,128)S(1)} %copy-done.3, f32[5,16,64,256]{3,1,2,0:T(8,128)S(1)} %copy-done.2, f32[]{:T(128)} %bitcast.66, ...), kind=kLoop, calls=%fused_computation.258 | loop fusion | flops 8126464 | bytes 17825852
  607.3 12.0 %fusion.205 = f32[5,16,64,256]{3,1,2,0:T(8,128)S(1)} fusion(f32[5,16,64,256]{3,1,2,0:T(8,128)S(1)} %fusion.221, f32[5,16,64,256]{3,1,2,0:T(8,128)S(1)} %bitcast.155, f32[5,16,64,256]{3,1,2,0:T(8,128)S(1)} %copy-done.4, f32[5,16,64,256]{3,1,2,0:T(8,128)S(1)} %copy-done.3, f32[5,16,64,256]{3,1,2,0:T(8,128)S(1)} %copy-done.2, f32[]{:T(128)} %bitcast.81, ...), kind=kLoop, calls=%fused_computation.241 | loop fusion | flops 8126464 | bytes 17825852
  619.3 11.9 %fusion.189 = f32[5,16,64,256]{3,1,2,0:T(8,128)S(1)} fusion(f32[5,16,64,256]{3,1,2,0:T(8,128)S(1)} %fusion.205, f32[5,16,64,256]{3,1,2,0:T(8,128)S(1)} %bitcast.155, f32[5,16,64,256]{3,1,2,0:T(8,128)S(1)} %copy-done.4, f32[5,16,64,256]{3,1,2,0:T(8,128)S(1)} %copy-done.3, f32[5,16,64,256]{3,1,2,0:T(8,128)S(1)} %copy-done.2, f32[]{:T(128)} %bitcast.96, ...), kind=kLoop, calls=%fused_computation.224 | loop fusion | flops 8126464 | bytes 17825852 | tf_op jit(solution)/shard_map/stack | solution.py:91
  631.3 3.5 multiply_add_fusion.1
  634.8 5.3 copy.32
  (109 shorter events, 8.3 us)
Async XLA Ops:
  7.2 334.5 %copy-start = (f32[5,5]{1,0:T(8,128)S(1)}, f32[5,5]{1,0:T(8,128)}, u32[]{:S(2)}) copy-start(f32[5,5]{1,0:T(8,128)} %param.9) | copy-start | bytes 304
  7.2 220.7 %all-gather.2.cloned.1.call-start = ((), (), s32[]{:S(2)}) async-start(), calls=%async_computation | async-start | bytes 11796480 | tf_op jit(solution)/shard_map/all_gather | solution.py:107
  18.2 173.1 %collective-permute-start = (f32[5,16,64,2]{2,1,3,0:T(8,128)S(1)}, f32[5,16,64,2]{2,1,3,0:T(8,128)S(1)}, u32[]{:S(2)}, u32[]{:S(2)}) collective-permute-start(f32[5,16,64,2]{2,1,3,0:T(8,128)S(1)} %copy.37), channel_id=1, source_target_pairs={{0,4},{4,8},{8,12},{12,16},{16,20},{20,24},{24,28},{28,0},{1,5},{5... | collective-permute-start | bytes 122888 | tf_op jit(solution)/shard_map/ppermute | solution.py:22
  22.0 170.5 %collective-permute-start.1 = (f32[5,16,64,2]{2,1,3,0:T(8,128)S(1)}, f32[5,16,64,2]{2,1,3,0:T(8,128)S(1)}, u32[]{:S(2)}, u32[]{:S(2)}) collective-permute-start(f32[5,16,64,2]{2,1,3,0:T(8,128)S(1)} %copy.38), channel_id=1, source_target_pairs={{4,0},{8,4},{12,8},{16,12},{20,16},{24,20},{28,24},{0,28},{5,1},{9... | collective-permute-start | bytes 122888 | tf_op jit(solution)/shard_map/ppermute | solution.py:25
  30.1 8.9 %copy-start.13 = (f32[3,5,5]{2,0,1:T(4,128)S(1)}, f32[3,5,5]{2,0,1:T(4,128)}, u32[]{:S(2)}) copy-start(f32[3,5,5]{2,0,1:T(4,128)} %param.8) | copy-start | bytes 904
  30.1 11.1 %copy-start.12 = (f32[5,2048]{1,0:T(8,128)S(1)}, f32[5,2048]{1,0:T(8,128)}, u32[]{:S(2)}) copy-start(f32[5,2048]{1,0:T(8,128)} %param.10) | copy-start | bytes 122884
  32.7 165.5 %collective-permute-start.4 = (f32[5,16,64,2]{2,1,3,0:T(8,128)S(1)}, f32[5,16,64,2]{2,1,3,0:T(8,128)S(1)}, u32[]{:S(2)}, u32[]{:S(2)}) collective-permute-start(f32[5,16,64,2]{2,1,3,0:T(8,128)S(1)} %copy.41), channel_id=1, source_target_pairs={{0,4},{4,8},{8,12},{12,16},{16,20},{20,24},{24,28},{28,0},{1,5},{5... | collective-permute-start | bytes 122888 | tf_op jit(solution)/shard_map/ppermute | solution.py:22
  33.6 167.1 %collective-permute-start.5 = (f32[5,16,64,2]{2,1,3,0:T(8,128)S(1)}, f32[5,16,64,2]{2,1,3,0:T(8,128)}, u32[]{:S(2)}, u32[]{:S(2)}) collective-permute-start(f32[5,16,64,2]{2,1,3,0:T(8,128)S(1)} %copy.42), channel_id=1, source_target_pairs={{4,0},{8,4},{12,8},{16,12},{20,16},{24,20},{28,24},{0,28},{5,1},{9... | collective-permute-start | bytes 122888 | tf_op jit(solution)/shard_map/ppermute | solution.py:25
  41.2 139.4 %slice-start.10 = ((s8[5242880]{0:T(1024)(128)(4,1)}), s8[4194304]{0:T(1024)(128)(4,1)S(1)}, s32[]{:S(2)}) async-start(s8[5242880]{0:T(1024)(128)(4,1)} %bitcast.147), calls=%async_computation.11 | async-start | bytes 8388608
  41.2 144.8 %slice-start.6 = ((s8[5242880]{0:T(1024)(128)(4,1)}), s8[4194304]{0:T(1024)(128)(4,1)S(1)}, s32[]{:S(2)}) async-start(s8[5242880]{0:T(1024)(128)(4,1)} %bitcast.143), calls=%async_computation.7 | async-start | bytes 8388608
  110.8 69.9 %slice-start.11 = ((s8[5242880]{0:T(1024)(128)(4,1)}), s8[1048576]{0:T(1024)(128)(4,1)S(1)}, s32[]{:S(2)}) async-start(s8[5242880]{0:T(1024)(128)(4,1)} %bitcast.147), calls=%async_computation.12 | async-start | bytes 2097152
  110.8 75.2 %slice-start.7 = ((s8[5242880]{0:T(1024)(128)(4,1)}), s8[1048576]{0:T(1024)(128)(4,1)S(1)}, s32[]{:S(2)}) async-start(s8[5242880]{0:T(1024)(128)(4,1)} %bitcast.143), calls=%async_computation.8 | async-start | bytes 2097152
  192.5 3.9 copy-start.8
  196.4 11.9 %collective-permute-start.2 = (f32[5,16,2,260]{3,1,2,0:T(8,128)S(1)}, f32[5,16,2,260]{3,1,2,0:T(8,128)S(1)}, u32[]{:S(2)}, u32[]{:S(2)}) collective-permute-start(f32[5,16,2,260]{3,1,2,0:T(8,128)S(1)} %get-tuple-element.14), channel_id=1, source_target_pairs={{0,1},{1,2},{2,3},{3,0},{4,5},{5,6},{6,7},{7,4},{8,9},{9,10},{10,1... | collective-permute-start | bytes 499208 | tf_op jit(solution)/shard_map/ppermute | solution.py:22
  196.5 11.8 %collective-permute-start.3 = (f32[5,16,2,260]{3,1,2,0:T(8,128)S(1)}, f32[5,16,2,260]{3,1,2,0:T(8,128)S(1)}, u32[]{:S(2)}, u32[]{:S(2)}) collective-permute-start(f32[5,16,2,260]{3,1,2,0:T(8,128)S(1)} %get-tuple-element.15), channel_id=1, source_target_pairs={{1,0},{2,1},{3,2},{0,3},{5,4},{6,5},{7,6},{4,7},{9,8},{10,9},{11,1... | collective-permute-start | bytes 499208 | tf_op jit(solution)/shard_map/ppermute | solution.py:25
  200.7 12.6 %slice-start.14 = ((s8[5242880]{0:T(1024)(128)(4,1)}), s8[1048576]{0:T(1024)(128)(4,1)S(1)}, s32[]{:S(2)}) async-start(s8[5242880]{0:T(1024)(128)(4,1)} %bitcast.151), calls=%async_computation.15 | async-start | bytes 2097152
  204.2 9.1 %slice-start.15 = ((s8[5242880]{0:T(1024)(128)(4,1)}), s8[4194304]{0:T(1024)(128)(4,1)S(1)}, s32[]{:S(2)}) async-start(s8[5242880]{0:T(1024)(128)(4,1)} %bitcast.151), calls=%async_computation.16 | async-start | bytes 8388608
  204.2 9.1 %copy-start.9 = (f32[5,16,64,2]{3,1,2,0:T(8,128)S(1)}, f32[5,16,64,2]{3,1,2,0:T(8,128)}, u32[]{:S(2)}) copy-start(f32[5,16,64,2]{3,1,2,0:T(8,128)} %copy-done.8) | copy-start | bytes 122884
  204.2 9.1 %copy-start.10 = (f32[5,16,64,2]{3,1,2,0:T(8,128)S(1)}, f32[5,16,64,2]{3,1,2,0:T(8,128)}, u32[]{:S(2)}) copy-start(f32[5,16,64,2]{3,1,2,0:T(8,128)} %copy.18) | copy-start | bytes 122884
  205.8 6.2 collective-permute-start.6
  205.9 7.4 %collective-permute-start.7 = (f32[5,16,2,260]{3,1,2,0:T(8,128)S(1)}, f32[5,16,2,260]{3,1,2,0:T(8,128)S(1)}, u32[]{:S(2)}, u32[]{:S(2)}) collective-permute-start(f32[5,16,2,260]{3,1,2,0:T(8,128)S(1)} %get-tuple-element.11), channel_id=1, source_target_pairs={{1,0},{2,1},{3,2},{0,3},{5,4},{6,5},{7,6},{4,7},{9,8},{10,9},{11,1... | collective-permute-start | bytes 499208 | tf_op jit(solution)/shard_map/ppermute | solution.py:25
  235.6 39.4 %slice-start.2 = ((s8[16777216]{0:T(1024)(128)(4,1)}), s8[4194304]{0:T(1024)(128)(4,1)S(1)}, s32[]{:S(2)}) async-start(s8[16777216]{0:T(1024)(128)(4,1)} %bitcast.141), calls=%async_computation.3 | async-start | bytes 8388608
  235.6 39.4 %slice-start.3 = ((s8[16777216]{0:T(1024)(128)(4,1)}), s8[4194304]{0:T(1024)(128)(4,1)S(1)}, s32[]{:S(2)}) async-start(s8[16777216]{0:T(1024)(128)(4,1)} %bitcast.141), calls=%async_computation.4 | async-start | bytes 8388608
  235.6 39.4 %slice-start.4 = ((s8[16777216]{0:T(1024)(128)(4,1)}), s8[4194304]{0:T(1024)(128)(4,1)S(1)}, s32[]{:S(2)}) async-start(s8[16777216]{0:T(1024)(128)(4,1)} %bitcast.141), calls=%async_computation.5 | async-start | bytes 8388608
  235.6 39.4 %slice-start.5 = ((s8[16777216]{0:T(1024)(128)(4,1)}), s8[4194304]{0:T(1024)(128)(4,1)S(1)}, s32[]{:S(2)}) async-start(s8[16777216]{0:T(1024)(128)(4,1)} %bitcast.141), calls=%async_computation.6 | async-start | bytes 8388608
  312.5 16.0 %copy-start.11 = (f32[2,5,64,2048]{3,2,1,0:T(8,128)S(1)}, f32[2,5,64,2048]{3,2,1,0:T(8,128)}, u32[]{:S(2)}) copy-start(f32[2,5,64,2048]{3,2,1,0:T(8,128)} %get-tuple-element.9) | copy-start | bytes 15728644
  411.0 20.2 %copy-start.5 = (f32[5,16,64,256]{3,1,2,0:T(8,128)S(1)}, f32[5,16,64,256]{3,1,2,0:T(8,128)}, u32[]{:S(2)}) copy-start(f32[5,16,64,256]{3,1,2,0:T(8,128)} %get-tuple-element.4) | copy-start | bytes 15728644
  411.0 20.2 %copy-start.6 = (f32[5,16,64,256]{3,1,2,0:T(8,128)S(1)}, f32[5,16,64,256]{3,1,2,0:T(8,128)}, u32[]{:S(2)}) copy-start(f32[5,16,64,256]{3,1,2,0:T(8,128)} %get-tuple-element.16) | copy-start | bytes 15728644
  411.0 20.2 %copy-start.7 = (f32[5,16,64,256]{3,1,2,0:T(8,128)S(1)}, f32[5,16,64,256]{3,1,2,0:T(8,128)}, u32[]{:S(2)}) copy-start(f32[5,16,64,256]{3,1,2,0:T(8,128)} %get-tuple-element.17) | copy-start | bytes 15728644
  411.1 33.6 %slice-start.18 = ((s8[5242880]{0:T(1024)(128)(4,1)}), s8[4194304]{0:T(1024)(128)(4,1)S(1)}, s32[]{:S(2)}) async-start(s8[5242880]{0:T(1024)(128)(4,1)} %bitcast.156), calls=%async_computation.19 | async-start | bytes 8388608
  431.3 13.4 %slice-start.19 = ((s8[5242880]{0:T(1024)(128)(4,1)}), s8[1048576]{0:T(1024)(128)(4,1)S(1)}, s32[]{:S(2)}) async-start(s8[5242880]{0:T(1024)(128)(4,1)} %bitcast.156), calls=%async_computation.20 | async-start | bytes 2097152
  457.0 25.9 %slice-start.8 = ((s8[5242880]{0:T(1024)(128)(4,1)}), s8[4194304]{0:T(1024)(128)(4,1)S(1)}, s32[]{:S(2)}) async-start(s8[5242880]{0:T(1024)(128)(4,1)} %bitcast.145), calls=%async_computation.9 | async-start | bytes 8388608
  469.8 13.2 %slice-start.9 = ((s8[5242880]{0:T(1024)(128)(4,1)}), s8[1048576]{0:T(1024)(128)(4,1)S(1)}, s32[]{:S(2)}) async-start(s8[5242880]{0:T(1024)(128)(4,1)} %bitcast.145), calls=%async_computation.10 | async-start | bytes 2097152
  469.8 30.0 %slice-start = ((s8[8355840]{0:T(1024)(128)(4,1)}), s8[4194304]{0:T(1024)(128)(4,1)S(1)}, s32[]{:S(2)}) async-start(s8[8355840]{0:T(1024)(128)(4,1)} %bitcast.139), calls=%async_computation.1 | async-start | bytes 8388608
  483.0 16.8 %slice-start.1 = ((s8[8355840]{0:T(1024)(128)(4,1)}), s8[4161536]{0:T(1024)(128)(4,1)S(1)}, s32[]{:S(2)}) async-start(s8[8355840]{0:T(1024)(128)(4,1)} %bitcast.139), calls=%async_computation.2 | async-start | bytes 8323072
  563.9 19.0 %copy-start.2 = (f32[5,16,64,256]{3,1,2,0:T(8,128)S(1)}, f32[5,16,64,256]{3,1,2,0:T(8,128)}, u32[]{:S(2)}) copy-start(f32[5,16,64,256]{3,1,2,0:T(8,128)} %get-tuple-element.6) | copy-start | bytes 15728644
  563.9 19.0 %copy-start.3 = (f32[5,16,64,256]{3,1,2,0:T(8,128)S(1)}, f32[5,16,64,256]{3,1,2,0:T(8,128)}, u32[]{:S(2)}) copy-start(f32[5,16,64,256]{3,1,2,0:T(8,128)} %get-tuple-element.18) | copy-start | bytes 15728644
  563.9 19.0 %copy-start.4 = (f32[5,16,64,256]{3,1,2,0:T(8,128)S(1)}, f32[5,16,64,256]{3,1,2,0:T(8,128)}, u32[]{:S(2)}) copy-start(f32[5,16,64,256]{3,1,2,0:T(8,128)} %get-tuple-element.19) | copy-start | bytes 15728644
  563.9 31.7 %slice-start.16 = ((s8[5242880]{0:T(1024)(128)(4,1)}), s8[4194304]{0:T(1024)(128)(4,1)S(1)}, s32[]{:S(2)}) async-start(s8[5242880]{0:T(1024)(128)(4,1)} %bitcast.154), calls=%async_computation.17 | async-start | bytes 8388608
  583.0 12.7 %slice-start.17 = ((s8[5242880]{0:T(1024)(128)(4,1)}), s8[1048576]{0:T(1024)(128)(4,1)S(1)}, s32[]{:S(2)}) async-start(s8[5242880]{0:T(1024)(128)(4,1)} %bitcast.154), calls=%async_computation.18 | async-start | bytes 2097152
  607.3 24.0 %slice-start.12 = ((s8[5242880]{0:T(1024)(128)(4,1)}), s8[4194304]{0:T(1024)(128)(4,1)S(1)}, s32[]{:S(2)}) async-start(s8[5242880]{0:T(1024)(128)(4,1)} %bitcast.149), calls=%async_computation.13 | async-start | bytes 8388608
  619.3 11.9 %slice-start.13 = ((s8[5242880]{0:T(1024)(128)(4,1)}), s8[1048576]{0:T(1024)(128)(4,1)S(1)}, s32[]{:S(2)}) async-start(s8[5242880]{0:T(1024)(128)(4,1)} %bitcast.149), calls=%async_computation.14 | async-start | bytes 2097152
  631.3 8.8 %copy-start.1 = (f32[5,5]{1,0:T(8,128)S(1)}, f32[5,5]{1,0:T(8,128)}, u32[]{:S(2)}) copy-start(f32[5,5]{1,0:T(8,128)} %param.9) | copy-start | bytes 304
Sparse Core Ops, SparseCore 0:
  10.9 160.0 all-gather.1
where the time goes:
time: 655 us; the launch traced here: 647 us
  other arithmetic  440 us (67%)
  matrix products  107 us (16%)
  local copies, waits for them, and re-layouts  65.2 us (10%)
  between operations  15.6 us (2%)
  starting transfers between devices  14.5 us (2%)
    mul x2, other arithmetic, update_block(): slopes.append(0.5 * (plus_one - minus_one))  115 us
    unnamed x17, other arithmetic  114 us
    add x1, other arithmetic, shards(): blend * rotor_modes + (1.0 - blend) * stator_modes  69.8 us
    dot_general x1, other arithmetic, shards(): jnp.dot(piece_rows[1], rotor_matrix, precision=highest, preferred_element...  69.5 us
    dot_general x1, matrix products, shards(): jnp.dot(piece_rows[1], rotor_matrix, precision=highest, preferred_element...  39.4 us
    dot_general x1, matrix products, shards(): jnp.dot(piece_rows[0], stator_matrix, precision=highest, preferred_elemen...  37.6 us
    unnamed x78, local copies, waits for them, and re-layouts  31.9 us
    dot_general x2, matrix products, contract_last(): lax.dot_general(left, right, (((1,), (1,)), ((), ())), precision=highest,...  28.2 us
  transfers between devices with their start and end apart: 9, of which 2 were waited for; matrix products, arithmetic and copies ran while one was open for 30% of the time, Pallas kernels for 0%

commit v1 on v0

v1 whole, which is shorter than its diff:
```python
import functools
import math

import jax
import jax.numpy as jnp
import ml_dtypes
import numpy as np
from jax import lax
from jax.experimental import pallas as pl
from jax.experimental.pallas import tpu as pltpu
from jax.sharding import PartitionSpec as P

NP = 2048
LANES = 128
OUTER = NP // LANES
PAIRS = OUTER // 2
UNITS = 12

time_step = 0.5
damping = 1.0 / 32.0
VMEM_LIMIT = 56 * 1024 * 1024


def mode_tables():
    inner = np.arange(LANES)
    out = np.zeros((PAIRS, 2 * LANES, 2 * LANES))

    def angles(outer):
        return 2.0 * math.pi * (np.outer(inner, outer + OUTER * inner) % NP) / NP

    for m in range(PAIRS):
        first, second = (0, PAIRS) if m == 0 else (m, OUTER - m)
        a, b = angles(first), angles(second)
        if m == 0:
            out[m, :LANES, :LANES] = np.cos(a) + np.sin(a)
            out[m, LANES:, LANES:] = np.cos(b) + np.sin(b)
        else:
            out[m, :LANES, :LANES] = np.cos(a)
            out[m, LANES:, :LANES] = np.sin(a)
            out[m, :LANES, LANES:] = np.sin(b)
            out[m, LANES:, LANES:] = np.cos(b)
    high = out.astype(ml_dtypes.bfloat16)
    low = (out - high.astype(np.float64)).astype(ml_dtypes.bfloat16)
    return high, low


def outer_order():
    order = [(0, PAIRS)] + [(m, OUTER - m) for m in range(1, PAIRS)]
    return np.array(order)


def fast_hartley(parts):
    count = len(parts)
    if count == 1:
        return parts
    half = count // 2
    even = fast_hartley(parts[0::2])
    odd = fast_hartley(parts[1::2])
    turned = []
    for k in range(half):
        if k == 0:
            turned.append(odd[0])
        elif 4 * k == count:
            turned.append(odd[half - k])
        else:
            angle = 2.0 * math.pi * k / count
            turned.append(odd[k] * math.cos(angle) + odd[half - k] * math.sin(angle))
    return [even[k] + turned[k] for k in range(half)] + [even[k] - turned[k] for k in range(half)]


def split_dot(x, high, low, dims):
    x_high = x.astype(jnp.bfloat16)
    x_low = (x - x_high.astype(jnp.float32)).astype(jnp.bfloat16)
    dot = functools.partial(
        lax.dot_general, dimension_numbers=(dims, ((), ())), preferred_element_type=jnp.float32
    )
    return dot(x_high, high) + (dot(x_low, high) + dot(x_high, low))


def transform_kernel(fields, offset_ref, got_ref, blend_ref, high_ref, low_ref, out_ref, turn, work):
    rows, cols = got_ref.shape[2:]
    per = cols // LANES
    offset = offset_ref[0]
    whole, part = offset // LANES, offset % LANES
    chunk = 8 if rows % 8 == 0 else rows
    lane = lax.broadcasted_iota(jnp.int32, (chunk, LANES), 1)
    pairs = outer_order()

    def block(i):
        return i // per, slice((i % per) * LANES, (i % per + 1) * LANES)

    for i in range(OUTER):
        device, lanes = block(i)
        turn[i] = pltpu.roll(got_ref[device, 1, :, lanes], part, 1)
    for at in range(0, rows, chunk):
        span = slice(at, at + chunk)
        parts = []
        for i in range(OUTER):
            device, lanes = block(i)
            now = turn[(i - whole + OUTER) % OUTER, span, :]
            before = turn[(i - whole - 1 + OUTER) % OUTER, span, :]
            parts.append(jnp.where(lane >= part, now, before) - got_ref[device, 0, span, lanes])
        modes = fast_hartley(parts)
        for m in range(PAIRS):
            work[m, span, :LANES] = modes[pairs[m, 0]]
            work[m, span, LANES:] = modes[pairs[m, 1]]
    for m in range(PAIRS):
        got = split_dot(work[m], high_ref[m], low_ref[m], ((1,), (0,)))
        per_field = rows // fields
        got = jnp.concatenate(
            [
                got[f * per_field : (f + 1) * per_field] * blend_ref[m, f : f + 1, :]
                for f in range(fields)
            ],
            axis=0,
        )
        work[m] = split_dot(got, high_ref[m], low_ref[m], ((1,), (1,)))
    back = (LANES - part) % LANES
    for at in range(0, rows, chunk):
        span = slice(at, at + chunk)
        modes = [None] * OUTER
        for m in range(PAIRS):
            modes[pairs[m, 0]] = work[m, span, :LANES]
            modes[pairs[m, 1]] = work[m, span, LANES:]
        parts = fast_hartley(modes)
        for i in range(OUTER):
            device, lanes = block(i)
            out_ref[device, 0, span, lanes] = parts[i]
            turn[i, span, :] = pltpu.roll(parts[i], back, 1)
        for i in range(OUTER):
            device, lanes = block(i)
            now = turn[(i + whole) % OUTER, span, :]
            after = turn[(i + whole + 1) % OUTER, span, :]
            out_ref[device, 1, span, lanes] = jnp.where(lane < LANES - part, now, after)


def transform(received, offset, blend, fields):
    high, low = mode_tables()
    count, _, rows, cols = received.shape
    vmem = pl.BlockSpec(memory_space=pltpu.VMEM)
    return pl.pallas_call(
        functools.partial(transform_kernel, fields),
        out_shape=jax.ShapeDtypeStruct(received.shape, jnp.float32),
        in_specs=[pl.BlockSpec(memory_space=pltpu.SMEM)] + [vmem] * 4,
        out_specs=vmem,
        scratch_shapes=[
            pltpu.VMEM((OUTER, rows, LANES), jnp.float32),
            pltpu.VMEM((PAIRS, rows, 2 * LANES), jnp.float32),
        ],
        compiler_params=pltpu.CompilerParams(vmem_limit_bytes=VMEM_LIMIT),
        cost_estimate=pl.CostEstimate(
            flops=12 * rows * PAIRS * 4 * LANES * LANES, bytes_accessed=5_000_000, transcendentals=0
        ),
        name="modes",
    )(offset, received, blend, jnp.asarray(high), jnp.asarray(low))


def pack_kernel(stator_ref, rotor_ref, low_ref, high_ref, left_ref, right_ref):
    step = pl.program_id(0)
    fields, _, rows, cols = stator_ref.shape
    lane = lax.broadcasted_iota(jnp.int32, (rows, LANES), 1)
    for side, ref in enumerate((stator_ref, rotor_ref)):
        unit = 2 * step + side
        place, first = unit // UNITS, unit % UNITS * (2 * fields)
        left = jnp.zeros((rows, LANES), jnp.float32)
        right = jnp.zeros((rows, LANES), jnp.float32)
        for f in range(fields):
            low_ref[side, 0, f] = ref[f, 0, :2, :]
            high_ref[side, 0, f] = ref[f, 0, rows - 2 :, :]
            here = lane // 2 == f
            a, b = ref[f, 0, :, :LANES], ref[f, 0, :, cols - LANES :]
            left = jnp.where(here, pltpu.roll(a, 2 * f, 1) if f else a, left)
            right = jnp.where(here, pltpu.roll(b, 2 * f + 2, 1), right)
        left = pltpu.roll(left, first, 1)
        right = pltpu.roll(right, first, 1)

        fresh = (lane >= first) & (lane < first + 2 * fields)
        left_ref[place] = jnp.where(fresh, left, left_ref[place])
        right_ref[place] = jnp.where(fresh, right, right_ref[place])


def pack_edges(stator, rotor):
    fields, layers, rows, cols = stator.shape
    blocks = -(-2 * layers // UNITS)
    one = (fields, 1, rows, cols)
    edge = jax.ShapeDtypeStruct((2, layers, fields, 2, cols), jnp.float32)
    side = jax.ShapeDtypeStruct((blocks, rows, LANES), jnp.float32)
    edge_spec = pl.BlockSpec((2, 1, fields, 2, cols), lambda t: (0, t, 0, 0, 0))
    side_spec = pl.BlockSpec((blocks, rows, LANES), lambda t: (0, 0, 0))
    return pl.pallas_call(
        pack_kernel,
        grid=(layers,),
        out_shape=(edge, edge, side, side),
        in_specs=[
            pl.BlockSpec(one, lambda t: (0, t, 0, 0)),
            pl.BlockSpec(one, lambda t: (0, layers - 1 - t, 0, 0)),
        ],
        out_specs=(edge_spec, edge_spec, side_spec, side_spec),
        compiler_params=pltpu.CompilerParams(vmem_limit_bytes=VMEM_LIMIT),
        cost_estimate=pl.CostEstimate(
            flops=0, bytes_accessed=2 * 4 * stator.size, transcendentals=0
        ),
        name="edges",
    )(stator, rotor)


def stencil_kernel(
    layers, jac_ref, mix_ref, stator_hbm, rotor_hbm, low_ref, high_ref, left_ref, right_ref,
    stator_out, rotor_out, state, sems,
):
    t = pl.program_id(0)
    fields, _, rows, cols = stator_out.shape
    blocks = cols // LANES
    sources = (stator_hbm, rotor_hbm)

    def load(side, layer):
        taken = layer if side == 0 else layers - 1 - layer
        return pltpu.make_async_copy(
            sources[side].at[:, taken], state.at[side, :, layer + 2], sems.at[side, layer]
        )

    @pl.when(t == 0)
    def _():
        for layer in range(layers):
            for side in range(2):
                load(side, layer).start()
        state[:, :, 0:2] = jnp.zeros((2, fields, 2, rows, cols), jnp.float32)
        for layer in range(2):
            for side in range(2):
                load(side, layer).wait()

    @pl.when(t + 2 < layers)
    def _():
        for side in range(2):
            load(side, t + 2).wait()

    @pl.when(t == layers - 2)
    def _():
        for side in range(2):
            for ghost in range(2):
                for at in range(0, rows, 8):
                    span = slice(at, at + 8)
                    planes = [state[side, g, layers + 1 - ghost, span, :] for g in range(fields)]
                    for f in range(fields):
                        total = mix_ref[f * fields] * planes[0]
                        for g in range(1, fields):
                            total = total + mix_ref[f * fields + g] * planes[g]
                        state[side, f, layers + 2 + ghost, span, :] = total

    lane = lax.broadcasted_iota(jnp.int32, (8, LANES), 1)
    row = lax.broadcasted_iota(jnp.int32, (8, LANES), 0)
    here = t + 2
    pad = jnp.zeros((6, cols), jnp.float32)
    for side, out in ((0, stator_out), (1, rotor_out)):
        unit = 2 * t + side
        place, first = unit // UNITS, unit % UNITS * (2 * fields)
        turn = (LANES - first) % LANES
        for at in range(0, rows, 8):
            span = slice(at, at + 8)
            from_left = pltpu.roll(left_ref[place, span, :], turn, 1)
            from_right = pltpu.roll(right_ref[place, span, :], turn, 1)
            slopes, bases = [], []
            for f in range(fields):
                shift = (LANES - 2 * f) % LANES
                rim = jnp.where(
                    lane < LANES // 2,
                    pltpu.roll(from_right, shift, 1) if shift else from_right,
                    pltpu.roll(from_left, LANES - 2 * f - 2, 1),
                )
                if at == 0:
                    above = jnp.concatenate([pad, low_ref[side, 0, f]], axis=0)
                else:
                    above = state[side, f, here, at - 8 : at, :]
                if at + 8 == rows:
                    below = jnp.concatenate([high_ref[side, 0, f], pad], axis=0)
                else:
                    below = state[side, f, here, at + 8 : at + 16, :]
                centre = [state[side, f, here, span, b * LANES : (b + 1) * LANES] for b in range(blocks)]
                ring = centre + [rim]
                field_slopes, field_bases = [], []
                for b in range(blocks):
                    lanes = slice(b * LANES, (b + 1) * LANES)
                    now = centre[b]
                    nxt, prv = ring[b + 1], ring[b - 1]
                    up, down = above[:, lanes], below[:, lanes]
                    a_p1, a_m1 = state[side, f, here + 1, span, lanes], state[side, f, here - 1, span, lanes]
                    a_p2, a_m2 = state[side, f, here + 2, span, lanes], state[side, f, here - 2, span, lanes]
                    r_p1 = pltpu.roll(jnp.where(row < 1, down, now), 7, 0)
                    r_p2 = pltpu.roll(jnp.where(row < 2, down, now), 6, 0)
                    r_m1 = pltpu.roll(jnp.where(row >= 7, up, now), 1, 0)
                    r_m2 = pltpu.roll(jnp.where(row >= 6, up, now), 2, 0)
                    p_p1 = pltpu.roll(jnp.where(lane < 1, nxt, now), LANES - 1, 1)
                    p_p2 = pltpu.roll(jnp.where(lane < 2, nxt, now), LANES - 2, 1)
                    p_m1 = pltpu.roll(jnp.where(lane >= LANES - 1, prv, now), 1, 1)
                    p_m2 = pltpu.roll(jnp.where(lane >= LANES - 2, prv, now), 2, 1)
                    field_slopes.append((a_p1 - a_m1, r_p1 - r_m1, p_p1 - p_m1))
                    near = ((a_p1 + a_m1) + (r_p1 + r_m1)) + (p_p1 + p_m1)
                    far = ((a_p2 + a_m2) + (r_p2 + r_m2)) + (p_p2 + p_m2)
                    field_bases.append(
                        now * (1.0 - 18.0 * time_step * damping)
                        + (near * 4.0 - far) * (time_step * damping)
                    )
                slopes.append(field_slopes)
                bases.append(field_bases)
            for f in range(fields):
                totals = list(bases[f])
                for d in range(3):
                    for g in range(fields):
                        weight = jac_ref[((side * 3 + d) * fields + f) * fields + g]
                        for b in range(blocks):
                            totals[b] = totals[b] + weight * slopes[g][b][d]
                for b in range(blocks):
                    out[f, 0, span, b * LANES : (b + 1) * LANES] = totals[b]


def stencil(stator, rotor, low, high, left, right, weights, mix):
    fields, layers, rows, cols = stator.shape
    one = (fields, 1, rows, cols)
    smem = pl.BlockSpec(memory_space=pltpu.SMEM)
    hbm = pl.BlockSpec(memory_space=pl.ANY)
    edge_spec = pl.BlockSpec((2, 1, fields, 2, cols), lambda t: (0, t, 0, 0, 0))
    side_spec = pl.BlockSpec(left.shape, lambda t: (0, 0, 0))
    shape = jax.ShapeDtypeStruct(stator.shape, jnp.float32)
    return pl.pallas_call(
        functools.partial(stencil_kernel, layers),
        grid=(layers,),
        out_shape=(shape, shape),
        in_specs=[smem, smem, hbm, hbm, edge_spec, edge_spec, side_spec, side_spec],
        out_specs=(
            pl.BlockSpec(one, lambda t: (0, t, 0, 0)),
            pl.BlockSpec(one, lambda t: (0, layers - 1 - t, 0, 0)),
        ),
        scratch_shapes=[
            pltpu.VMEM((2, fields, layers + 4, rows, cols), jnp.float32),
            pltpu.SemaphoreType.DMA((2, layers)),
        ],
        compiler_params=pltpu.CompilerParams(vmem_limit_bytes=VMEM_LIMIT),
        cost_estimate=pl.CostEstimate(
            flops=60 * 2 * stator.size, bytes_accessed=16 * stator.size, transcendentals=0
        ),
        name="stencil",
    )(weights, mix, stator, rotor, low, high, left, right)


def close_kernel(weight_ref, modes_ref, stator_ref, rotor_ref, stator_out, rotor_out):
    fields, _, rows, cols = stator_ref.shape
    count = modes_ref.shape[0]
    step = modes_ref.shape[4]
    for side, (ref, out) in enumerate(((stator_ref, stator_out), (rotor_ref, rotor_out))):
        near, far = (1, 0) if side == 0 else (0, 1)
        for q in range(count):
            span = slice(q * step, (q + 1) * step)
            first = [modes_ref[q, side, g, 0] for g in range(fields)]
            second = [modes_ref[q, side, g, 1] for g in range(fields)]
            for f in range(fields):
                rim, inner = ref[f, near, span, :], ref[f, far, span, :]
                for g in range(fields):
                    at = (side * 2 * fields + f) * fields + g
                    weight_near = weight_ref[at]
                    weight_far = weight_ref[at + fields * fields]
                    rim = rim + (weight_near * first[g] + weight_far * second[g])
                    inner = inner + weight_far * first[g]
                out[f, near, span, :] = rim
                out[f, far, span, :] = inner


def close(modes, stator, rotor, weights):
    fields, layers, rows, cols = stator.shape
    count, _, _, _, step, _ = modes.shape
    group = max(1, count // 4)
    block = (fields, 2, rows // count * group, cols)
    specs = (
        pl.BlockSpec(block, lambda q: (0, layers // 2 - 1, q, 0)),
        pl.BlockSpec(block, lambda q: (0, 0, q, 0)),
    )
    shape = jax.ShapeDtypeStruct(stator.shape, jnp.float32)
    return pl.pallas_call(
        close_kernel,
        grid=(count // group,),
        out_shape=(shape, shape),
        in_specs=[
            pl.BlockSpec(memory_space=pltpu.SMEM),
            pl.BlockSpec((group,) + modes.shape[1:], lambda q: (q, 0, 0, 0, 0, 0)),
            *specs,
        ],
        out_specs=specs,
        input_output_aliases={2: 0, 3: 1},
        compiler_params=pltpu.CompilerParams(vmem_limit_bytes=VMEM_LIMIT),
        cost_estimate=pl.CostEstimate(
            flops=30 * modes.size, bytes_accessed=12 * modes.size, transcendentals=0
        ),
        name="interface",
    )(weights, modes, stator, rotor)


def exact_dot(a, b):
    return jnp.matmul(a, b, precision=lax.Precision.HIGHEST)


def shards(stator, rotor, jacobians, field_mix, mode_blend, rotor_offset):
    fields, layers, rows, cols = stator.shape
    count = lax.axis_size("pitch")
    spans = lax.axis_size("span")
    step = rows // count

    def by_owner(planes):
        return jnp.moveaxis(planes.reshape(fields, 2, count, step, cols), 2, 0)

    planes = jnp.stack([by_owner(stator[:, layers - 2 :][:, ::-1]), by_owner(rotor[:, :2])], axis=1)
    planes = planes.reshape(count, 2, fields * 2 * step, cols)
    received = lax.all_to_all(planes, "pitch", 0, 0, tiled=True)

    low, high, left, right = pack_edges(stator, rotor)
    ring = [(i, (i + 1) % count) for i in range(count)]
    line = [(i, i + 1) for i in range(spans - 1)]
    from_left = lax.ppermute(right, "pitch", ring)
    from_right = lax.ppermute(left, "pitch", [(b, a) for a, b in ring])
    from_below = lax.ppermute(high, "span", line)
    from_above = lax.ppermute(low, "span", [(b, a) for a, b in line])

    mirrored = jacobians * jnp.array([-1.0, 1.0, 1.0], jnp.float32)[:, None, None]
    courses = jnp.stack([jacobians, mirrored])
    weights = (-0.5 * time_step) * courses
    mixed = exact_dot(courses[:, 0], field_mix)
    far = (-time_step * damping) * field_mix
    near = (-0.5 * time_step) * mixed + (4.0 * time_step * damping) * field_mix
    signs = jnp.array([1.0, -1.0], jnp.float32)[:, None, None]
    rim_weights = jnp.stack([signs * near, signs * far], axis=1)

    stator_mid, rotor_mid = stencil(
        stator, rotor, from_below, from_above, from_left, from_right,
        weights.reshape(-1), field_mix.reshape(-1),
    )

    blend = mode_blend.reshape(fields, LANES, OUTER) * (1.0 / NP)
    blend = jnp.moveaxis(blend, 2, 0)[outer_order().reshape(-1)]
    blend = blend.reshape(PAIRS, 2, fields, LANES).transpose(0, 2, 1, 3).reshape(PAIRS, fields, 2 * LANES)
    sent = transform(received, rotor_offset, blend, fields)
    modes = lax.all_to_all(sent, "pitch", 0, 0, tiled=True)
    modes = modes.reshape(count, 2, fields, 2, step, cols)
    return close(modes, stator_mid, rotor_mid, rim_weights.reshape(-1))


def solution(mesh):
    block = P(None, None, "span", "pitch")
    in_specs = (block, block, P(), P(), P(), P())
    return jax.shard_map(
        shards, mesh=mesh, in_specs=in_specs, out_specs=(block, block), check_vma=False
    )
```

time: 655 us -> 185 us (0.28)
  other arithmetic: 440 us -> 1.36 us
  Pallas kernels: 0 us -> 116 us
  matrix products: 107 us -> 0.16 us
  local copies, waits for them, and re-layouts: 65.2 us -> 9.61 us
  waiting for transfers between devices: 5.02 us -> 34.6 us
  between operations: 15.6 us -> 1.57 us
    mul x3 -> x4, other arithmetic: 130 us -> 0.09 us  [the longest x1 0.07 us: shards(): rim_weights = jnp.stack([signs * near, signs * far], axis=1)]
    pallas_call x0 -> x4, Pallas kernels: none -> 116 us  [the longest x1 93.3 us: stencil(): pl.pallas_call(functools.partial(stencil_kernel, layers), grid=(layers,),...]
    unnamed x17 -> x0, other arithmetic: 114 us -> none
    dot_general x5 -> x1, matrix products: 107 us -> 0.16 us  [exact_dot(): return jnp.matmul(a, b, precision=lax.Precision.HIGHEST)]
    add x3 -> x0, other arithmetic: 81.8 us -> none  [the longest x1 69.8 us: shards(): blend * rotor_modes + (1.0 - blend) * stator_modes]
    dot_general x1 -> x0, other arithmetic: 69.5 us -> none  [shards(): jnp.dot(piece_rows[1], rotor_matrix, precision=highest, preferred_element...]
    all_to_all x0 -> x2, waiting for transfers between devices: none -> 29.1 us  [the longest x1 29.1 us: shards(): received = lax.all_to_all(planes, 'pitch', 0, 0, tiled=True)]
    unnamed x78 -> x24, local copies, waits for them, and re-layouts: 31.9 us -> 3.68 us
  transfers between devices with their start and end apart: 9 -> 6, of which waited for: 2 -> 2; matrix products, arithmetic and copies ran while one was open for 30% -> 2% of each run, Pallas kernels for 0% -> 59%
where the time goes in v1:
time: 185 us; the launch traced here: 182 us
  Pallas kernels  116 us (63%)
  waiting for transfers between devices  34.6 us (19%)
  starting transfers between devices  18.3 us (10%)
  local copies, waits for them, and re-layouts  9.61 us (5%)
    pallas_call x1, Pallas kernels, stencil(): pl.pallas_call(functools.partial(stencil_kernel, layers), grid=(layers,),...  93.3 us
    all_to_all x1, waiting for transfers between devices, shards(): received = lax.all_to_all(planes, 'pitch', 0, 0, tiled=True)  29.1 us
    pallas_call x1, Pallas kernels, pack_edges(): pl.pallas_call(pack_kernel, grid=(layers,), out_shape=(edge, edge, side,...  13.3 us
    all_to_all x1, starting transfers between devices, shards(): received = lax.all_to_all(planes, 'pitch', 0, 0, tiled=True)  7.25 us
    ppermute x1, waiting for transfers between devices, shards(): from_left = lax.ppermute(right, 'pitch', ring)  5.48 us
    pallas_call x1, Pallas kernels, transform(): pl.pallas_call(functools.partial(transform_kernel, fields), out_shape=jax...  5.35 us
    pallas_call x1, Pallas kernels, close(): pl.pallas_call(close_kernel, grid=(count // group,), out_shape=(shape, sh...  4.05 us
  transfers between devices with their start and end apart: 6, of which 2 were waited for; matrix products, arithmetic and copies ran while one was open for 2% of the time, Pallas kernels for 59%

profile of v1, /device:TPU:0, one launch (start us, length us, event | category | flops | bytes accessed | tf_op | source)
XLA Modules:
  0.0 181.6 jit_solution(17384270157862452969)
XLA Ops:
  0.6 1.1 slice.10
  1.8 0.0 copy-start.7
  1.8 0.0 copy-start.10
  1.9 0.1 copy.26
  1.9 1.1 slice_bitcast_fusion
  3.1 0.1 copy.27
  3.2 1.2 pad_maximum_fusion
  4.3 7.3 %all-to-all-start = ((f32[8,2,80,256]{3,2,1,0:T(8,128)}), f32[8,2,80,256]{3,2,1,0:T(8,128)S(1)}, u32[]{:S(2)}, u32[]{:S(2)}) async-start(f32[8,2,80,256]{3,2,1,0:T(8,128)} %pad_maximum_fusion), calls=%async_computation | async-start | bytes 2621440 | tf_op jit(solution)/shard_map/all_to_all | solution.py:411
  12.2 0.0 copy-done.7
  12.3 0.1 mul.80
  12.4 0.2 copy.28
  12.6 0.0 copy-done.10
  12.6 0.6 gather_fusion
  13.2 0.6 copy.30.blend_ref
  13.9 29.1 %all-to-all-done.got_ref = f32[8,2,80,256]{3,2,1,0:T(8,128)S(1)} async-done(((f32[8,2,80,256]{3,2,1,0:T(8,128)}), f32[8,2,80,256]{3,2,1,0:T(8,128)S(1)}, u32[]{:S(2)}, u32[]{:S(2)}) %all-to-all-start) | async-done | bytes 1310752 | tf_op jit(solution)/shard_map/all_to_all | solution.py:411
  43.0 1.1 copy-done.1
  44.0 5.3 %modes.1 = f32[8,2,80,256]{3,2,1,0:T(8,128)} custom-call(s32[1]{0:T(128)S(6)} %copy.40.offset_ref, f32[8,2,80,256]{3,2,1,0:T(8,128)} %copy-done.1, f32[8,5,256]{2,1,0:T(8,128)} %copy.30.blend_ref, bf16[8,256,256]{2,1,0:T(8,128)(2,1)} %constant.27.clone.high_ref, bf16[8,256,256]{2,1,0:T(8,128)(2,1)} %constant.28.clone.low_ref), custom_call_target="tpu_custom_call" | custom-call | flops 503316480 | bytes 5000000 | tf_op jit(solution)/shard_map/modes/pallas_call | solution.py:141
  49.4 3.6 %all-to-all-start.1 = ((f32[8,2,80,256]{3,2,1,0:T(8,128)}), f32[8,2,80,256]{3,2,1,0:T(8,128)S(1)}, u32[]{:S(2)}, u32[]{:S(2)}) async-start(f32[8,2,80,256]{3,2,1,0:T(8,128)} %modes.1), calls=%async_computation.1 | async-start | bytes 2621440 | tf_op jit(solution)/shard_map/all_to_all | solution.py:439
  53.0 0.0 copy-start.11
  53.0 0.0 copy-start.8
  53.0 0.0 copy-start.9
  53.1 13.3 %edges.1 = (f32[2,16,5,2,256]{4,3,2,1,0:T(2,128)}, f32[2,16,5,2,256]{4,3,2,1,0:T(2,128)}, f32[3,64,128]{2,1,0:T(8,128)}, f32[3,64,128]{2,1,0:T(8,128)}) custom-call(f32[5,16,64,256]{3,2,1,0:T(8,128)} %stator_hbm.1, f32[5,16,64,256]{3,2,1,0:T(8,128)} %rotor_hbm.1), custom_call_target="tpu_custom_call" | custom-call | bytes 10485760 | tf_op jit(solution)/shard_map/edges/pallas_call | solution.py:190
  66.4 2.1 %collective-permute-start.2 = (f32[3,64,128]{2,1,0:T(8,128)}, f32[3,64,128]{2,1,0:T(8,128)S(1)}, u32[]{:S(2)}, u32[]{:S(2)}) collective-permute-start(f32[3,64,128]{2,1,0:T(8,128)} %get-tuple-element.10), channel_id=1, source_target_pairs={{0,4},{4,8},{8,12},{12,16},{16,20},{20,24},{24,28},{28,0},{1,5},{5... | collective-permute-start | bytes 294920 | tf_op jit(solution)/shard_map/ppermute | solution.py:416
  68.4 2.8 %collective-permute-start.3 = (f32[3,64,128]{2,1,0:T(8,128)}, f32[3,64,128]{2,1,0:T(8,128)S(1)}, u32[]{:S(2)}, u32[]{:S(2)}) collective-permute-start(f32[3,64,128]{2,1,0:T(8,128)} %get-tuple-element.11), channel_id=1, source_target_pairs={{4,0},{8,4},{12,8},{16,12},{20,16},{24,20},{28,24},{0,28},{5,1},{9... | collective-permute-start | bytes 294920 | tf_op jit(solution)/shard_map/ppermute | solution.py:417
  71.2 1.3 collective-permute-start
  72.5 1.3 collective-permute-start.1
  73.8 0.0 copy-done.6
  73.8 0.0 copy-done.11
  73.8 0.1 multiply_bitcast_fusion
  73.9 0.0 copy-done.8
  74.0 0.2 fusion.1
  74.1 0.1 broadcast_multiply_fusion.1
  74.2 0.6 reshape.50.mix_ref
  74.8 0.6 reshape.44.weight_ref
  75.5 0.6 mul.83.jac_ref
  76.1 5.5 %collective-permute-done.2.left_ref = f32[3,64,128]{2,1,0:T(8,128)S(1)} collective-permute-done((f32[3,64,128]{2,1,0:T(8,128)}, f32[3,64,128]{2,1,0:T(8,128)S(1)}, u32[]{:S(2)}, u32[]{:S(2)}) %collective-permute-start.2) | collective-permute-done | bytes 98336 | tf_op jit(solution)/shard_map/ppermute | solution.py:416
  81.6 0.0 collective-permute-done.3.right_ref
  81.6 0.0 collective-permute-done.low_ref
  81.6 0.0 copy-start.2
  81.6 0.0 collective-permute-done.1.high_ref
  81.6 0.6 copy-done.4
  82.2 0.0 copy-done.5
  82.3 0.1 copy-done.2
  82.4 0.7 copy-done.3
  83.2 93.3 %stencil.1 = (f32[5,16,64,256]{3,2,1,0:T(8,128)}, f32[5,16,64,256]{3,2,1,0:T(8,128)}) custom-call(f32[150]{0:T(256)} %mul.83.jac_ref, f32[25]{0:T(128)} %reshape.50.mix_ref, f32[5,16,64,256]{3,2,1,0:T(8,128)} %stator_hbm.1, f32[5,16,64,256]{3,2,1,0:T(8,128)} %rotor_hbm.1, f32[2,16,5,2,256]{4,3,2,1,0:T(2,128)} %copy-done.2, f32[2,16,5,2,256]{4,3,2,1,0:T(2,128)} %copy-done.3, ...), custom_call_target="tpu_custom_call" | custom-call | flops 157286400 | bytes 20971520 | tf_op jit(solution)/shard_map/stencil/pallas_call | solution.py:324
  176.4 0.0 all-to-all-done.1
  176.4 1.1 copy-done
  177.5 4.0 %interface.1 = (f32[5,16,64,256]{3,2,1,0:T(8,128)}, f32[5,16,64,256]{3,2,1,0:T(8,128)}) custom-call(f32[100]{0:T(128)} %reshape.44.weight_ref, f32[8,2,5,2,8,256]{5,4,3,2,1,0:T(8,128)} %bitcast.29, f32[5,16,64,256]{3,2,1,0:T(8,128)} %get-tuple-element.12.stator_ref, ...), custom_call_target="tpu_custom_call", output_to_operand_aliasing={{0}: (2, {}), {1}: (3, {})} | custom-call | flops 9830400 | bytes 3932160 | tf_op jit(solution)/shard_map/interface/pallas_call | solution.py:377
  (20 shorter events, 0.2 us)
Async XLA Ops:
  1.8 10.5 %copy-start.7 = (f32[5,2048]{1,0:T(8,128)S(1)}, f32[5,2048]{1,0:T(8,128)}, u32[]{:S(2)}) copy-start(f32[5,2048]{1,0:T(8,128)} %param.16) | copy-start | bytes 122884
  1.8 10.7 %copy-start.10 = (s32[16]{0:T(128)S(1)}, s32[16]{0:T(128)}, u32[]{:S(2)}) copy-start(s32[16]{0:T(128)} %constant.30) | copy-start | bytes 196
  4.3 38.6 %all-to-all-start = ((f32[8,2,80,256]{3,2,1,0:T(8,128)}), f32[8,2,80,256]{3,2,1,0:T(8,128)S(1)}, u32[]{:S(2)}, u32[]{:S(2)}) async-start(f32[8,2,80,256]{3,2,1,0:T(8,128)} %pad_maximum_fusion), calls=%async_computation | async-start | bytes 2621440 | tf_op jit(solution)/shard_map/all_to_all | solution.py:411
  43.0 1.1 copy-start.1
  49.4 127.0 %all-to-all-start.1 = ((f32[8,2,80,256]{3,2,1,0:T(8,128)}), f32[8,2,80,256]{3,2,1,0:T(8,128)S(1)}, u32[]{:S(2)}, u32[]{:S(2)}) async-start(f32[8,2,80,256]{3,2,1,0:T(8,128)} %modes.1), calls=%async_computation.1 | async-start | bytes 2621440 | tf_op jit(solution)/shard_map/all_to_all | solution.py:439
  53.0 20.8 %copy-start.6 = (f32[3,5,5]{2,0,1:T(4,128)S(1)}, f32[3,5,5]{2,0,1:T(4,128)}, u32[]{:S(2)}) copy-start(f32[3,5,5]{2,0,1:T(4,128)} %param.14) | copy-start | bytes 904
  53.0 20.8 %copy-start.11 = (f32[3]{0:T(128)S(1)}, f32[3]{0:T(128)}, u32[]{:S(2)}) copy-start(f32[3]{0:T(128)} %constant.10.clone) | copy-start | bytes 40
  53.0 20.9 %copy-start.8 = (f32[5,5]{1,0:T(8,128)S(1)}, f32[5,5]{1,0:T(8,128)}, u32[]{:S(2)}) copy-start(f32[5,5]{1,0:T(8,128)} %param.15) | copy-start | bytes 304
  53.0 20.9 %copy-start.9 = (f32[2]{0:T(128)S(1)}, f32[2]{0:T(128)}, u32[]{:S(2)}) copy-start(f32[2]{0:T(128)} %constant.24.clone) | copy-start | bytes 28
  66.4 15.2 %collective-permute-start.2 = (f32[3,64,128]{2,1,0:T(8,128)}, f32[3,64,128]{2,1,0:T(8,128)S(1)}, u32[]{:S(2)}, u32[]{:S(2)}) collective-permute-start(f32[3,64,128]{2,1,0:T(8,128)} %get-tuple-element.10), channel_id=1, source_target_pairs={{0,4},{4,8},{8,12},{12,16},{16,20},{20,24},{24,28},{28,0},{1,5},{5... | collective-permute-start | bytes 294920 | tf_op jit(solution)/shard_map/ppermute | solution.py:416
  68.4 13.2 %collective-permute-start.3 = (f32[3,64,128]{2,1,0:T(8,128)}, f32[3,64,128]{2,1,0:T(8,128)S(1)}, u32[]{:S(2)}, u32[]{:S(2)}) collective-permute-start(f32[3,64,128]{2,1,0:T(8,128)} %get-tuple-element.11), channel_id=1, source_target_pairs={{4,0},{8,4},{12,8},{16,12},{20,16},{24,20},{28,24},{0,28},{5,1},{9... | collective-permute-start | bytes 294920 | tf_op jit(solution)/shard_map/ppermute | solution.py:417
  71.2 10.4 %collective-permute-start = (f32[2,16,5,2,256]{4,3,2,1,0:T(2,128)}, f32[2,16,5,2,256]{4,3,2,1,0:T(2,128)S(1)}, u32[]{:S(2)}, u32[]{:S(2)}) collective-permute-start(f32[2,16,5,2,256]{4,3,2,1,0:T(2,128)} %get-tuple-element.8), channel_id=1, source_target_pairs={{0,1},{1,2},{2,3},{4,5},{5,6},{6,7},{8,9},{9,10},{10,11},{12,13},{... | collective-permute-start | bytes 983048 | tf_op jit(solution)/shard_map/ppermute | solution.py:418
  72.5 9.1 %collective-permute-start.1 = (f32[2,16,5,2,256]{4,3,2,1,0:T(2,128)}, f32[2,16,5,2,256]{4,3,2,1,0:T(2,128)S(1)}, u32[]{:S(2)}, u32[]{:S(2)}) collective-permute-start(f32[2,16,5,2,256]{4,3,2,1,0:T(2,128)} %get-tuple-element.9), channel_id=1, source_target_pairs={{1,0},{2,1},{3,2},{5,4},{6,5},{7,6},{9,8},{10,9},{11,10},{13,12},{... | collective-permute-start | bytes 983048 | tf_op jit(solution)/shard_map/ppermute | solution.py:419
  81.6 0.6 copy-start.4
  81.6 0.7 copy-start.5
  81.6 0.8 copy-start.2
  82.4 0.7 copy-start.3
  176.4 1.1 copy-start

commit v2 on v1

--- a/solution.py
+++ b/solution.py
@@ -204,142 +204,154 @@
     )(stator, rotor)
 
 
+def difference_tables(rows, cols):
+    scale = time_step * damping
+    slope = {1: 1.0, -1: -1.0}
+    smooth = {0: -6.0 * scale, 1: 4.0 * scale, -1: 4.0 * scale, 2: -scale, -2: -scale}
+
+    def banded(extent, halo_places, halo_width):
+        whole = np.zeros((2, extent, extent))
+        halo = np.zeros((2, extent, halo_width))
+        for which, taps in enumerate((slope, smooth)):
+            for i in range(extent):
+                for shift, value in taps.items():
+                    j = i + shift
+                    if 0 <= j < extent:
+                        whole[which, i, j] += value
+                    else:
+                        halo[which, i, halo_places[j if j < 0 else j - extent]] += value
+        return whole.reshape(2 * extent, extent), halo.reshape(2 * extent, halo_width)
+
+    main, rim = banded(rows, {-2: 0, -1: 1, 0: 2, 1: 3}, 8)
+    along_rows = np.concatenate([main, main, rim, rim], axis=1)
+    main, rim = banded(cols, {0: 0, 1: 1, -2: LANES - 2, -1: LANES - 1}, LANES)
+    along_cols = np.concatenate([main, main, rim, rim], axis=1).T
+    return along_rows.astype(ml_dtypes.bfloat16), along_cols.astype(ml_dtypes.bfloat16)
+
+
+def halves(x):
+    high = x.astype(jnp.bfloat16)
+    return high, (x - high.astype(jnp.float32)).astype(jnp.bfloat16)
+
+
 def stencil_kernel(
-    layers, jac_ref, mix_ref, stator_hbm, rotor_hbm, low_ref, high_ref, left_ref, right_ref,
-    stator_out, rotor_out, state, sems,
+    side, layers, jac_ref, mix_ref, source, low_ref, high_ref, left_ref, right_ref, rows_ref, cols_ref,
+    out, state, radial, pitch, parts, sems,
 ):
     t = pl.program_id(0)
-    fields, _, rows, cols = stator_out.shape
-    blocks = cols // LANES
-    sources = (stator_hbm, rotor_hbm)
-
-    def load(side, layer):
+    fields, _, rows, cols = out.shape
+    chunk = 16
+
+    def load(layer):
         taken = layer if side == 0 else layers - 1 - layer
-        return pltpu.make_async_copy(
-            sources[side].at[:, taken], state.at[side, :, layer + 2], sems.at[side, layer]
-        )
+        return pltpu.make_async_copy(source.at[:, taken], state.at[:, layer + 2], sems.at[layer])
 
     @pl.when(t == 0)
     def _():
         for layer in range(layers):
-            for side in range(2):
-                load(side, layer).start()
-        state[:, :, 0:2] = jnp.zeros((2, fields, 2, rows, cols), jnp.float32)
+            load(layer).start()
+        state[:, 0:2] = jnp.zeros((fields, 2, rows, cols), jnp.float32)
         for layer in range(2):
-            for side in range(2):
-                load(side, layer).wait()
+            load(layer).wait()
 
     @pl.when(t + 2 < layers)
     def _():
-        for side in range(2):
-            load(side, t + 2).wait()
+        load(t + 2).wait()
 
     @pl.when(t == layers - 2)
     def _():
-        for side in range(2):
-            for ghost in range(2):
-                for at in range(0, rows, 8):
-                    span = slice(at, at + 8)
-                    planes = [state[side, g, layers + 1 - ghost, span, :] for g in range(fields)]
-                    for f in range(fields):
-                        total = mix_ref[f * fields] * planes[0]
-                        for g in range(1, fields):
-                            total = total + mix_ref[f * fields + g] * planes[g]
-                        state[side, f, layers + 2 + ghost, span, :] = total
-
-    lane = lax.broadcasted_iota(jnp.int32, (8, LANES), 1)
-    row = lax.broadcasted_iota(jnp.int32, (8, LANES), 0)
+        for ghost in range(2):
+            for at in range(0, rows, chunk):
+                span = slice(at, at + chunk)
+                planes = [state[g, layers + 1 - ghost, span, :] for g in range(fields)]
+                for f in range(fields):
+                    total = mix_ref[f * fields] * planes[0]
+                    for g in range(1, fields):
+                        total = total + mix_ref[f * fields + g] * planes[g]
+                    state[f, layers + 2 + ghost, span, :] = total
+
     here = t + 2
-    pad = jnp.zeros((6, cols), jnp.float32)
-    for side, out in ((0, stator_out), (1, rotor_out)):
-        unit = 2 * t + side
-        place, first = unit // UNITS, unit % UNITS * (2 * fields)
-        turn = (LANES - first) % LANES
-        for at in range(0, rows, 8):
-            span = slice(at, at + 8)
-            from_left = pltpu.roll(left_ref[place, span, :], turn, 1)
-            from_right = pltpu.roll(right_ref[place, span, :], turn, 1)
-            slopes, bases = [], []
-            for f in range(fields):
-                shift = (LANES - 2 * f) % LANES
-                rim = jnp.where(
-                    lane < LANES // 2,
-                    pltpu.roll(from_right, shift, 1) if shift else from_right,
-                    pltpu.roll(from_left, LANES - 2 * f - 2, 1),
-                )
-                if at == 0:
-                    above = jnp.concatenate([pad, low_ref[side, 0, f]], axis=0)
-                else:
-                    above = state[side, f, here, at - 8 : at, :]
-                if at + 8 == rows:
-                    below = jnp.concatenate([high_ref[side, 0, f], pad], axis=0)
-                else:
-                    below = state[side, f, here, at + 8 : at + 16, :]
-                centre = [state[side, f, here, span, b * LANES : (b + 1) * LANES] for b in range(blocks)]
-                ring = centre + [rim]
-                field_slopes, field_bases = [], []
-                for b in range(blocks):
-                    lanes = slice(b * LANES, (b + 1) * LANES)
-                    now = centre[b]
-                    nxt, prv = ring[b + 1], ring[b - 1]
-                    up, down = above[:, lanes], below[:, lanes]
-                    a_p1, a_m1 = state[side, f, here + 1, span, lanes], state[side, f, here - 1, span, lanes]
-                    a_p2, a_m2 = state[side, f, here + 2, span, lanes], state[side, f, here - 2, span, lanes]
-                    r_p1 = pltpu.roll(jnp.where(row < 1, down, now), 7, 0)
-                    r_p2 = pltpu.roll(jnp.where(row < 2, down, now), 6, 0)
-                    r_m1 = pltpu.roll(jnp.where(row >= 7, up, now), 1, 0)
-                    r_m2 = pltpu.roll(jnp.where(row >= 6, up, now), 2, 0)
-                    p_p1 = pltpu.roll(jnp.where(lane < 1, nxt, now), LANES - 1, 1)
-                    p_p2 = pltpu.roll(jnp.where(lane < 2, nxt, now), LANES - 2, 1)
-                    p_m1 = pltpu.roll(jnp.where(lane >= LANES - 1, prv, now), 1, 1)
-                    p_m2 = pltpu.roll(jnp.where(lane >= LANES - 2, prv, now), 2, 1)
-                    field_slopes.append((a_p1 - a_m1, r_p1 - r_m1, p_p1 - p_m1))
-                    near = ((a_p1 + a_m1) + (r_p1 + r_m1)) + (p_p1 + p_m1)
-                    far = ((a_p2 + a_m2) + (r_p2 + r_m2)) + (p_p2 + p_m2)
-                    field_bases.append(
-                        now * (1.0 - 18.0 * time_step * damping)
-                        + (near * 4.0 - far) * (time_step * damping)
-                    )
-                slopes.append(field_slopes)
-                bases.append(field_bases)
-            for f in range(fields):
-                totals = list(bases[f])
-                for d in range(3):
-                    for g in range(fields):
-                        weight = jac_ref[((side * 3 + d) * fields + f) * fields + g]
-                        for b in range(blocks):
-                            totals[b] = totals[b] + weight * slopes[g][b][d]
-                for b in range(blocks):
-                    out[f, 0, span, b * LANES : (b + 1) * LANES] = totals[b]
-
-
-def stencil(stator, rotor, low, high, left, right, weights, mix):
-    fields, layers, rows, cols = stator.shape
-    one = (fields, 1, rows, cols)
+    unit = 2 * t + side
+    place, first = unit // UNITS, unit % UNITS * (2 * fields)
+    turn = (LANES - first) % LANES
+    lane = lax.broadcasted_iota(jnp.int32, (rows, LANES), 1)
+    from_left = pltpu.roll(left_ref[place], turn, 1)
+    from_right = pltpu.roll(right_ref[place], turn, 1)
+    for f in range(fields):
+        shift = (LANES - 2 * f) % LANES
+        rim = jnp.where(lane < 2, pltpu.roll(from_right, shift, 1) if shift else from_right, 0.0)
+        rim = jnp.where(lane < LANES - 2, rim, pltpu.roll(from_left, LANES - 2 * f - 2, 1))
+        span = slice(f * rows, (f + 1) * rows)
+        x_high, x_low = halves(state[f, here])
+        rim_high, rim_low = halves(rim)
+        parts[span, :cols] = x_high
+        parts[span, cols : 2 * cols] = x_low
+        parts[span, 2 * cols : 2 * cols + LANES] = rim_high
+        parts[span, 2 * cols + LANES :] = rim_low
+        halo = jnp.concatenate(
+            [low_ref[0, 0, f], high_ref[0, 0, f], jnp.zeros((4, cols), jnp.float32)], axis=0
+        )
+        halo_high = halo.astype(jnp.bfloat16).astype(jnp.float32)
+        halo = jnp.concatenate([halo_high, halo - halo_high], axis=0).astype(jnp.bfloat16)
+        radial[f] = jnp.dot(
+            rows_ref[...],
+            jnp.concatenate([x_high, x_low, halo], axis=0),
+            preferred_element_type=jnp.float32,
+        )
+    pitch[...] = jnp.dot(parts[...], cols_ref[...], preferred_element_type=jnp.float32)
+
+    scale = time_step * damping
+    for at in range(0, rows, chunk):
+        span = slice(at, at + chunk)
+        totals = []
+        for f in range(fields):
+            near = state[f, here + 1, span, :] + state[f, here - 1, span, :]
+            far = state[f, here + 2, span, :] + state[f, here - 2, span, :]
+            totals.append(
+                (state[f, here, span, :] * (1.0 - 6.0 * scale) + (near * 4.0 - far) * scale)
+                + (radial[f, rows + at : rows + at + chunk, :] + pitch[f * rows + at : f * rows + at + chunk, cols:])
+            )
+        for g in range(fields):
+            slopes = (
+                state[g, here + 1, span, :] - state[g, here - 1, span, :],
+                radial[g, span, :],
+                pitch[g * rows + at : g * rows + at + chunk, :cols],
+            )
+            for d in range(3):
+                for f in range(fields):
+                    totals[f] = totals[f] + jac_ref[(d * fields + f) * fields + g] * slopes[d]
+        for f in range(fields):
+            out[f, 0, span, :] = totals[f]
+
+
+def stencil(side, state, low, high, left, right, weights, mix):
+    fields, layers, rows, cols = state.shape
+    along_rows, along_cols = difference_tables(rows, cols)
     smem = pl.BlockSpec(memory_space=pltpu.SMEM)
-    hbm = pl.BlockSpec(memory_space=pl.ANY)
-    edge_spec = pl.BlockSpec((2, 1, fields, 2, cols), lambda t: (0, t, 0, 0, 0))
+    vmem = pl.BlockSpec(memory_space=pltpu.VMEM)
+    edge_spec = pl.BlockSpec((1, 1, fields, 2, cols), lambda t: (side, t, 0, 0, 0))
     side_spec = pl.BlockSpec(left.shape, lambda t: (0, 0, 0))
-    shape = jax.ShapeDtypeStruct(stator.shape, jnp.float32)
     return pl.pallas_call(
-        functools.partial(stencil_kernel, layers),
+        functools.partial(stencil_kernel, side, layers),
         grid=(layers,),
-        out_shape=(shape, shape),
-        in_specs=[smem, smem, hbm, hbm, edge_spec, edge_spec, side_spec, side_spec],
-        out_specs=(
-            pl.BlockSpec(one, lambda t: (0, t, 0, 0)),
-            pl.BlockSpec(one, lambda t: (0, layers - 1 - t, 0, 0)),
+        out_shape=jax.ShapeDtypeStruct(state.shape, jnp.float32),
+        in_specs=[smem, smem, pl.BlockSpec(memory_space=pl.ANY), edge_spec, edge_spec, side_spec, side_spec, vmem, vmem],
+        out_specs=pl.BlockSpec(
+            (fields, 1, rows, cols), lambda t: (0, t if side == 0 else layers - 1 - t, 0, 0)
         ),
         scratch_shapes=[
-            pltpu.VMEM((2, fields, layers + 4, rows, cols), jnp.float32),
-            pltpu.SemaphoreType.DMA((2, layers)),
+            pltpu.VMEM((fields, layers + 4, rows, cols), jnp.float32),
+            pltpu.VMEM((fields, 2 * rows, cols), jnp.float32),
+            pltpu.VMEM((fields * rows, 2 * cols), jnp.float32),
+            pltpu.VMEM((fields * rows, 2 * cols + 2 * LANES), jnp.bfloat16),
+            pltpu.SemaphoreType.DMA((layers,)),
         ],
         compiler_params=pltpu.CompilerParams(vmem_limit_bytes=VMEM_LIMIT),
         cost_estimate=pl.CostEstimate(
-            flops=60 * 2 * stator.size, bytes_accessed=16 * stator.size, transcendentals=0
+            flops=60 * state.size, bytes_accessed=16 * state.size, transcendentals=0
         ),
-        name="stencil",
-    )(weights, mix, stator, rotor, low, high, left, right)
+        name=("stator_stencil", "rotor_stencil")[side],
+    )(weights, mix, state, low, high, left, right, jnp.asarray(along_rows), jnp.asarray(along_cols))
 
 
 def close_kernel(weight_ref, modes_ref, stator_ref, rotor_ref, stator_out, rotor_out):
@@ -427,10 +439,10 @@
     signs = jnp.array([1.0, -1.0], jnp.float32)[:, None, None]
     rim_weights = jnp.stack([signs * near, signs * far], axis=1)
 
-    stator_mid, rotor_mid = stencil(
-        stator, rotor, from_below, from_above, from_left, from_right,
-        weights.reshape(-1), field_mix.reshape(-1),
-    )
+    edges = (from_below, from_above, from_left, from_right)
+    mix = field_mix.reshape(-1)
+    stator_mid = stencil(0, stator, *edges, weights[0].reshape(-1), mix)
+    received, stator_mid = lax.optimization_barrier((received, stator_mid))
 
     blend = mode_blend.reshape(fields, LANES, OUTER) * (1.0 / NP)
     blend = jnp.moveaxis(blend, 2, 0)[outer_order().reshape(-1)]
@@ -438,6 +450,7 @@
     sent = transform(received, rotor_offset, blend, fields)
     modes = lax.all_to_all(sent, "pitch", 0, 0, tiled=True)
     modes = modes.reshape(count, 2, fields, 2, step, cols)
+    rotor_mid = stencil(1, rotor, *edges, weights[1].reshape(-1), mix)
     return close(modes, stator_mid, rotor_mid, rim_weights.reshape(-1))
 
 

time: 185 us -> 111 us (0.60); the launches traced: 182 us -> 110 us
  Pallas kernels: 116 us -> 58.4 us
  waiting for transfers between devices: 34.6 us -> 15.9 us
  starting transfers between devices: 18.3 us -> 22.5 us
    pallas_call x1 -> x2, Pallas kernels: 93.3 us -> 35.7 us  [stencil(): pl.pallas_call(functools.partial(stencil_kernel, side, layers), grid=(lay...]
    all_to_all x1, waiting for transfers between devices: 29.1 us -> 0.01 us  [shards(): received = lax.all_to_all(planes, 'pitch', 0, 0, tiled=True)]
    all_to_all x1, waiting for transfers between devices: 0.01 us -> 12.1 us  [shards(): modes = lax.all_to_all(sent, 'pitch', 0, 0, tiled=True)]
    all_to_all x1, starting transfers between devices: 3.64 us -> 7.86 us  [shards(): modes = lax.all_to_all(sent, 'pitch', 0, 0, tiled=True)]
  transfers between devices with their start and end apart: 6 -> 6, of which waited for: 2 -> 2; matrix products, arithmetic and copies ran while one was open for 2% -> 4% of each run, Pallas kernels for 59% -> 44%
where the time goes in v2:
time: 111 us; the launch traced here: 110 us
  Pallas kernels  58.4 us (53%)
  starting transfers between devices  22.5 us (20%)
  waiting for transfers between devices  15.9 us (14%)
  local copies, waits for them, and re-layouts  10.3 us (9%)
  between operations  1.57 us (1%)
  other arithmetic  1.36 us (1%)
    pallas_call x2, Pallas kernels, stencil(): pl.pallas_call(functools.partial(stencil_kernel, side, layers), grid=(lay...  35.7 us
    pallas_call x1, Pallas kernels, pack_edges(): pl.pallas_call(pack_kernel, grid=(layers,), out_shape=(edge, edge, side,...  13.3 us
    all_to_all x1, waiting for transfers between devices, shards(): modes = lax.all_to_all(sent, 'pitch', 0, 0, tiled=True)  12.1 us
    all_to_all x1, starting transfers between devices, shards(): modes = lax.all_to_all(sent, 'pitch', 0, 0, tiled=True)  7.86 us
    all_to_all x1, starting transfers between devices, shards(): received = lax.all_to_all(planes, 'pitch', 0, 0, tiled=True)  7.25 us
    pallas_call x1, Pallas kernels, transform(): pl.pallas_call(functools.partial(transform_kernel, fields), out_shape=jax...  5.35 us
    pallas_call x1, Pallas kernels, close(): pl.pallas_call(close_kernel, grid=(count // group,), out_shape=(shape, sh...  4.05 us
    ppermute x1, waiting for transfers between devices, shards(): from_left = lax.ppermute(right, 'pitch', ring)  3.79 us
  transfers between devices with their start and end apart: 6, of which 2 were waited for; matrix products, arithmetic and copies ran while one was open for 4% of the time, Pallas kernels for 44%

profile of v2, /device:TPU:0, one launch (start us, length us, event | category | flops | bytes accessed | tf_op | source)
XLA Modules:
  0.0 110.2 jit_solution(2821141071704361346)
XLA Ops:
  0.6 1.1 %slice.16 = f32[5,2,64,256]{3,2,1,0:T(8,128)S(1)} slice(f32[5,16,64,256]{3,2,1,0:T(8,128)} %source.2), slice={[0:5], [14:16], [0:64], [0:256]} | slice | bytes 1310720 | tf_op jit(solution)/shard_map/slice | solution.py:421
  1.8 0.1 copy.32
  1.9 1.1 %slice_bitcast_fusion = f32[5,2,8,8,256]{4,3,2,1,0:T(8,128)S(1)} fusion(f32[5,16,64,256]{3,2,1,0:T(8,128)} %source.3), kind=kLoop, calls=%fused_computation.5 | loop fusion | bytes 1310720 | tf_op jit(solution)/shard_map/reshape | solution.py:419
  3.0 0.1 copy.33
  3.1 1.2 %pad_maximum_fusion = f32[8,2,80,256]{3,2,1,0:T(8,128)} fusion(f32[8,1,80,256]{3,2,1,0:T(8,128)S(1)} %bitcast.31, f32[8,1,80,256]{3,2,1,0:T(8,128)S(1)} %bitcast.30), kind=kLoop, calls=%fused_computation.1 | loop fusion | flops 327680 | bytes 2621440 | tf_op jit(solution)/shard_map/stack | solution.py:421
  4.3 7.3 %all-to-all-start = ((f32[8,2,80,256]{3,2,1,0:T(8,128)}), f32[8,2,80,256]{3,2,1,0:T(8,128)S(1)}, u32[]{:S(2)}, u32[]{:S(2)}) async-start(f32[8,2,80,256]{3,2,1,0:T(8,128)} %pad_maximum_fusion), calls=%async_computation | async-start | bytes 2621440 | tf_op jit(solution)/shard_map/all_to_all | solution.py:423
  11.5 0.0 copy-start.6
  11.6 0.0 copy-start.11
  11.6 0.0 copy-start.7
  11.6 0.0 copy-start.10
  11.6 13.3 %edges.1 = (f32[2,16,5,2,256]{4,3,2,1,0:T(2,128)}, f32[2,16,5,2,256]{4,3,2,1,0:T(2,128)}, f32[3,64,128]{2,1,0:T(8,128)}, f32[3,64,128]{2,1,0:T(8,128)}) custom-call(f32[5,16,64,256]{3,2,1,0:T(8,128)} %source.2, f32[5,16,64,256]{3,2,1,0:T(8,128)} %source.3), custom_call_target="tpu_custom_call" | custom-call | bytes 10485760 | tf_op jit(solution)/shard_map/edges/pallas_call | solution.py:190
  24.9 2.1 %collective-permute-start.2 = (f32[3,64,128]{2,1,0:T(8,128)}, f32[3,64,128]{2,1,0:T(8,128)S(1)}, u32[]{:S(2)}, u32[]{:S(2)}) collective-permute-start(f32[3,64,128]{2,1,0:T(8,128)} %get-tuple-element.10), channel_id=1, source_target_pairs={{0,4},{4,8},{8,12},{12,16},{16,20},{20,24},{24,28},{28,0},{1,5},{5... | collective-permute-start | bytes 294920 | tf_op jit(solution)/shard_map/ppermute | solution.py:428
  27.0 2.8 %collective-permute-start.3 = (f32[3,64,128]{2,1,0:T(8,128)}, f32[3,64,128]{2,1,0:T(8,128)S(1)}, u32[]{:S(2)}, u32[]{:S(2)}) collective-permute-start(f32[3,64,128]{2,1,0:T(8,128)} %get-tuple-element.11), channel_id=1, source_target_pairs={{4,0},{8,4},{12,8},{16,12},{20,16},{24,20},{28,24},{0,28},{5,1},{9... | collective-permute-start | bytes 294920 | tf_op jit(solution)/shard_map/ppermute | solution.py:429
  29.8 1.3 %collective-permute-start = (f32[2,16,5,2,256]{4,3,2,1,0:T(2,128)}, f32[2,16,5,2,256]{4,3,2,1,0:T(2,128)S(1)}, u32[]{:S(2)}, u32[]{:S(2)}) collective-permute-start(f32[2,16,5,2,256]{4,3,2,1,0:T(2,128)} %get-tuple-element.8), channel_id=1, source_target_pairs={{0,1},{1,2},{2,3},{4,5},{5,6},{6,7},{8,9},{9,10},{10,11},{12,13},{... | collective-permute-start | bytes 983048 | tf_op jit(solution)/shard_map/ppermute | solution.py:430
  31.1 1.3 %collective-permute-start.1 = (f32[2,16,5,2,256]{4,3,2,1,0:T(2,128)}, f32[2,16,5,2,256]{4,3,2,1,0:T(2,128)S(1)}, u32[]{:S(2)}, u32[]{:S(2)}) collective-permute-start(f32[2,16,5,2,256]{4,3,2,1,0:T(2,128)} %get-tuple-element.9), channel_id=1, source_target_pairs={{1,0},{2,1},{3,2},{5,4},{6,5},{7,6},{9,8},{10,9},{11,10},{13,12},{... | collective-permute-start | bytes 983048 | tf_op jit(solution)/shard_map/ppermute | solution.py:431
  33.0 0.0 copy-done.8
  33.0 0.7 reshape.43.mix_ref
  33.7 0.0 copy-done.11
  33.7 0.1 multiply_bitcast_fusion
  33.8 0.7 reshape_squeeze.6.jac_ref
  34.5 0.1 mul.78
  34.6 0.2 copy.35
  34.8 0.0 copy-done.10
  34.8 0.6 gather_fusion
  35.5 0.7 copy.37.blend_ref
  36.1 3.8 %collective-permute-done.2.left_ref = f32[3,64,128]{2,1,0:T(8,128)S(1)} collective-permute-done((f32[3,64,128]{2,1,0:T(8,128)}, f32[3,64,128]{2,1,0:T(8,128)S(1)}, u32[]{:S(2)}, u32[]{:S(2)}) %collective-permute-start.2) | collective-permute-done | bytes 98336 | tf_op jit(solution)/shard_map/ppermute | solution.py:428
  39.9 0.0 collective-permute-done.3.right_ref
  39.9 0.0 collective-permute-done.low_ref
  39.9 0.0 collective-permute-done.1.high_ref
  39.9 0.6 copy-done.4
  40.5 0.0 copy-done.5
  40.6 0.1 copy-done.2
  40.7 0.7 copy-done.3
  41.5 17.8 %stator_stencil.1.stator_ref = f32[5,16,64,256]{3,2,1,0:T(8,128)} custom-call(f32[75]{0:T(128)} %reshape_squeeze.6.jac_ref, f32[25]{0:T(128)} %reshape.43.mix_ref, f32[5,16,64,256]{3,2,1,0:T(8,128)} %source.2, f32[2,16,5,2,256]{4,3,2,1,0:T(2,128)} %copy-done.2, f32[2,16,5,2,256]{4,3,2,1,0:T(2,128)} %copy-done.3, f32[3,64,128]{2,1,0:T(8,128)} %copy-done.4, ...), custom_call_target="tpu_custom_call" | custom-call | flops 78643200 | bytes 20971520 | tf_op jit(solution)/shard_map/stator_stencil/pallas_call | solution.py:334
  59.3 0.0 copy-start.9
  59.3 0.0 all-to-all-done.got_ref
  59.3 0.0 copy-start
  59.3 1.0 copy-done
  60.3 5.4 %modes.1 = f32[8,2,80,256]{3,2,1,0:T(8,128)} custom-call(s32[1]{0:T(128)S(6)} %copy.47.offset_ref, f32[8,2,80,256]{3,2,1,0:T(8,128)} %copy-done, f32[8,5,256]{2,1,0:T(8,128)} %copy.37.blend_ref, bf16[8,256,256]{2,1,0:T(8,128)(2,1)} %constant.33.clone.high_ref, bf16[8,256,256]{2,1,0:T(8,128)(2,1)} %constant.34.clone.low_ref), custom_call_target="tpu_custom_call" | custom-call | flops 503316480 | bytes 5000000 | tf_op jit(solution)/shard_map/modes/pallas_call | solution.py:141
  65.7 7.9 %all-to-all-start.1 = ((f32[8,2,80,256]{3,2,1,0:T(8,128)}), f32[8,2,80,256]{3,2,1,0:T(8,128)S(1)}, u32[]{:S(2)}, u32[]{:S(2)}) async-start(f32[8,2,80,256]{3,2,1,0:T(8,128)} %modes.1), calls=%async_computation.1 | async-start | bytes 2621440 | tf_op jit(solution)/shard_map/all_to_all | solution.py:451
  73.6 0.2 fusion.1
  73.8 0.1 broadcast_multiply_fusion.1
  73.9 0.6 reshape.40.weight_ref
  74.5 0.6 reshape_squeeze.7.jac_ref
  75.1 17.9 %rotor_stencil.1.rotor_ref = f32[5,16,64,256]{3,2,1,0:T(8,128)} custom-call(f32[75]{0:T(128)} %reshape_squeeze.7.jac_ref, f32[25]{0:T(128)} %reshape.43.mix_ref, f32[5,16,64,256]{3,2,1,0:T(8,128)} %source.3, f32[2,16,5,2,256]{4,3,2,1,0:T(2,128)} %copy-done.2, f32[2,16,5,2,256]{4,3,2,1,0:T(2,128)} %copy-done.3, f32[3,64,128]{2,1,0:T(8,128)} %copy-done.4, ...), custom_call_target="tpu_custom_call" | custom-call | flops 78643200 | bytes 20971520 | tf_op jit(solution)/shard_map/rotor_stencil/pallas_call | solution.py:334
  93.1 12.1 %all-to-all-done.1 = f32[8,2,80,256]{3,2,1,0:T(8,128)S(1)} async-done(((f32[8,2,80,256]{3,2,1,0:T(8,128)}), f32[8,2,80,256]{3,2,1,0:T(8,128)S(1)}, u32[]{:S(2)}, u32[]{:S(2)}) %all-to-all-start.1) | async-done | bytes 1310752 | tf_op jit(solution)/shard_map/all_to_all | solution.py:451
  105.1 1.1 copy-done.1
  106.2 4.0 %interface.1 = (f32[5,16,64,256]{3,2,1,0:T(8,128)}, f32[5,16,64,256]{3,2,1,0:T(8,128)}) custom-call(f32[100]{0:T(128)} %reshape.40.weight_ref, f32[8,2,5,2,8,256]{5,4,3,2,1,0:T(8,128)} %bitcast.29, f32[5,16,64,256]{3,2,1,0:T(8,128)} %stator_stencil.1.stator_ref, f32[5,16,64,256]{3,2,1,0:T(8,128)} %rotor_stencil.1.rotor_ref), custom_call_target="tpu_custom_call", output_to_operand_aliasing={{0}: (2, {}), {1}: (3, {})} | custom-call | flops 9830400 | bytes 3932160 | tf_op jit(solution)/shard_map/interface/pallas_call | solution.py:389
  (24 shorter events, 0.2 us)
Async XLA Ops:
  4.3 55.0 %all-to-all-start = ((f32[8,2,80,256]{3,2,1,0:T(8,128)}), f32[8,2,80,256]{3,2,1,0:T(8,128)S(1)}, u32[]{:S(2)}, u32[]{:S(2)}) async-start(f32[8,2,80,256]{3,2,1,0:T(8,128)} %pad_maximum_fusion), calls=%async_computation | async-start | bytes 2621440 | tf_op jit(solution)/shard_map/all_to_all | solution.py:423
  11.5 21.5 %copy-start.8 = (f32[5,5]{1,0:T(8,128)S(1)}, f32[5,5]{1,0:T(8,128)}, u32[]{:S(2)}) copy-start(f32[5,5]{1,0:T(8,128)} %param.19) | copy-start | bytes 304
  11.5 22.1 %copy-start.6 = (f32[3,5,5]{2,0,1:T(4,128)S(1)}, f32[3,5,5]{2,0,1:T(4,128)}, u32[]{:S(2)}) copy-start(f32[3,5,5]{2,0,1:T(4,128)} %param.18) | copy-start | bytes 904
  11.6 22.1 %copy-start.11 = (f32[3]{0:T(128)S(1)}, f32[3]{0:T(128)}, u32[]{:S(2)}) copy-start(f32[3]{0:T(128)} %constant.12.clone) | copy-start | bytes 40
  11.6 22.2 %copy-start.7 = (f32[5,2048]{1,0:T(8,128)S(1)}, f32[5,2048]{1,0:T(8,128)}, u32[]{:S(2)}) copy-start(f32[5,2048]{1,0:T(8,128)} %param.20) | copy-start | bytes 122884
  11.6 23.2 %copy-start.10 = (s32[16]{0:T(128)S(1)}, s32[16]{0:T(128)}, u32[]{:S(2)}) copy-start(s32[16]{0:T(128)} %constant.36) | copy-start | bytes 196
  24.9 15.0 %collective-permute-start.2 = (f32[3,64,128]{2,1,0:T(8,128)}, f32[3,64,128]{2,1,0:T(8,128)S(1)}, u32[]{:S(2)}, u32[]{:S(2)}) collective-permute-start(f32[3,64,128]{2,1,0:T(8,128)} %get-tuple-element.10), channel_id=1, source_target_pairs={{0,4},{4,8},{8,12},{12,16},{16,20},{20,24},{24,28},{28,0},{1,5},{5... | collective-permute-start | bytes 294920 | tf_op jit(solution)/shard_map/ppermute | solution.py:428
  27.0 12.9 %collective-permute-start.3 = (f32[3,64,128]{2,1,0:T(8,128)}, f32[3,64,128]{2,1,0:T(8,128)S(1)}, u32[]{:S(2)}, u32[]{:S(2)}) collective-permute-start(f32[3,64,128]{2,1,0:T(8,128)} %get-tuple-element.11), channel_id=1, source_target_pairs={{4,0},{8,4},{12,8},{16,12},{20,16},{24,20},{28,24},{0,28},{5,1},{9... | collective-permute-start | bytes 294920 | tf_op jit(solution)/shard_map/ppermute | solution.py:429
  29.8 10.2 %collective-permute-start = (f32[2,16,5,2,256]{4,3,2,1,0:T(2,128)}, f32[2,16,5,2,256]{4,3,2,1,0:T(2,128)S(1)}, u32[]{:S(2)}, u32[]{:S(2)}) collective-permute-start(f32[2,16,5,2,256]{4,3,2,1,0:T(2,128)} %get-tuple-element.8), channel_id=1, source_target_pairs={{0,1},{1,2},{2,3},{4,5},{5,6},{6,7},{8,9},{9,10},{10,11},{12,13},{... | collective-permute-start | bytes 983048 | tf_op jit(solution)/shard_map/ppermute | solution.py:430
  31.1 8.9 %collective-permute-start.1 = (f32[2,16,5,2,256]{4,3,2,1,0:T(2,128)}, f32[2,16,5,2,256]{4,3,2,1,0:T(2,128)S(1)}, u32[]{:S(2)}, u32[]{:S(2)}) collective-permute-start(f32[2,16,5,2,256]{4,3,2,1,0:T(2,128)} %get-tuple-element.9), channel_id=1, source_target_pairs={{1,0},{2,1},{3,2},{5,4},{6,5},{7,6},{9,8},{10,9},{11,10},{13,12},{... | collective-permute-start | bytes 983048 | tf_op jit(solution)/shard_map/ppermute | solution.py:431
  39.9 0.6 copy-start.4
  39.9 0.7 copy-start.5
  39.9 0.8 copy-start.2
  40.7 0.7 copy-start.3
  59.3 14.3 %copy-start.9 = (f32[2]{0:T(128)S(1)}, f32[2]{0:T(128)}, u32[]{:S(2)}) copy-start(f32[2]{0:T(128)} %constant.28.clone) | copy-start | bytes 28
  59.3 1.1 copy-start
  65.7 39.4 %all-to-all-start.1 = ((f32[8,2,80,256]{3,2,1,0:T(8,128)}), f32[8,2,80,256]{3,2,1,0:T(8,128)S(1)}, u32[]{:S(2)}, u32[]{:S(2)}) async-start(f32[8,2,80,256]{3,2,1,0:T(8,128)} %modes.1), calls=%async_computation.1 | async-start | bytes 2621440 | tf_op jit(solution)/shard_map/all_to_all | solution.py:451
  105.1 1.1 copy-start.1

commit v3 on v2

--- a/solution.py
+++ b/solution.py
@@ -18,7 +18,8 @@
 
 time_step = 0.5
 damping = 1.0 / 32.0
-VMEM_LIMIT = 56 * 1024 * 1024
+WIDE = 56 * 1024 * 1024
+NARROW = 16 * 1024 * 1024
 
 
 def mode_tables():
@@ -147,12 +148,49 @@
             pltpu.VMEM((OUTER, rows, LANES), jnp.float32),
             pltpu.VMEM((PAIRS, rows, 2 * LANES), jnp.float32),
         ],
-        compiler_params=pltpu.CompilerParams(vmem_limit_bytes=VMEM_LIMIT),
+        compiler_params=pltpu.CompilerParams(vmem_limit_bytes=NARROW),
         cost_estimate=pl.CostEstimate(
             flops=12 * rows * PAIRS * 4 * LANES * LANES, bytes_accessed=5_000_000, transcendentals=0
         ),
         name="modes",
     )(offset, received, blend, jnp.asarray(high), jnp.asarray(low))
+
+
+def planes_kernel(stator, rotor, out, sems):
+    count, _, _, _, step, _ = out.shape
+    layers = stator.shape[1]
+    copies = []
+    for q in range(count):
+        span = pl.ds(q * step, step)
+        for ghost in range(2):
+            copies.append((stator.at[:, layers - 1 - ghost, span], out.at[q, 0, :, ghost]))
+            copies.append((rotor.at[:, ghost, span], out.at[q, 1, :, ghost]))
+    copies = [pltpu.make_async_copy(a, b, sems.at[i]) for i, (a, b) in enumerate(copies)]
+    for copy in copies:
+        copy.start()
+    for copy in copies:
+        copy.wait()
+
+
+def interface_planes(stator, rotor, count):
+    fields, layers, rows, cols = stator.shape
+    step = rows // count
+    if step % 8:
+
+        def by_owner(planes):
+            return jnp.moveaxis(planes.reshape(fields, 2, count, step, cols), 2, 0)
+
+        return jnp.stack([by_owner(stator[:, layers - 2 :][:, ::-1]), by_owner(rotor[:, :2])], axis=1)
+    hbm = pl.BlockSpec(memory_space=pl.ANY)
+    return pl.pallas_call(
+        planes_kernel,
+        out_shape=jax.ShapeDtypeStruct((count, 2, fields, 2, step, cols), jnp.float32),
+        in_specs=[hbm, hbm],
+        out_specs=hbm,
+        scratch_shapes=[pltpu.SemaphoreType.DMA((4 * count,))],
+        compiler_params=pltpu.CompilerParams(vmem_limit_bytes=WIDE),
+        name="planes",
+    )(stator, rotor)
 
 
 def pack_kernel(stator_ref, rotor_ref, low_ref, high_ref, left_ref, right_ref):
@@ -196,7 +234,7 @@
             pl.BlockSpec(one, lambda t: (0, layers - 1 - t, 0, 0)),
         ],
         out_specs=(edge_spec, edge_spec, side_spec, side_spec),
-        compiler_params=pltpu.CompilerParams(vmem_limit_bytes=VMEM_LIMIT),
+        compiler_params=pltpu.CompilerParams(vmem_limit_bytes=WIDE),
         cost_estimate=pl.CostEstimate(
             flops=0, bytes_accessed=2 * 4 * stator.size, transcendentals=0
         ),
@@ -238,27 +276,87 @@
     side, layers, jac_ref, mix_ref, source, low_ref, high_ref, left_ref, right_ref, rows_ref, cols_ref,
     out, state, radial, pitch, parts, sems,
 ):
-    t = pl.program_id(0)
+    step = pl.program_id(0)
     fields, _, rows, cols = out.shape
     chunk = 16
+    scale = time_step * damping
+    lane = lax.broadcasted_iota(jnp.int32, (rows, LANES), 1)
 
     def load(layer):
         taken = layer if side == 0 else layers - 1 - layer
         return pltpu.make_async_copy(source.at[:, taken], state.at[:, layer + 2], sems.at[layer])
 
-    @pl.when(t == 0)
+    def products(t, slot):
+        unit = 2 * t + side
+        place, first = unit // UNITS, unit % UNITS * (2 * fields)
+        turn = (LANES - first) % LANES
+        from_left = pltpu.roll(left_ref[place], turn, 1)
+        from_right = pltpu.roll(right_ref[place], turn, 1)
+        for f in range(fields):
+            shift = (LANES - 2 * f) % LANES
+            rim = jnp.where(lane < 2, pltpu.roll(from_right, shift, 1) if shift else from_right, 0.0)
+            rim = jnp.where(lane < LANES - 2, rim, pltpu.roll(from_left, LANES - 2 * f - 2, 1))
+            span = slice(f * rows, (f + 1) * rows)
+            x_high, x_low = halves(state[f, t + 2])
+            rim_high, rim_low = halves(rim)
+            parts[span, :cols] = x_high
+            parts[span, cols : 2 * cols] = x_low
+            parts[span, 2 * cols : 2 * cols + LANES] = rim_high
+            parts[span, 2 * cols + LANES :] = rim_low
+            halo = jnp.concatenate(
+                [low_ref[0, t, f], high_ref[0, t, f], jnp.zeros((4, cols), jnp.float32)], axis=0
+            )
+            halo_high = halo.astype(jnp.bfloat16).astype(jnp.float32)
+            halo = jnp.concatenate([halo_high, halo - halo_high], axis=0).astype(jnp.bfloat16)
+            radial[slot, f] = jnp.dot(
+                rows_ref[...],
+                jnp.concatenate([x_high, x_low, halo], axis=0),
+                preferred_element_type=jnp.float32,
+            )
+        pitch[slot] = jnp.dot(parts[...], cols_ref[...], preferred_element_type=jnp.float32)
+
+    def advance(t, slot):
+        here = t + 2
+        for at in range(0, rows, chunk):
+            span = slice(at, at + chunk)
+            totals = []
+            for f in range(fields):
+                near = state[f, here + 1, span, :] + state[f, here - 1, span, :]
+                far = state[f, here + 2, span, :] + state[f, here - 2, span, :]
+                totals.append(
+                    (state[f, here, span, :] * (1.0 - 6.0 * scale) + (near * 4.0 - far) * scale)
+                    + (
+                        radial[slot, f, rows + at : rows + at + chunk, :]
+                        + pitch[slot, f * rows + at : f * rows + at + chunk, cols:]
+                    )
+                )
+            for g in range(fields):
+                slopes = (
+                    state[g, here + 1, span, :] - state[g, here - 1, span, :],
+                    radial[slot, g, span, :],
+                    pitch[slot, g * rows + at : g * rows + at + chunk, :cols],
+                )
+                for d in range(3):
+                    for f in range(fields):
+                        totals[f] = totals[f] + jac_ref[(d * fields + f) * fields + g] * slopes[d]
+            for f in range(fields):
+                out[f, slot if side == 0 else 1 - slot, span, :] = totals[f]
+
+    @pl.when(step == 0)
     def _():
         for layer in range(layers):
             load(layer).start()
         state[:, 0:2] = jnp.zeros((fields, 2, rows, cols), jnp.float32)
-        for layer in range(2):
-            load(layer).wait()
-
-    @pl.when(t + 2 < layers)
+        load(0).wait()
+        load(1).wait()
+        products(0, 0)
+
+    @pl.when(2 * step + 2 < layers)
     def _():
-        load(t + 2).wait()
-
-    @pl.when(t == layers - 2)
+        load(2 * step + 2).wait()
+        load(2 * step + 3).wait()
+
+    @pl.when(2 * step == layers - 2)
     def _():
         for ghost in range(2):
             for at in range(0, rows, chunk):
@@ -270,58 +368,10 @@
                         total = total + mix_ref[f * fields + g] * planes[g]
                     state[f, layers + 2 + ghost, span, :] = total
 
-    here = t + 2
-    unit = 2 * t + side
-    place, first = unit // UNITS, unit % UNITS * (2 * fields)
-    turn = (LANES - first) % LANES
-    lane = lax.broadcasted_iota(jnp.int32, (rows, LANES), 1)
-    from_left = pltpu.roll(left_ref[place], turn, 1)
-    from_right = pltpu.roll(right_ref[place], turn, 1)
-    for f in range(fields):
-        shift = (LANES - 2 * f) % LANES
-        rim = jnp.where(lane < 2, pltpu.roll(from_right, shift, 1) if shift else from_right, 0.0)
-        rim = jnp.where(lane < LANES - 2, rim, pltpu.roll(from_left, LANES - 2 * f - 2, 1))
-        span = slice(f * rows, (f + 1) * rows)
-        x_high, x_low = halves(state[f, here])
-        rim_high, rim_low = halves(rim)
-        parts[span, :cols] = x_high
-        parts[span, cols : 2 * cols] = x_low
-        parts[span, 2 * cols : 2 * cols + LANES] = rim_high
-        parts[span, 2 * cols + LANES :] = rim_low
-        halo = jnp.concatenate(
-            [low_ref[0, 0, f], high_ref[0, 0, f], jnp.zeros((4, cols), jnp.float32)], axis=0
-        )
-        halo_high = halo.astype(jnp.bfloat16).astype(jnp.float32)
-        halo = jnp.concatenate([halo_high, halo - halo_high], axis=0).astype(jnp.bfloat16)
-        radial[f] = jnp.dot(
-            rows_ref[...],
-            jnp.concatenate([x_high, x_low, halo], axis=0),
-            preferred_element_type=jnp.float32,
-        )
-    pitch[...] = jnp.dot(parts[...], cols_ref[...], preferred_element_type=jnp.float32)
-
-    scale = time_step * damping
-    for at in range(0, rows, chunk):
-        span = slice(at, at + chunk)
-        totals = []
-        for f in range(fields):
-            near = state[f, here + 1, span, :] + state[f, here - 1, span, :]
-            far = state[f, here + 2, span, :] + state[f, here - 2, span, :]
-            totals.append(
-                (state[f, here, span, :] * (1.0 - 6.0 * scale) + (near * 4.0 - far) * scale)
-                + (radial[f, rows + at : rows + at + chunk, :] + pitch[f * rows + at : f * rows + at + chunk, cols:])
-            )
-        for g in range(fields):
-            slopes = (
-                state[g, here + 1, span, :] - state[g, here - 1, span, :],
-                radial[g, span, :],
-                pitch[g * rows + at : g * rows + at + chunk, :cols],
-            )
-            for d in range(3):
-                for f in range(fields):
-                    totals[f] = totals[f] + jac_ref[(d * fields + f) * fields + g] * slopes[d]
-        for f in range(fields):
-            out[f, 0, span, :] = totals[f]
+    products(2 * step + 1, 1)
+    advance(2 * step, 0)
+    products(jnp.minimum(2 * step + 2, layers - 1), 0)
+    advance(2 * step + 1, 1)
 
 
 def stencil(side, state, low, high, left, right, weights, mix):
@@ -329,24 +379,25 @@
     along_rows, along_cols = difference_tables(rows, cols)
     smem = pl.BlockSpec(memory_space=pltpu.SMEM)
     vmem = pl.BlockSpec(memory_space=pltpu.VMEM)
-    edge_spec = pl.BlockSpec((1, 1, fields, 2, cols), lambda t: (side, t, 0, 0, 0))
+    edge_spec = pl.BlockSpec((1, layers, fields, 2, cols), lambda t: (side, 0, 0, 0, 0))
     side_spec = pl.BlockSpec(left.shape, lambda t: (0, 0, 0))
+    steps = layers // 2
     return pl.pallas_call(
         functools.partial(stencil_kernel, side, layers),
-        grid=(layers,),
+        grid=(steps,),
         out_shape=jax.ShapeDtypeStruct(state.shape, jnp.float32),
         in_specs=[smem, smem, pl.BlockSpec(memory_space=pl.ANY), edge_spec, edge_spec, side_spec, side_spec, vmem, vmem],
         out_specs=pl.BlockSpec(
-            (fields, 1, rows, cols), lambda t: (0, t if side == 0 else layers - 1 - t, 0, 0)
+            (fields, 2, rows, cols), lambda t: (0, t if side == 0 else steps - 1 - t, 0, 0)
         ),
         scratch_shapes=[
             pltpu.VMEM((fields, layers + 4, rows, cols), jnp.float32),
-            pltpu.VMEM((fields, 2 * rows, cols), jnp.float32),
-            pltpu.VMEM((fields * rows, 2 * cols), jnp.float32),
+            pltpu.VMEM((2, fields, 2 * rows, cols), jnp.float32),
+            pltpu.VMEM((2, fields * rows, 2 * cols), jnp.float32),
             pltpu.VMEM((fields * rows, 2 * cols + 2 * LANES), jnp.bfloat16),
             pltpu.SemaphoreType.DMA((layers,)),
         ],
-        compiler_params=pltpu.CompilerParams(vmem_limit_bytes=VMEM_LIMIT),
+        compiler_params=pltpu.CompilerParams(vmem_limit_bytes=WIDE),
         cost_estimate=pl.CostEstimate(
             flops=60 * state.size, bytes_accessed=16 * state.size, transcendentals=0
         ),
@@ -397,7 +448,7 @@
         ],
         out_specs=specs,
         input_output_aliases={2: 0, 3: 1},
-        compiler_params=pltpu.CompilerParams(vmem_limit_bytes=VMEM_LIMIT),
+        compiler_params=pltpu.CompilerParams(vmem_limit_bytes=NARROW),
         cost_estimate=pl.CostEstimate(
             flops=30 * modes.size, bytes_accessed=12 * modes.size, transcendentals=0
         ),
@@ -415,14 +466,11 @@
     spans = lax.axis_size("span")
     step = rows // count
 
-    def by_owner(planes):
-        return jnp.moveaxis(planes.reshape(fields, 2, count, step, cols), 2, 0)
-
-    planes = jnp.stack([by_owner(stator[:, layers - 2 :][:, ::-1]), by_owner(rotor[:, :2])], axis=1)
-    planes = planes.reshape(count, 2, fields * 2 * step, cols)
+    planes = interface_planes(stator, rotor, count).reshape(count, 2, fields * 2 * step, cols)
+
+    planes, *states = lax.optimization_barrier((planes, stator, rotor))
     received = lax.all_to_all(planes, "pitch", 0, 0, tiled=True)
-
-    low, high, left, right = pack_edges(stator, rotor)
+    low, high, left, right = pack_edges(*states)
     ring = [(i, (i + 1) % count) for i in range(count)]
     line = [(i, i + 1) for i in range(spans - 1)]
     from_left = lax.ppermute(right, "pitch", ring)
@@ -441,15 +489,14 @@
 
     edges = (from_below, from_above, from_left, from_right)
     mix = field_mix.reshape(-1)
-    stator_mid = stencil(0, stator, *edges, weights[0].reshape(-1), mix)
-    received, stator_mid = lax.optimization_barrier((received, stator_mid))
-
     blend = mode_blend.reshape(fields, LANES, OUTER) * (1.0 / NP)
     blend = jnp.moveaxis(blend, 2, 0)[outer_order().reshape(-1)]
     blend = blend.reshape(PAIRS, 2, fields, LANES).transpose(0, 2, 1, 3).reshape(PAIRS, fields, 2 * LANES)
+    received, edges = lax.optimization_barrier((received, edges))
     sent = transform(received, rotor_offset, blend, fields)
     modes = lax.all_to_all(sent, "pitch", 0, 0, tiled=True)
     modes = modes.reshape(count, 2, fields, 2, step, cols)
+    stator_mid = stencil(0, stator, *edges, weights[0].reshape(-1), mix)
     rotor_mid = stencil(1, rotor, *edges, weights[1].reshape(-1), mix)
     return close(modes, stator_mid, rotor_mid, rim_weights.reshape(-1))
 

time: 111 us -> 134 us (1.21)
  Pallas kernels: 58.4 us -> 97.9 us
  waiting for transfers between devices: 15.9 us -> 6.7 us
  local copies, waits for them, and re-layouts: 10.3 us -> 4.75 us
  starting transfers between devices: 22.5 us -> 19.3 us
    pallas_call x2 -> x3, Pallas kernels: 35.7 us -> 77.2 us  [the longest x1 41.1 us: interface_planes(): pl.pallas_call(planes_kernel, out_shape=jax.ShapeDtypeStruct((count, 2, f...]
    all_to_all x1, waiting for transfers between devices: 12.1 us -> 0.01 us  [shards(): modes = lax.all_to_all(sent, 'pitch', 0, 0, tiled=True)]
    all_to_all x1, waiting for transfers between devices: 0.01 us -> 3.95 us  [shards(): received = lax.all_to_all(planes, 'pitch', 0, 0, tiled=True)]
    all_to_all x1, starting transfers between devices: 7.86 us -> 3.96 us  [shards(): modes = lax.all_to_all(sent, 'pitch', 0, 0, tiled=True)]
    unnamed x24 -> x12, local copies, waits for them, and re-layouts: 3.68 us -> 0.04 us
    pallas_call x1, Pallas kernels: 5.35 us -> 3.38 us  [transform(): pl.pallas_call(functools.partial(transform_kernel, fields), out_shape=jax...]
    mul x2, local copies, waits for them, and re-layouts: 0.3 us -> 2.01 us  [shards(): blend = mode_blend.reshape(fields, LANES, OUTER) * (1.0 / NP)]
  transfers between devices with their start and end apart: 6 -> 6, of which waited for: 2 -> 2; matrix products, arithmetic and copies ran while one was open for 4% -> 6% of each run, Pallas kernels for 44% -> 37%
where the time goes in v3:
time: 134 us; the launch traced here: 133 us
  Pallas kernels  97.9 us (73%)
  starting transfers between devices  19.3 us (14%)
  waiting for transfers between devices  6.7 us (5%)
  local copies, waits for them, and re-layouts  4.75 us (4%)
  other arithmetic  2.1 us (2%)
  between operations  1.49 us (1%)
    pallas_call x1, Pallas kernels, interface_planes(): pl.pallas_call(planes_kernel, out_shape=jax.ShapeDtypeStruct((count, 2, f...  41.1 us
    pallas_call x2, Pallas kernels, stencil(): pl.pallas_call(functools.partial(stencil_kernel, side, layers), grid=(ste...  36.1 us
    pallas_call x1, Pallas kernels, pack_edges(): pl.pallas_call(pack_kernel, grid=(layers,), out_shape=(edge, edge, side,...  13.5 us
    all_to_all x1, starting transfers between devices, shards(): received = lax.all_to_all(planes, 'pitch', 0, 0, tiled=True)  7.26 us
    all_to_all x1, starting transfers between devices, shards(): modes = lax.all_to_all(sent, 'pitch', 0, 0, tiled=True)  3.96 us
    all_to_all x1, waiting for transfers between devices, shards(): received = lax.all_to_all(planes, 'pitch', 0, 0, tiled=True)  3.95 us
    pallas_call x1, Pallas kernels, close(): pl.pallas_call(close_kernel, grid=(count // group,), out_shape=(shape, sh...  3.88 us
    pallas_call x1, Pallas kernels, transform(): pl.pallas_call(functools.partial(transform_kernel, fields), out_shape=jax...  3.38 us
  transfers between devices with their start and end apart: 6, of which 2 were waited for; matrix products, arithmetic and copies ran while one was open for 6% of the time, Pallas kernels for 37%

profile of v3, /device:TPU:0, one launch (start us, length us, event | category | flops | bytes accessed | tf_op | source)
XLA Modules:
  0.0 133.1 jit_solution(5646732588725009922)
XLA Ops:
  0.6 41.1 %planes.1 = f32[8,2,5,2,8,256]{5,4,3,2,1,0:T(8,128)} custom-call(f32[5,16,64,256]{3,2,1,0:T(8,128)} %source.2, f32[5,16,64,256]{3,2,1,0:T(8,128)} %source.3), custom_call_target="tpu_custom_call" | custom-call | tf_op jit(solution)/shard_map/planes/pallas_call | solution.py:185
  41.7 7.3 %all-to-all-start = ((f32[8,2,80,256]{3,2,1,0:T(8,128)}), f32[8,2,80,256]{3,2,1,0:T(8,128)S(1)}, u32[]{:S(2)}, u32[]{:S(2)}) async-start(f32[8,2,80,256]{3,2,1,0:T(8,128)} %bitcast.21), calls=%async_computation | async-start | bytes 2621440 | tf_op jit(solution)/shard_map/all_to_all | solution.py:472
  49.0 0.0 copy-start.3
  49.0 0.0 copy-start.5
  49.0 0.0 copy-start
  49.0 0.0 copy-start.1
  49.0 13.5 %edges.1 = (f32[2,16,5,2,256]{4,3,2,1,0:T(2,128)}, f32[2,16,5,2,256]{4,3,2,1,0:T(2,128)}, f32[3,64,128]{2,1,0:T(8,128)}, f32[3,64,128]{2,1,0:T(8,128)}) custom-call(f32[5,16,64,256]{3,2,1,0:T(8,128)} %source.2, f32[5,16,64,256]{3,2,1,0:T(8,128)} %source.3), custom_call_target="tpu_custom_call" | custom-call | bytes 10485760 | tf_op jit(solution)/shard_map/edges/pallas_call | solution.py:228
  62.5 0.0 copy-start.4
  62.5 0.0 copy-start.2
  62.5 2.1 %collective-permute-start.2 = (f32[3,64,128]{2,1,0:T(8,128)}, f32[3,64,128]{2,1,0:T(8,128)}, u32[]{:S(2)}, u32[]{:S(2)}) collective-permute-start(f32[3,64,128]{2,1,0:T(8,128)} %get-tuple-element.19), channel_id=1, source_target_pairs={{0,4},{4,8},{8,12},{12,16},{16,20},{20,24},{24,28},{28,0},{1,5},{5... | collective-permute-start | bytes 294920 | tf_op jit(solution)/shard_map/ppermute | solution.py:476
  64.6 2.8 %collective-permute-start.3 = (f32[3,64,128]{2,1,0:T(8,128)}, f32[3,64,128]{2,1,0:T(8,128)}, u32[]{:S(2)}, u32[]{:S(2)}) collective-permute-start(f32[3,64,128]{2,1,0:T(8,128)} %get-tuple-element.20), channel_id=1, source_target_pairs={{4,0},{8,4},{12,8},{16,12},{20,16},{24,20},{28,24},{0,28},{5,1},{9... | collective-permute-start | bytes 294920 | tf_op jit(solution)/shard_map/ppermute | solution.py:477
  67.4 2.0 %collective-permute-start = (f32[2,16,5,2,256]{4,3,2,1,0:T(2,128)}, f32[2,16,5,2,256]{4,3,2,1,0:T(2,128)}, u32[]{:S(2)}, u32[]{:S(2)}) collective-permute-start(f32[2,16,5,2,256]{4,3,2,1,0:T(2,128)} %get-tuple-element.17), channel_id=1, source_target_pairs={{0,1},{1,2},{2,3},{4,5},{5,6},{6,7},{8,9},{9,10},{10,11},{12,13},{... | collective-permute-start | bytes 983048 | tf_op jit(solution)/shard_map/ppermute | solution.py:478
  69.4 1.3 collective-permute-start.1
  70.7 0.0 copy-done.3
  71.3 0.9 mul.76
  72.2 1.1 copy.30
  73.3 0.0 copy-done.5
  73.4 0.6 pad_clamp_fusion
  74.0 0.7 gather_fusion
  74.7 2.7 %collective-permute-done.2.left_ref = f32[3,64,128]{2,1,0:T(8,128)} collective-permute-done((f32[3,64,128]{2,1,0:T(8,128)}, f32[3,64,128]{2,1,0:T(8,128)}, u32[]{:S(2)}, u32[]{:S(2)}) %collective-permute-start.2) | collective-permute-done | bytes 98336 | tf_op jit(solution)/shard_map/ppermute | solution.py:476
  77.5 0.0 collective-permute-done.3.right_ref
  77.5 0.0 collective-permute-done.low_ref
  77.5 0.0 collective-permute-done.1.high_ref
  77.5 3.9 %all-to-all-done.got_ref = f32[8,2,80,256]{3,2,1,0:T(8,128)S(1)} async-done(((f32[8,2,80,256]{3,2,1,0:T(8,128)}), f32[8,2,80,256]{3,2,1,0:T(8,128)S(1)}, u32[]{:S(2)}, u32[]{:S(2)}) %all-to-all-start) | async-done | bytes 1310752 | tf_op jit(solution)/shard_map/all_to_all | solution.py:472
  81.4 0.0 copy-done
  81.4 0.0 copy-done.1
  81.5 3.4 %modes.1 = f32[8,2,80,256]{3,2,1,0:T(8,128)} custom-call(s32[1]{0:T(128)S(6)} %copy.43.offset_ref, f32[8,2,80,256]{3,2,1,0:T(8,128)S(1)} %all-to-all-done.got_ref, f32[8,5,256]{2,1,0:T(8,128)S(1)} %copy.32.blend_ref, bf16[8,256,256]{2,1,0:T(8,128)(2,1)S(1)} %copy-done.1, bf16[8,256,256]{2,1,0:T(8,128)(2,1)S(1)} %copy-done), custom_call_target="tpu_custom_call" | custom-call | flops 503316480 | bytes 5000000 | tf_op jit(solution)/shard_map/modes/pallas_call | solution.py:142
  84.8 4.0 %all-to-all-start.1 = ((f32[8,2,80,256]{3,2,1,0:T(8,128)}), f32[8,2,80,256]{3,2,1,0:T(8,128)S(1)}, u32[]{:S(2)}, u32[]{:S(2)}) async-start(f32[8,2,80,256]{3,2,1,0:T(8,128)} %modes.1), calls=%async_computation.1 | async-start | bytes 2621440 | tf_op jit(solution)/shard_map/all_to_all | solution.py:497
  88.8 0.0 copy-done.4
  88.8 0.7 reshape.37.mix_ref
  89.4 0.0 copy-done.2
  89.4 0.7 multiply_bitcast_fusion
  90.2 0.8 fusion.1
  91.0 0.7 broadcast_multiply_fusion.1
  91.8 0.1 reshape.32.weight_ref
  91.9 0.6 reshape_squeeze.7.jac_ref
  92.5 0.6 reshape_squeeze.6.jac_ref
  93.1 18.0 %rotor_stencil.1.rotor_ref = f32[5,16,64,256]{3,2,1,0:T(8,128)} custom-call(f32[75]{0:T(128)} %reshape_squeeze.7.jac_ref, f32[25]{0:T(128)} %reshape.37.mix_ref, f32[5,16,64,256]{3,2,1,0:T(8,128)} %source.3, f32[2,16,5,2,256]{4,3,2,1,0:T(2,128)} %collective-permute-done.low_ref, f32[2,16,5,2,256]{4,3,2,1,0:T(2,128)} %collective-permute-done.1.high_ref, ...), custom_call_target="tpu_custom_call" | custom-call | flops 78643200 | bytes 20971520 | tf_op jit(solution)/shard_map/rotor_stencil/pallas_call | solution.py:385
  111.1 18.1 %stator_stencil.1.stator_ref = f32[5,16,64,256]{3,2,1,0:T(8,128)} custom-call(f32[75]{0:T(128)} %reshape_squeeze.6.jac_ref, f32[25]{0:T(128)} %reshape.37.mix_ref, f32[5,16,64,256]{3,2,1,0:T(8,128)} %source.2, f32[2,16,5,2,256]{4,3,2,1,0:T(2,128)} %collective-permute-done.low_ref, f32[2,16,5,2,256]{4,3,2,1,0:T(2,128)} %collective-permute-done.1.high_ref, ...), custom_call_target="tpu_custom_call" | custom-call | flops 78643200 | bytes 20971520 | tf_op jit(solution)/shard_map/stator_stencil/pallas_call | solution.py:385
  129.2 0.0 all-to-all-done.1
  129.2 3.9 %interface.1 = (f32[5,16,64,256]{3,2,1,0:T(8,128)}, f32[5,16,64,256]{3,2,1,0:T(8,128)}) custom-call(f32[100]{0:T(128)S(1)} %reshape.32.weight_ref, f32[8,2,5,2,8,256]{5,4,3,2,1,0:T(8,128)S(1)} %bitcast.20, f32[5,16,64,256]{3,2,1,0:T(8,128)} %stator_stencil.1.stator_ref, ...), custom_call_target="tpu_custom_call", output_to_operand_aliasing={{0}: (2, {}), {1}: (3, {})} | custom-call | flops 9830400 | bytes 3932160 | tf_op jit(solution)/shard_map/interface/pallas_call | solution.py:440
  (14 shorter events, 0.1 us)
Async XLA Ops:
  41.7 39.7 %all-to-all-start = ((f32[8,2,80,256]{3,2,1,0:T(8,128)}), f32[8,2,80,256]{3,2,1,0:T(8,128)S(1)}, u32[]{:S(2)}, u32[]{:S(2)}) async-start(f32[8,2,80,256]{3,2,1,0:T(8,128)} %bitcast.21), calls=%async_computation | async-start | bytes 2621440 | tf_op jit(solution)/shard_map/all_to_all | solution.py:472
  49.0 21.7 %copy-start.3 = (f32[5,2048]{1,0:T(8,128)S(1)}, f32[5,2048]{1,0:T(8,128)}, u32[]{:S(2)}) copy-start(f32[5,2048]{1,0:T(8,128)} %param.20) | copy-start | bytes 122884
  49.0 24.3 %copy-start.5 = (s32[16]{0:T(128)S(1)}, s32[16]{0:T(128)}, u32[]{:S(2)}) copy-start(s32[16]{0:T(128)} %constant.36) | copy-start | bytes 196
  49.0 32.4 %copy-start = (bf16[8,256,256]{2,1,0:T(8,128)(2,1)S(1)}, bf16[8,256,256]{2,1,0:T(8,128)(2,1)}, u32[]{:S(2)}) copy-start(bf16[8,256,256]{2,1,0:T(8,128)(2,1)} %constant.32.clone.low_ref) | copy-start | bytes 3145732
  49.0 32.4 %copy-start.1 = (bf16[8,256,256]{2,1,0:T(8,128)(2,1)S(1)}, bf16[8,256,256]{2,1,0:T(8,128)(2,1)}, u32[]{:S(2)}) copy-start(bf16[8,256,256]{2,1,0:T(8,128)(2,1)} %constant.31.clone.high_ref) | copy-start | bytes 3145732
  62.5 26.3 %copy-start.4 = (f32[5,5]{1,0:T(8,128)S(1)}, f32[5,5]{1,0:T(8,128)}, u32[]{:S(2)}) copy-start(f32[5,5]{1,0:T(8,128)} %param.19) | copy-start | bytes 304
  62.5 26.9 %copy-start.2 = (f32[3,5,5]{2,0,1:T(4,128)S(1)}, f32[3,5,5]{2,0,1:T(4,128)}, u32[]{:S(2)}) copy-start(f32[3,5,5]{2,0,1:T(4,128)} %param.18) | copy-start | bytes 904
  62.5 14.9 %collective-permute-start.2 = (f32[3,64,128]{2,1,0:T(8,128)}, f32[3,64,128]{2,1,0:T(8,128)}, u32[]{:S(2)}, u32[]{:S(2)}) collective-permute-start(f32[3,64,128]{2,1,0:T(8,128)} %get-tuple-element.19), channel_id=1, source_target_pairs={{0,4},{4,8},{8,12},{12,16},{16,20},{20,24},{24,28},{28,0},{1,5},{5... | collective-permute-start | bytes 294920 | tf_op jit(solution)/shard_map/ppermute | solution.py:476
  64.6 12.9 %collective-permute-start.3 = (f32[3,64,128]{2,1,0:T(8,128)}, f32[3,64,128]{2,1,0:T(8,128)}, u32[]{:S(2)}, u32[]{:S(2)}) collective-permute-start(f32[3,64,128]{2,1,0:T(8,128)} %get-tuple-element.20), channel_id=1, source_target_pairs={{4,0},{8,4},{12,8},{16,12},{20,16},{24,20},{28,24},{0,28},{5,1},{9... | collective-permute-start | bytes 294920 | tf_op jit(solution)/shard_map/ppermute | solution.py:477
  67.4 10.1 %collective-permute-start = (f32[2,16,5,2,256]{4,3,2,1,0:T(2,128)}, f32[2,16,5,2,256]{4,3,2,1,0:T(2,128)}, u32[]{:S(2)}, u32[]{:S(2)}) collective-permute-start(f32[2,16,5,2,256]{4,3,2,1,0:T(2,128)} %get-tuple-element.17), channel_id=1, source_target_pairs={{0,1},{1,2},{2,3},{4,5},{5,6},{6,7},{8,9},{9,10},{10,11},{12,13},{... | collective-permute-start | bytes 983048 | tf_op jit(solution)/shard_map/ppermute | solution.py:478
  69.4 8.1 %collective-permute-start.1 = (f32[2,16,5,2,256]{4,3,2,1,0:T(2,128)}, f32[2,16,5,2,256]{4,3,2,1,0:T(2,128)}, u32[]{:S(2)}, u32[]{:S(2)}) collective-permute-start(f32[2,16,5,2,256]{4,3,2,1,0:T(2,128)} %get-tuple-element.18), channel_id=1, source_target_pairs={{1,0},{2,1},{3,2},{5,4},{6,5},{7,6},{9,8},{10,9},{11,10},{13,12},{... | collective-permute-start | bytes 983048 | tf_op jit(solution)/shard_map/ppermute | solution.py:479
  84.8 44.4 %all-to-all-start.1 = ((f32[8,2,80,256]{3,2,1,0:T(8,128)}), f32[8,2,80,256]{3,2,1,0:T(8,128)S(1)}, u32[]{:S(2)}, u32[]{:S(2)}) async-start(f32[8,2,80,256]{3,2,1,0:T(8,128)} %modes.1), calls=%async_computation.1 | async-start | bytes 2621440 | tf_op jit(solution)/shard_map/all_to_all | solution.py:497

commit v4 on v3

--- a/solution.py
+++ b/solution.py
@@ -156,82 +156,77 @@
     )(offset, received, blend, jnp.asarray(high), jnp.asarray(low))
 
 
-def planes_kernel(stator, rotor, out, sems):
+def planes_kernel(stator, rotor, out):
     count, _, _, _, step, _ = out.shape
-    layers = stator.shape[1]
-    copies = []
     for q in range(count):
-        span = pl.ds(q * step, step)
+        span = slice(q * step, (q + 1) * step)
         for ghost in range(2):
-            copies.append((stator.at[:, layers - 1 - ghost, span], out.at[q, 0, :, ghost]))
-            copies.append((rotor.at[:, ghost, span], out.at[q, 1, :, ghost]))
-    copies = [pltpu.make_async_copy(a, b, sems.at[i]) for i, (a, b) in enumerate(copies)]
-    for copy in copies:
-        copy.start()
-    for copy in copies:
-        copy.wait()
+            out[q, 0, :, ghost] = stator[:, 1 - ghost, span, :]
+            out[q, 1, :, ghost] = rotor[:, ghost, span, :]
 
 
 def interface_planes(stator, rotor, count):
     fields, layers, rows, cols = stator.shape
     step = rows // count
-    if step % 8:
-
-        def by_owner(planes):
-            return jnp.moveaxis(planes.reshape(fields, 2, count, step, cols), 2, 0)
-
-        return jnp.stack([by_owner(stator[:, layers - 2 :][:, ::-1]), by_owner(rotor[:, :2])], axis=1)
-    hbm = pl.BlockSpec(memory_space=pl.ANY)
+    group = max(1, count // 2)
+    block = (fields, 2, group * step, cols)
     return pl.pallas_call(
         planes_kernel,
+        grid=(count // group,),
         out_shape=jax.ShapeDtypeStruct((count, 2, fields, 2, step, cols), jnp.float32),
-        in_specs=[hbm, hbm],
-        out_specs=hbm,
-        scratch_shapes=[pltpu.SemaphoreType.DMA((4 * count,))],
+        in_specs=[
+            pl.BlockSpec(block, lambda q: (0, layers // 2 - 1, q, 0)),
+            pl.BlockSpec(block, lambda q: (0, 0, q, 0)),
+        ],
+        out_specs=pl.BlockSpec((group, 2, fields, 2, step, cols), lambda q: (q, 0, 0, 0, 0, 0)),
         compiler_params=pltpu.CompilerParams(vmem_limit_bytes=WIDE),
         name="planes",
     )(stator, rotor)
 
 
 def pack_kernel(stator_ref, rotor_ref, low_ref, high_ref, left_ref, right_ref):
-    step = pl.program_id(0)
-    fields, _, rows, cols = stator_ref.shape
+    fields, layers, rows, cols = stator_ref.shape
     lane = lax.broadcasted_iota(jnp.int32, (rows, LANES), 1)
-    for side, ref in enumerate((stator_ref, rotor_ref)):
-        unit = 2 * step + side
-        place, first = unit // UNITS, unit % UNITS * (2 * fields)
-        left = jnp.zeros((rows, LANES), jnp.float32)
-        right = jnp.zeros((rows, LANES), jnp.float32)
-        for f in range(fields):
-            low_ref[side, 0, f] = ref[f, 0, :2, :]
-            high_ref[side, 0, f] = ref[f, 0, rows - 2 :, :]
-            here = lane // 2 == f
-            a, b = ref[f, 0, :, :LANES], ref[f, 0, :, cols - LANES :]
-            left = jnp.where(here, pltpu.roll(a, 2 * f, 1) if f else a, left)
-            right = jnp.where(here, pltpu.roll(b, 2 * f + 2, 1), right)
-        left = pltpu.roll(left, first, 1)
-        right = pltpu.roll(right, first, 1)
-
-        fresh = (lane >= first) & (lane < first + 2 * fields)
-        left_ref[place] = jnp.where(fresh, left, left_ref[place])
-        right_ref[place] = jnp.where(fresh, right, right_ref[place])
+    for layer in range(layers):
+        for side, ref in enumerate((stator_ref, rotor_ref)):
+            taken = layer if side == 0 else layers - 1 - layer
+            unit = 2 * (pl.program_id(0) * layers + layer) + side
+            place, first = unit // UNITS, unit % UNITS * (2 * fields)
+            left = jnp.zeros((rows, LANES), jnp.float32)
+            right = jnp.zeros((rows, LANES), jnp.float32)
+            for f in range(fields):
+                low_ref[side, layer, f] = ref[f, taken, :2, :]
+                high_ref[side, layer, f] = ref[f, taken, rows - 2 :, :]
+                ends = jnp.where(
+                    lane < LANES // 2, ref[f, taken, :, :LANES], ref[f, taken, :, cols - LANES :]
+                )
+                ends = pltpu.roll(ends, 2 * f, 1) if f else ends
+                left = jnp.where(lane // 2 == f, ends, left)
+                right = jnp.where(lane // 2 == (f - 1) % (LANES // 2), ends, right)
+            fresh = (lane >= first) & (lane < first + 2 * fields)
+            left_ref[place] = jnp.where(fresh, pltpu.roll(left, first, 1), left_ref[place])
+            after = jnp.where(lane < LANES - 2, lane + 2, lane + 2 - LANES)
+            fresh = (after >= first) & (after < first + 2 * fields)
+            right_ref[place] = jnp.where(fresh, pltpu.roll(right, first, 1), right_ref[place])
 
 
 def pack_edges(stator, rotor):
     fields, layers, rows, cols = stator.shape
     blocks = -(-2 * layers // UNITS)
-    one = (fields, 1, rows, cols)
+    each = max(n for n in (4, 2, 1) if layers % n == 0)
+    steps = layers // each
+    block = (fields, each, rows, cols)
     edge = jax.ShapeDtypeStruct((2, layers, fields, 2, cols), jnp.float32)
     side = jax.ShapeDtypeStruct((blocks, rows, LANES), jnp.float32)
-    edge_spec = pl.BlockSpec((2, 1, fields, 2, cols), lambda t: (0, t, 0, 0, 0))
+    edge_spec = pl.BlockSpec((2, each, fields, 2, cols), lambda t: (0, t, 0, 0, 0))
     side_spec = pl.BlockSpec((blocks, rows, LANES), lambda t: (0, 0, 0))
     return pl.pallas_call(
         pack_kernel,
-        grid=(layers,),
+        grid=(steps,),
         out_shape=(edge, edge, side, side),
         in_specs=[
-            pl.BlockSpec(one, lambda t: (0, t, 0, 0)),
-            pl.BlockSpec(one, lambda t: (0, layers - 1 - t, 0, 0)),
+            pl.BlockSpec(block, lambda t: (0, t, 0, 0)),
+            pl.BlockSpec(block, lambda t: (0, steps - 1 - t, 0, 0)),
         ],
         out_specs=(edge_spec, edge_spec, side_spec, side_spec),
         compiler_params=pltpu.CompilerParams(vmem_limit_bytes=WIDE),
@@ -244,7 +239,7 @@
 
 def difference_tables(rows, cols):
     scale = time_step * damping
-    slope = {1: 1.0, -1: -1.0}
+    slope = {1: -0.5 * time_step, -1: 0.5 * time_step}
     smooth = {0: -6.0 * scale, 1: 4.0 * scale, -1: 4.0 * scale, 2: -scale, -2: -scale}
 
     def banded(extent, halo_places, halo_width):
@@ -280,6 +275,7 @@
     fields, _, rows, cols = out.shape
     chunk = 16
     scale = time_step * damping
+    axial = (0.5 if side else -0.5) * time_step
     lane = lax.broadcasted_iota(jnp.int32, (rows, LANES), 1)
 
     def load(layer):
@@ -289,13 +285,13 @@
     def products(t, slot):
         unit = 2 * t + side
         place, first = unit // UNITS, unit % UNITS * (2 * fields)
-        turn = (LANES - first) % LANES
-        from_left = pltpu.roll(left_ref[place], turn, 1)
-        from_right = pltpu.roll(right_ref[place], turn, 1)
+        from_left, from_right = left_ref[place], right_ref[place]
         for f in range(fields):
-            shift = (LANES - 2 * f) % LANES
-            rim = jnp.where(lane < 2, pltpu.roll(from_right, shift, 1) if shift else from_right, 0.0)
-            rim = jnp.where(lane < LANES - 2, rim, pltpu.roll(from_left, LANES - 2 * f - 2, 1))
+            at = first + 2 * f
+            before = jnp.where(lane < LANES - 2, lane + 2, lane + 2 - LANES)
+            rim = jnp.where((before >= at) & (before < at + 2), from_left, from_right)
+            rim = pltpu.roll(rim, (LANES - at) % LANES, 1)
+            rim = jnp.where((lane < 2) | (lane >= LANES - 2), rim, 0.0)
             span = slice(f * rows, (f + 1) * rows)
             x_high, x_low = halves(state[f, t + 2])
             rim_high, rim_low = halves(rim)
@@ -332,13 +328,13 @@
                 )
             for g in range(fields):
                 slopes = (
-                    state[g, here + 1, span, :] - state[g, here - 1, span, :],
+                    (state[g, here + 1, span, :] - state[g, here - 1, span, :]) * axial,
                     radial[slot, g, span, :],
                     pitch[slot, g * rows + at : g * rows + at + chunk, :cols],
                 )
                 for d in range(3):
                     for f in range(fields):
-                        totals[f] = totals[f] + jac_ref[(d * fields + f) * fields + g] * slopes[d]
+                        totals[f] = totals[f] + jac_ref[d, f, g] * slopes[d]
             for f in range(fields):
                 out[f, slot if side == 0 else 1 - slot, span, :] = totals[f]
 
@@ -349,7 +345,6 @@
         state[:, 0:2] = jnp.zeros((fields, 2, rows, cols), jnp.float32)
         load(0).wait()
         load(1).wait()
-        products(0, 0)
 
     @pl.when(2 * step + 2 < layers)
     def _():
@@ -363,15 +358,15 @@
                 span = slice(at, at + chunk)
                 planes = [state[g, layers + 1 - ghost, span, :] for g in range(fields)]
                 for f in range(fields):
-                    total = mix_ref[f * fields] * planes[0]
+                    total = mix_ref[f, 0] * planes[0]
                     for g in range(1, fields):
-                        total = total + mix_ref[f * fields + g] * planes[g]
+                        total = total + mix_ref[f, g] * planes[g]
                     state[f, layers + 2 + ghost, span, :] = total
 
-    products(2 * step + 1, 1)
-    advance(2 * step, 0)
-    products(jnp.minimum(2 * step + 2, layers - 1), 0)
-    advance(2 * step + 1, 1)
+    for slot in range(2):
+        products(2 * step + slot, slot)
+    for slot in range(2):
+        advance(2 * step + slot, slot)
 
 
 def stencil(side, state, low, high, left, right, weights, mix):
@@ -405,29 +400,36 @@
     )(weights, mix, state, low, high, left, right, jnp.asarray(along_rows), jnp.asarray(along_cols))
 
 
-def close_kernel(weight_ref, modes_ref, stator_ref, rotor_ref, stator_out, rotor_out):
-    fields, _, rows, cols = stator_ref.shape
+def close_kernel(jac_ref, mix_ref, modes_ref, stator_ref, rotor_ref, stator_out, rotor_out):
+    fields = stator_ref.shape[0]
     count = modes_ref.shape[0]
     step = modes_ref.shape[4]
+    scale = time_step * damping
+
+    def combine(row, sources):
+        total = row(0) * sources[0]
+        for g in range(1, fields):
+            total = total + row(g) * sources[g]
+        return total
+
     for side, (ref, out) in enumerate(((stator_ref, stator_out), (rotor_ref, rotor_out))):
         near, far = (1, 0) if side == 0 else (0, 1)
+        sign = -1.0 if side else 1.0
         for q in range(count):
             span = slice(q * step, (q + 1) * step)
-            first = [modes_ref[q, side, g, 0] for g in range(fields)]
-            second = [modes_ref[q, side, g, 1] for g in range(fields)]
+            ghosts = []
+            for ghost in range(2):
+                planes = [modes_ref[q, side, g, ghost] for g in range(fields)]
+                ghosts.append([combine(lambda g: mix_ref[f, g], planes) for f in range(fields)])
+            first, second = ghosts
             for f in range(fields):
-                rim, inner = ref[f, near, span, :], ref[f, far, span, :]
-                for g in range(fields):
-                    at = (side * 2 * fields + f) * fields + g
-                    weight_near = weight_ref[at]
-                    weight_far = weight_ref[at + fields * fields]
-                    rim = rim + (weight_near * first[g] + weight_far * second[g])
-                    inner = inner + weight_far * first[g]
-                out[f, near, span, :] = rim
-                out[f, far, span, :] = inner
-
-
-def close(modes, stator, rotor, weights):
+                slope = combine(lambda g: jac_ref[0, f, g], first) * (-0.5 * time_step)
+                bend = first[f] * 4.0 - second[f]
+                out[f, near, span, :] = ref[f, near, span, :] + (slope + bend * (sign * scale))
+                out[f, far, span, :] = ref[f, far, span, :] - first[f] * (sign * scale)
+
+
+def close(modes, stator, rotor, jacobians, field_mix):
     fields, layers, rows, cols = stator.shape
     count, _, _, _, step, _ = modes.shape
     group = max(1, count // 4)
@@ -443,21 +445,18 @@
         out_shape=(shape, shape),
         in_specs=[
             pl.BlockSpec(memory_space=pltpu.SMEM),
+            pl.BlockSpec(memory_space=pltpu.SMEM),
             pl.BlockSpec((group,) + modes.shape[1:], lambda q: (q, 0, 0, 0, 0, 0)),
             *specs,
         ],
         out_specs=specs,
-        input_output_aliases={2: 0, 3: 1},
+        input_output_aliases={3: 0, 4: 1},
         compiler_params=pltpu.CompilerParams(vmem_limit_bytes=NARROW),
         cost_estimate=pl.CostEstimate(
             flops=30 * modes.size, bytes_accessed=12 * modes.size, transcendentals=0
         ),
         name="interface",
-    )(weights, modes, stator, rotor)
-
-
-def exact_dot(a, b):
-    return jnp.matmul(a, b, precision=lax.Precision.HIGHEST)
+    )(jacobians, field_mix, modes, stator, rotor)
 
 
 def shards(stator, rotor, jacobians, field_mix, mode_blend, rotor_offset):
@@ -478,17 +477,7 @@
     from_below = lax.ppermute(high, "span", line)
     from_above = lax.ppermute(low, "span", [(b, a) for a, b in line])
 
-    mirrored = jacobians * jnp.array([-1.0, 1.0, 1.0], jnp.float32)[:, None, None]
-    courses = jnp.stack([jacobians, mirrored])
-    weights = (-0.5 * time_step) * courses
-    mixed = exact_dot(courses[:, 0], field_mix)
-    far = (-time_step * damping) * field_mix
-    near = (-0.5 * time_step) * mixed + (4.0 * time_step * damping) * field_mix
-    signs = jnp.array([1.0, -1.0], jnp.float32)[:, None, None]
-    rim_weights = jnp.stack([signs * near, signs * far], axis=1)
-
     edges = (from_below, from_above, from_left, from_right)
-    mix = field_mix.reshape(-1)
     blend = mode_blend.reshape(fields, LANES, OUTER) * (1.0 / NP)
     blend = jnp.moveaxis(blend, 2, 0)[outer_order().reshape(-1)]
     blend = blend.reshape(PAIRS, 2, fields, LANES).transpose(0, 2, 1, 3).reshape(PAIRS, fields, 2 * LANES)
@@ -496,9 +485,9 @@
     sent = transform(received, rotor_offset, blend, fields)
     modes = lax.all_to_all(sent, "pitch", 0, 0, tiled=True)
     modes = modes.reshape(count, 2, fields, 2, step, cols)
-    stator_mid = stencil(0, stator, *edges, weights[0].reshape(-1), mix)
-    rotor_mid = stencil(1, rotor, *edges, weights[1].reshape(-1), mix)
-    return close(modes, stator_mid, rotor_mid, rim_weights.reshape(-1))
+    stator_mid = stencil(0, stator, *edges, jacobians, field_mix)
+    rotor_mid = stencil(1, rotor, *edges, jacobians, field_mix)
+    return close(modes, stator_mid, rotor_mid, jacobians, field_mix)
 
 
 def solution(mesh):

time: 134 us -> 89.4 us (0.67)
  Pallas kernels: 97.9 us -> 51.1 us
  waiting for transfers between devices: 6.7 us -> 13.7 us
  other arithmetic: 2.1 us -> 0.01 us
  local copies, waits for them, and re-layouts: 4.75 us -> 3.28 us
    pallas_call x2, Pallas kernels: 54.6 us -> 9.42 us  [the longest x1 7.22 us: pack_edges(): pl.pallas_call(pack_kernel, grid=(steps,), out_shape=(edge, edge, side, s...]
    ppermute x1, waiting for transfers between devices: 2.74 us -> 9.7 us  [shards(): from_left = lax.ppermute(right, 'pitch', ring)]
    pallas_call x2, Pallas kernels: 36.1 us -> 34.4 us  [stencil(): pl.pallas_call(functools.partial(stencil_kernel, side, layers), grid=(ste...]
  transfers between devices with their start and end apart: 6 -> 6, of which waited for: 2 -> 2; matrix products, arithmetic and copies ran while one was open for 6% -> 4% of each run, Pallas kernels for 37% -> 47%
where the time goes in v4:
time: 89.4 us; the launch traced here: 88.9 us
  Pallas kernels  51.1 us (57%)
  starting transfers between devices  19.4 us (22%)
  waiting for transfers between devices  13.7 us (15%)
  local copies, waits for them, and re-layouts  3.28 us (4%)
  between operations  1.46 us (2%)
    pallas_call x2, Pallas kernels, stencil(): pl.pallas_call(functools.partial(stencil_kernel, side, layers), grid=(ste...  34.4 us
    ppermute x1, waiting for transfers between devices, shards(): from_left = lax.ppermute(right, 'pitch', ring)  9.7 us
    all_to_all x1, starting transfers between devices, shards(): received = lax.all_to_all(planes, 'pitch', 0, 0, tiled=True)  7.25 us
    pallas_call x1, Pallas kernels, pack_edges(): pl.pallas_call(pack_kernel, grid=(steps,), out_shape=(edge, edge, side, s...  7.22 us
    all_to_all x1, starting transfers between devices, shards(): modes = lax.all_to_all(sent, 'pitch', 0, 0, tiled=True)  3.98 us
    all_to_all x1, waiting for transfers between devices, shards(): received = lax.all_to_all(planes, 'pitch', 0, 0, tiled=True)  3.95 us
    pallas_call x1, Pallas kernels, close(): pl.pallas_call(close_kernel, grid=(count // group,), out_shape=(shape, sh...  3.94 us
    pallas_call x1, Pallas kernels, transform(): pl.pallas_call(functools.partial(transform_kernel, fields), out_shape=jax...  3.37 us
  transfers between devices with their start and end apart: 6, of which 2 were waited for; matrix products, arithmetic and copies ran while one was open for 4% of the time, Pallas kernels for 47%

profile of v4, /device:TPU:0, one launch (start us, length us, event | category | flops | bytes accessed | tf_op | source)
XLA Modules:
  0.0 88.9 jit_solution(6234334028588535485)
XLA Ops:
  0.6 2.2 %planes.1 = f32[8,2,5,2,8,256]{5,4,3,2,1,0:T(8,128)} custom-call(f32[5,16,64,256]{3,2,1,0:T(8,128)} %source.2, f32[5,16,64,256]{3,2,1,0:T(8,128)} %source.3), custom_call_target="tpu_custom_call" | custom-call | tf_op jit(solution)/shard_map/planes/pallas_call | solution.py:173
  2.8 7.3 %all-to-all-start = ((f32[8,2,80,256]{3,2,1,0:T(8,128)}), f32[8,2,80,256]{3,2,1,0:T(8,128)S(1)}, u32[]{:S(2)}, u32[]{:S(2)}) async-start(f32[8,2,80,256]{3,2,1,0:T(8,128)} %bitcast.9), calls=%async_computation | async-start | bytes 2621440 | tf_op jit(solution)/shard_map/all_to_all | solution.py:471
  10.1 0.0 copy-start.4
  10.1 0.0 copy-start.6
  10.1 0.0 copy-start
  10.1 0.0 copy-start.1
  10.1 7.2 %edges.1 = (f32[2,16,5,2,256]{4,3,2,1,0:T(2,128)}, f32[2,16,5,2,256]{4,3,2,1,0:T(2,128)}, f32[3,64,128]{2,1,0:T(8,128)}, f32[3,64,128]{2,1,0:T(8,128)}) custom-call(f32[5,16,64,256]{3,2,1,0:T(8,128)} %source.2, f32[5,16,64,256]{3,2,1,0:T(8,128)} %source.3), custom_call_target="tpu_custom_call" | custom-call | bytes 10485760 | tf_op jit(solution)/shard_map/edges/pallas_call | solution.py:223
  17.3 0.0 copy-start.5
  17.4 2.1 %collective-permute-start.2 = (f32[3,64,128]{2,1,0:T(8,128)}, f32[3,64,128]{2,1,0:T(8,128)}, u32[]{:S(2)}, u32[]{:S(2)}) collective-permute-start(f32[3,64,128]{2,1,0:T(8,128)} %get-tuple-element.19), channel_id=1, source_target_pairs={{0,4},{4,8},{8,12},{12,16},{16,20},{20,24},{24,28},{28,0},{1,5},{5... | collective-permute-start | bytes 294920 | tf_op jit(solution)/shard_map/ppermute | solution.py:475
  19.4 2.8 %collective-permute-start.3 = (f32[3,64,128]{2,1,0:T(8,128)}, f32[3,64,128]{2,1,0:T(8,128)}, u32[]{:S(2)}, u32[]{:S(2)}) collective-permute-start(f32[3,64,128]{2,1,0:T(8,128)} %get-tuple-element.20), channel_id=1, source_target_pairs={{4,0},{8,4},{12,8},{16,12},{20,16},{24,20},{28,24},{0,28},{5,1},{9... | collective-permute-start | bytes 294920 | tf_op jit(solution)/shard_map/ppermute | solution.py:476
  22.2 2.0 %collective-permute-start = (f32[2,16,5,2,256]{4,3,2,1,0:T(2,128)}, f32[2,16,5,2,256]{4,3,2,1,0:T(2,128)}, u32[]{:S(2)}, u32[]{:S(2)}) collective-permute-start(f32[2,16,5,2,256]{4,3,2,1,0:T(2,128)} %get-tuple-element.17), channel_id=1, source_target_pairs={{0,1},{1,2},{2,3},{4,5},{5,6},{6,7},{8,9},{9,10},{10,11},{12,13},{... | collective-permute-start | bytes 983048 | tf_op jit(solution)/shard_map/ppermute | solution.py:477
  24.2 1.3 %collective-permute-start.1 = (f32[2,16,5,2,256]{4,3,2,1,0:T(2,128)}, f32[2,16,5,2,256]{4,3,2,1,0:T(2,128)}, u32[]{:S(2)}, u32[]{:S(2)}) collective-permute-start(f32[2,16,5,2,256]{4,3,2,1,0:T(2,128)} %get-tuple-element.18), channel_id=1, source_target_pairs={{1,0},{2,1},{3,2},{5,4},{6,5},{7,6},{9,8},{10,9},{11,10},{13,12},{... | collective-permute-start | bytes 983048 | tf_op jit(solution)/shard_map/ppermute | solution.py:478
  25.5 0.0 copy-done.4
  26.2 0.9 mul.11
  27.0 1.1 %copy.21 = f32[5,128,16]{1,0,2:T(8,128)S(1)} copy(f32[5,128,16]{2,1,0:T(8,128)} %mul.11) | data formatting | bytes 81920 | tf_op jit(solution)/shard_map/mul | solution.py:481
  28.2 0.0 copy-done.6
  28.2 0.6 gather_fusion
  28.9 9.7 %collective-permute-done.2.left_ref = f32[3,64,128]{2,1,0:T(8,128)} collective-permute-done((f32[3,64,128]{2,1,0:T(8,128)}, f32[3,64,128]{2,1,0:T(8,128)}, u32[]{:S(2)}, u32[]{:S(2)}) %collective-permute-start.2) | collective-permute-done | bytes 98336 | tf_op jit(solution)/shard_map/ppermute | solution.py:475
  38.6 0.0 collective-permute-done.3.right_ref
  38.6 0.0 collective-permute-done.low_ref
  38.6 0.0 collective-permute-done.1.high_ref
  38.6 3.9 %all-to-all-done.got_ref = f32[8,2,80,256]{3,2,1,0:T(8,128)S(1)} async-done(((f32[8,2,80,256]{3,2,1,0:T(8,128)}), f32[8,2,80,256]{3,2,1,0:T(8,128)S(1)}, u32[]{:S(2)}, u32[]{:S(2)}) %all-to-all-start) | async-done | bytes 1310752 | tf_op jit(solution)/shard_map/all_to_all | solution.py:471
  42.5 0.0 copy-done
  42.5 0.0 copy-done.1
  42.5 3.4 %modes.1 = f32[8,2,80,256]{3,2,1,0:T(8,128)} custom-call(s32[1]{0:T(128)S(6)} %copy.29.offset_ref, f32[8,2,80,256]{3,2,1,0:T(8,128)S(1)} %all-to-all-done.got_ref, f32[8,5,256]{2,1,0:T(8,128)S(1)} %copy.23.blend_ref, bf16[8,256,256]{2,1,0:T(8,128)(2,1)S(1)} %copy-done.1, bf16[8,256,256]{2,1,0:T(8,128)(2,1)S(1)} %copy-done), custom_call_target="tpu_custom_call" | custom-call | flops 503316480 | bytes 5000000 | tf_op jit(solution)/shard_map/modes/pallas_call | solution.py:142
  45.9 4.0 %all-to-all-start.1 = ((f32[8,2,80,256]{3,2,1,0:T(8,128)}), f32[8,2,80,256]{3,2,1,0:T(8,128)S(1)}, u32[]{:S(2)}, u32[]{:S(2)}) async-start(f32[8,2,80,256]{3,2,1,0:T(8,128)} %modes.1), calls=%async_computation.1 | async-start | bytes 2621440 | tf_op jit(solution)/shard_map/all_to_all | solution.py:486
  49.9 0.0 copy-done.5
  49.9 0.6 copy.26.jac_ref
  50.5 17.2 %rotor_stencil.1.rotor_ref = f32[5,16,64,256]{3,2,1,0:T(8,128)} custom-call(f32[3,5,5]{2,1,0:T(8,128)} %copy.26.jac_ref, f32[5,5]{1,0:T(8,128)} %mix_ref.5, f32[5,16,64,256]{3,2,1,0:T(8,128)} %source.3, f32[2,16,5,2,256]{4,3,2,1,0:T(2,128)} %collective-permute-done.low_ref, f32[2,16,5,2,256]{4,3,2,1,0:T(2,128)} %collective-permute-done.1.high_ref, ...), custom_call_target="tpu_custom_call" | custom-call | flops 78643200 | bytes 20971520 | tf_op jit(solution)/shard_map/rotor_stencil/pallas_call | solution.py:380
  67.7 0.0 copy-start.2
  67.7 0.0 copy-start.3
  67.7 17.2 %stator_stencil.1.stator_ref = f32[5,16,64,256]{3,2,1,0:T(8,128)} custom-call(f32[3,5,5]{2,1,0:T(8,128)} %copy.26.jac_ref, f32[5,5]{1,0:T(8,128)} %mix_ref.5, f32[5,16,64,256]{3,2,1,0:T(8,128)} %source.2, f32[2,16,5,2,256]{4,3,2,1,0:T(2,128)} %collective-permute-done.low_ref, f32[2,16,5,2,256]{4,3,2,1,0:T(2,128)} %collective-permute-done.1.high_ref, ...), custom_call_target="tpu_custom_call" | custom-call | flops 78643200 | bytes 20971520 | tf_op jit(solution)/shard_map/stator_stencil/pallas_call | solution.py:380
  84.9 0.0 all-to-all-done.1
  84.9 0.0 copy-done.2
  84.9 0.0 copy-done.3
  84.9 3.9 %interface.1 = (f32[5,16,64,256]{3,2,1,0:T(8,128)}, f32[5,16,64,256]{3,2,1,0:T(8,128)}) custom-call(f32[3,5,5]{2,1,0:T(8,128)S(1)} %copy-done.2, f32[5,5]{1,0:T(8,128)S(1)} %copy-done.3, f32[8,2,5,2,8,256]{5,4,3,2,1,0:T(8,128)S(1)} %bitcast.8, f32[5,16,64,256]{3,2,1,0:T(8,128)} %stator_stencil.1.stator_ref, ...), custom_call_target="tpu_custom_call", output_to_operand_aliasing={{0}: (3, {}), {1}: (4, {})} | custom-call | flops 9830400 | bytes 3932160 | tf_op jit(solution)/shard_map/interface/pallas_call | solution.py:442
  (5 shorter events, 0.1 us)
Async XLA Ops:
  2.8 39.7 %all-to-all-start = ((f32[8,2,80,256]{3,2,1,0:T(8,128)}), f32[8,2,80,256]{3,2,1,0:T(8,128)S(1)}, u32[]{:S(2)}, u32[]{:S(2)}) async-start(f32[8,2,80,256]{3,2,1,0:T(8,128)} %bitcast.9), calls=%async_computation | async-start | bytes 2621440 | tf_op jit(solution)/shard_map/all_to_all | solution.py:471
  10.1 15.4 %copy-start.4 = (f32[5,2048]{1,0:T(8,128)S(1)}, f32[5,2048]{1,0:T(8,128)}, u32[]{:S(2)}) copy-start(f32[5,2048]{1,0:T(8,128)} %param.18) | copy-start | bytes 122884
  10.1 18.1 %copy-start.6 = (s32[16]{0:T(128)S(1)}, s32[16]{0:T(128)}, u32[]{:S(2)}) copy-start(s32[16]{0:T(128)} %constant.23) | copy-start | bytes 196
  10.1 32.4 %copy-start = (bf16[8,256,256]{2,1,0:T(8,128)(2,1)S(1)}, bf16[8,256,256]{2,1,0:T(8,128)(2,1)}, u32[]{:S(2)}) copy-start(bf16[8,256,256]{2,1,0:T(8,128)(2,1)} %constant.19.clone.low_ref) | copy-start | bytes 3145732
  10.1 32.4 %copy-start.1 = (bf16[8,256,256]{2,1,0:T(8,128)(2,1)S(1)}, bf16[8,256,256]{2,1,0:T(8,128)(2,1)}, u32[]{:S(2)}) copy-start(bf16[8,256,256]{2,1,0:T(8,128)(2,1)} %constant.18.clone.high_ref) | copy-start | bytes 3145732
  17.3 32.5 %copy-start.5 = (f32[3,5,5]{2,0,1:T(4,128)S(1)}, f32[3,5,5]{2,0,1:T(4,128)}, u32[]{:S(2)}) copy-start(f32[3,5,5]{2,0,1:T(4,128)} %param.16) | copy-start | bytes 904
  17.4 21.2 %collective-permute-start.2 = (f32[3,64,128]{2,1,0:T(8,128)}, f32[3,64,128]{2,1,0:T(8,128)}, u32[]{:S(2)}, u32[]{:S(2)}) collective-permute-start(f32[3,64,128]{2,1,0:T(8,128)} %get-tuple-element.19), channel_id=1, source_target_pairs={{0,4},{4,8},{8,12},{12,16},{16,20},{20,24},{24,28},{28,0},{1,5},{5... | collective-permute-start | bytes 294920 | tf_op jit(solution)/shard_map/ppermute | solution.py:475
  19.4 19.1 %collective-permute-start.3 = (f32[3,64,128]{2,1,0:T(8,128)}, f32[3,64,128]{2,1,0:T(8,128)}, u32[]{:S(2)}, u32[]{:S(2)}) collective-permute-start(f32[3,64,128]{2,1,0:T(8,128)} %get-tuple-element.20), channel_id=1, source_target_pairs={{4,0},{8,4},{12,8},{16,12},{20,16},{24,20},{28,24},{0,28},{5,1},{9... | collective-permute-start | bytes 294920 | tf_op jit(solution)/shard_map/ppermute | solution.py:476
  22.2 16.4 %collective-permute-start = (f32[2,16,5,2,256]{4,3,2,1,0:T(2,128)}, f32[2,16,5,2,256]{4,3,2,1,0:T(2,128)}, u32[]{:S(2)}, u32[]{:S(2)}) collective-permute-start(f32[2,16,5,2,256]{4,3,2,1,0:T(2,128)} %get-tuple-element.17), channel_id=1, source_target_pairs={{0,1},{1,2},{2,3},{4,5},{5,6},{6,7},{8,9},{9,10},{10,11},{12,13},{... | collective-permute-start | bytes 983048 | tf_op jit(solution)/shard_map/ppermute | solution.py:477
  24.2 14.4 %collective-permute-start.1 = (f32[2,16,5,2,256]{4,3,2,1,0:T(2,128)}, f32[2,16,5,2,256]{4,3,2,1,0:T(2,128)}, u32[]{:S(2)}, u32[]{:S(2)}) collective-permute-start(f32[2,16,5,2,256]{4,3,2,1,0:T(2,128)} %get-tuple-element.18), channel_id=1, source_target_pairs={{1,0},{2,1},{3,2},{5,4},{6,5},{7,6},{9,8},{10,9},{11,10},{13,12},{... | collective-permute-start | bytes 983048 | tf_op jit(solution)/shard_map/ppermute | solution.py:478
  45.9 39.0 %all-to-all-start.1 = ((f32[8,2,80,256]{3,2,1,0:T(8,128)}), f32[8,2,80,256]{3,2,1,0:T(8,128)S(1)}, u32[]{:S(2)}, u32[]{:S(2)}) async-start(f32[8,2,80,256]{3,2,1,0:T(8,128)} %modes.1), calls=%async_computation.1 | async-start | bytes 2621440 | tf_op jit(solution)/shard_map/all_to_all | solution.py:486
  67.7 17.2 %copy-start.2 = (f32[3,5,5]{2,1,0:T(8,128)S(1)}, f32[3,5,5]{2,1,0:T(8,128)}, u32[]{:S(2)}) copy-start(f32[3,5,5]{2,1,0:T(8,128)} %copy.26.jac_ref) | copy-start | bytes 904
  67.7 17.2 %copy-start.3 = (f32[5,5]{1,0:T(8,128)S(1)}, f32[5,5]{1,0:T(8,128)}, u32[]{:S(2)}) copy-start(f32[5,5]{1,0:T(8,128)} %mix_ref.5) | copy-start | bytes 304

commit v5 on v4

--- a/solution.py
+++ b/solution.py
@@ -269,11 +269,11 @@
 
 def stencil_kernel(
     side, layers, jac_ref, mix_ref, source, low_ref, high_ref, left_ref, right_ref, rows_ref, cols_ref,
-    out, state, radial, pitch, parts, sems,
+    out, state, radial, pitch, parts, mixer, slopes, sems,
 ):
     step = pl.program_id(0)
     fields, _, rows, cols = out.shape
-    chunk = 16
+    chunk, wide = 16, 2 * LANES
     scale = time_step * damping
     axial = (0.5 if side else -0.5) * time_step
     lane = lax.broadcasted_iota(jnp.int32, (rows, LANES), 1)
@@ -326,23 +326,51 @@
                         + pitch[slot, f * rows + at : f * rows + at + chunk, cols:]
                     )
                 )
+            place = at // chunk
             for g in range(fields):
-                slopes = (
-                    (state[g, here + 1, span, :] - state[g, here - 1, span, :]) * axial,
-                    radial[slot, g, span, :],
-                    pitch[slot, g * rows + at : g * rows + at + chunk, :cols],
+                for d, slope in enumerate(
+                    (
+                        state[g, here + 1, span, :] - state[g, here - 1, span, :],
+                        radial[slot, g, span, :],
+                        pitch[slot, g * rows + at : g * rows + at + chunk, :cols],
+                    )
+                ):
+                    first = (d * fields + g) * chunk
+                    high, low = halves(slope)
+                    slopes[slot, place, first : first + chunk, :] = high
+                    slopes[slot, place, wide + first : wide + first + chunk, :] = low
+            mixed = jnp.dot(
+                mixer[:, : 2 * wide], slopes[slot, place], preferred_element_type=jnp.float32
+            ) + jnp.dot(
+                mixer[:, 2 * wide :], slopes[slot, place, :wide, :], preferred_element_type=jnp.float32
+            )
+            for f in range(fields):
+                out[f, slot if side == 0 else 1 - slot, span, :] = (
+                    totals[f] + mixed[f * chunk : (f + 1) * chunk]
                 )
-                for d in range(3):
-                    for f in range(fields):
-                        totals[f] = totals[f] + jac_ref[d, f, g] * slopes[d]
-            for f in range(fields):
-                out[f, slot if side == 0 else 1 - slot, span, :] = totals[f]
 
     @pl.when(step == 0)
     def _():
         for layer in range(layers):
             load(layer).start()
         state[:, 0:2] = jnp.zeros((fields, 2, rows, cols), jnp.float32)
+        spot = lax.broadcasted_iota(jnp.int32, (chunk, wide), 1)
+        own = spot % chunk == lax.broadcasted_iota(jnp.int32, (chunk, wide), 0)
+        for f in range(fields):
+            entries = jnp.zeros((chunk, wide), jnp.float32)
+            for d in range(3):
+                for g in range(fields):
+                    entry = jnp.where(own & (spot // chunk == d * fields + g), jac_ref[d, f, g], 0.0)
+                    entries = entries + (entry * axial if d == 0 else entry)
+            high, low = halves(entries)
+            band = slice(f * chunk, (f + 1) * chunk)
+            mixer[band, :wide] = high
+            mixer[band, wide : 2 * wide] = high
+            mixer[band, 2 * wide :] = low
+        used = 3 * fields * chunk
+        blank = jnp.zeros((2, rows // chunk, wide - used, cols), jnp.bfloat16)
+        slopes[:, :, used:wide, :] = blank
+        slopes[:, :, wide + used :, :] = blank
         load(0).wait()
         load(1).wait()
 
@@ -390,6 +418,8 @@
             pltpu.VMEM((2, fields, 2 * rows, cols), jnp.float32),
             pltpu.VMEM((2, fields * rows, 2 * cols), jnp.float32),
             pltpu.VMEM((fields * rows, 2 * cols + 2 * LANES), jnp.bfloat16),
+            pltpu.VMEM((fields * 16, 6 * LANES), jnp.bfloat16),
+            pltpu.VMEM((2, rows // 16, 4 * LANES, cols), jnp.bfloat16),
             pltpu.SemaphoreType.DMA((layers,)),
         ],
         compiler_params=pltpu.CompilerParams(vmem_limit_bytes=WIDE),

time: 89.4 us -> 87.1 us (0.974)
  Pallas kernels: 51.1 us -> 48.9 us
    pallas_call x2, Pallas kernels: 34.4 us -> 32.2 us  [stencil(): pl.pallas_call(functools.partial(stencil_kernel, side, layers), grid=(ste...]
  transfers between devices with their start and end apart: 6 -> 6, of which waited for: 2 -> 2; matrix products, arithmetic and copies ran while one was open for 4% -> 4% of each run, Pallas kernels for 47% -> 45%
where the time goes in v5:
time: 87.1 us; the launch traced here: 86.7 us
  Pallas kernels  48.9 us (56%)
  starting transfers between devices  19.4 us (22%)
  waiting for transfers between devices  13.7 us (16%)
  local copies, waits for them, and re-layouts  3.28 us (4%)
  between operations  1.46 us (2%)
    pallas_call x2, Pallas kernels, stencil(): pl.pallas_call(functools.partial(stencil_kernel, side, layers), grid=(ste...  32.2 us
    ppermute x1, waiting for transfers between devices, shards(): from_left = lax.ppermute(right, 'pitch', ring)  9.7 us
    all_to_all x1, starting transfers between devices, shards(): received = lax.all_to_all(planes, 'pitch', 0, 0, tiled=True)  7.25 us
    pallas_call x1, Pallas kernels, pack_edges(): pl.pallas_call(pack_kernel, grid=(steps,), out_shape=(edge, edge, side, s...  7.22 us
    all_to_all x1, starting transfers between devices, shards(): modes = lax.all_to_all(sent, 'pitch', 0, 0, tiled=True)  3.98 us
    all_to_all x1, waiting for transfers between devices, shards(): received = lax.all_to_all(planes, 'pitch', 0, 0, tiled=True)  3.95 us
    pallas_call x1, Pallas kernels, close(): pl.pallas_call(close_kernel, grid=(count // group,), out_shape=(shape, sh...  3.94 us
    pallas_call x1, Pallas kernels, transform(): pl.pallas_call(functools.partial(transform_kernel, fields), out_shape=jax...  3.38 us
  transfers between devices with their start and end apart: 6, of which 2 were waited for; matrix products, arithmetic and copies ran while one was open for 4% of the time, Pallas kernels for 45%

profile of v5, /device:TPU:0, one launch (start us, length us, event | category | flops | bytes accessed | tf_op | source)
XLA Modules:
  0.0 86.7 jit_solution(11146818338177639892)
XLA Ops:
  0.6 2.2 %planes.1 = f32[8,2,5,2,8,256]{5,4,3,2,1,0:T(8,128)} custom-call(f32[5,16,64,256]{3,2,1,0:T(8,128)} %source.2, f32[5,16,64,256]{3,2,1,0:T(8,128)} %source.3), custom_call_target="tpu_custom_call" | custom-call | tf_op jit(solution)/shard_map/planes/pallas_call | solution.py:173
  2.8 7.3 %all-to-all-start = ((f32[8,2,80,256]{3,2,1,0:T(8,128)}), f32[8,2,80,256]{3,2,1,0:T(8,128)S(1)}, u32[]{:S(2)}, u32[]{:S(2)}) async-start(f32[8,2,80,256]{3,2,1,0:T(8,128)} %bitcast.9), calls=%async_computation | async-start | bytes 2621440 | tf_op jit(solution)/shard_map/all_to_all | solution.py:501
  10.1 0.0 copy-start.4
  10.1 0.0 copy-start.6
  10.1 0.0 copy-start
  10.1 0.0 copy-start.1
  10.1 7.2 %edges.1 = (f32[2,16,5,2,256]{4,3,2,1,0:T(2,128)}, f32[2,16,5,2,256]{4,3,2,1,0:T(2,128)}, f32[3,64,128]{2,1,0:T(8,128)}, f32[3,64,128]{2,1,0:T(8,128)}) custom-call(f32[5,16,64,256]{3,2,1,0:T(8,128)} %source.2, f32[5,16,64,256]{3,2,1,0:T(8,128)} %source.3), custom_call_target="tpu_custom_call" | custom-call | bytes 10485760 | tf_op jit(solution)/shard_map/edges/pallas_call | solution.py:223
  17.3 0.0 copy-start.5
  17.4 2.1 %collective-permute-start.2 = (f32[3,64,128]{2,1,0:T(8,128)}, f32[3,64,128]{2,1,0:T(8,128)}, u32[]{:S(2)}, u32[]{:S(2)}) collective-permute-start(f32[3,64,128]{2,1,0:T(8,128)} %get-tuple-element.19), channel_id=1, source_target_pairs={{0,4},{4,8},{8,12},{12,16},{16,20},{20,24},{24,28},{28,0},{1,5},{5... | collective-permute-start | bytes 294920 | tf_op jit(solution)/shard_map/ppermute | solution.py:505
  19.4 2.8 %collective-permute-start.3 = (f32[3,64,128]{2,1,0:T(8,128)}, f32[3,64,128]{2,1,0:T(8,128)}, u32[]{:S(2)}, u32[]{:S(2)}) collective-permute-start(f32[3,64,128]{2,1,0:T(8,128)} %get-tuple-element.20), channel_id=1, source_target_pairs={{4,0},{8,4},{12,8},{16,12},{20,16},{24,20},{28,24},{0,28},{5,1},{9... | collective-permute-start | bytes 294920 | tf_op jit(solution)/shard_map/ppermute | solution.py:506
  22.2 2.0 %collective-permute-start = (f32[2,16,5,2,256]{4,3,2,1,0:T(2,128)}, f32[2,16,5,2,256]{4,3,2,1,0:T(2,128)}, u32[]{:S(2)}, u32[]{:S(2)}) collective-permute-start(f32[2,16,5,2,256]{4,3,2,1,0:T(2,128)} %get-tuple-element.17), channel_id=1, source_target_pairs={{0,1},{1,2},{2,3},{4,5},{5,6},{6,7},{8,9},{9,10},{10,11},{12,13},{... | collective-permute-start | bytes 983048 | tf_op jit(solution)/shard_map/ppermute | solution.py:507
  24.2 1.3 %collective-permute-start.1 = (f32[2,16,5,2,256]{4,3,2,1,0:T(2,128)}, f32[2,16,5,2,256]{4,3,2,1,0:T(2,128)}, u32[]{:S(2)}, u32[]{:S(2)}) collective-permute-start(f32[2,16,5,2,256]{4,3,2,1,0:T(2,128)} %get-tuple-element.18), channel_id=1, source_target_pairs={{1,0},{2,1},{3,2},{5,4},{6,5},{7,6},{9,8},{10,9},{11,10},{13,12},{... | collective-permute-start | bytes 983048 | tf_op jit(solution)/shard_map/ppermute | solution.py:508
  25.5 0.0 copy-done.4
  26.2 0.9 %mul.11 = f32[5,128,16]{2,1,0:T(8,128)} reshape(f32[5,2048]{1,0:T(8,128)S(1)} %broadcast_multiply_fusion) | data formatting | bytes 81920 | tf_op jit(solution)/shard_map/mul | solution.py:511
  27.0 1.1 %copy.21 = f32[5,128,16]{1,0,2:T(8,128)S(1)} copy(f32[5,128,16]{2,1,0:T(8,128)} %mul.11) | data formatting | bytes 81920 | tf_op jit(solution)/shard_map/mul | solution.py:511
  28.2 0.0 copy-done.6
  28.2 0.6 gather_fusion
  28.9 9.7 %collective-permute-done.2.left_ref = f32[3,64,128]{2,1,0:T(8,128)} collective-permute-done((f32[3,64,128]{2,1,0:T(8,128)}, f32[3,64,128]{2,1,0:T(8,128)}, u32[]{:S(2)}, u32[]{:S(2)}) %collective-permute-start.2) | collective-permute-done | bytes 98336 | tf_op jit(solution)/shard_map/ppermute | solution.py:505
  38.6 0.0 collective-permute-done.3.right_ref
  38.6 0.0 collective-permute-done.low_ref
  38.6 0.0 collective-permute-done.1.high_ref
  38.6 3.9 %all-to-all-done.got_ref = f32[8,2,80,256]{3,2,1,0:T(8,128)S(1)} async-done(((f32[8,2,80,256]{3,2,1,0:T(8,128)}), f32[8,2,80,256]{3,2,1,0:T(8,128)S(1)}, u32[]{:S(2)}, u32[]{:S(2)}) %all-to-all-start) | async-done | bytes 1310752 | tf_op jit(solution)/shard_map/all_to_all | solution.py:501
  42.5 0.0 copy-done
  42.5 0.0 copy-done.1
  42.5 3.4 %modes.1 = f32[8,2,80,256]{3,2,1,0:T(8,128)} custom-call(s32[1]{0:T(128)S(6)} %copy.29.offset_ref, f32[8,2,80,256]{3,2,1,0:T(8,128)S(1)} %all-to-all-done.got_ref, f32[8,5,256]{2,1,0:T(8,128)S(1)} %copy.23.blend_ref, bf16[8,256,256]{2,1,0:T(8,128)(2,1)S(1)} %copy-done.1, bf16[8,256,256]{2,1,0:T(8,128)(2,1)S(1)} %copy-done), custom_call_target="tpu_custom_call" | custom-call | flops 503316480 | bytes 5000000 | tf_op jit(solution)/shard_map/modes/pallas_call | solution.py:142
  45.9 4.0 %all-to-all-start.1 = ((f32[8,2,80,256]{3,2,1,0:T(8,128)}), f32[8,2,80,256]{3,2,1,0:T(8,128)S(1)}, u32[]{:S(2)}, u32[]{:S(2)}) async-start(f32[8,2,80,256]{3,2,1,0:T(8,128)} %modes.1), calls=%async_computation.1 | async-start | bytes 2621440 | tf_op jit(solution)/shard_map/all_to_all | solution.py:516
  49.9 0.0 copy-done.5
  49.9 0.6 copy.26.jac_ref
  50.5 16.1 %rotor_stencil.1.rotor_ref = f32[5,16,64,256]{3,2,1,0:T(8,128)} custom-call(f32[3,5,5]{2,1,0:T(8,128)} %copy.26.jac_ref, f32[5,5]{1,0:T(8,128)} %mix_ref.5, f32[5,16,64,256]{3,2,1,0:T(8,128)} %source.3, f32[2,16,5,2,256]{4,3,2,1,0:T(2,128)} %collective-permute-done.low_ref, f32[2,16,5,2,256]{4,3,2,1,0:T(2,128)} %collective-permute-done.1.high_ref, ...), custom_call_target="tpu_custom_call" | custom-call | flops 78643200 | bytes 20971520 | tf_op jit(solution)/shard_map/rotor_stencil/pallas_call | solution.py:408
  66.5 0.0 copy-start.2
  66.6 0.0 copy-start.3
  66.6 16.1 %stator_stencil.1.stator_ref = f32[5,16,64,256]{3,2,1,0:T(8,128)} custom-call(f32[3,5,5]{2,1,0:T(8,128)} %copy.26.jac_ref, f32[5,5]{1,0:T(8,128)} %mix_ref.5, f32[5,16,64,256]{3,2,1,0:T(8,128)} %source.2, f32[2,16,5,2,256]{4,3,2,1,0:T(2,128)} %collective-permute-done.low_ref, f32[2,16,5,2,256]{4,3,2,1,0:T(2,128)} %collective-permute-done.1.high_ref, ...), custom_call_target="tpu_custom_call" | custom-call | flops 78643200 | bytes 20971520 | tf_op jit(solution)/shard_map/stator_stencil/pallas_call | solution.py:408
  82.7 0.0 all-to-all-done.1
  82.7 0.0 copy-done.2
  82.7 0.0 copy-done.3
  82.7 3.9 %interface.1 = (f32[5,16,64,256]{3,2,1,0:T(8,128)}, f32[5,16,64,256]{3,2,1,0:T(8,128)}) custom-call(f32[3,5,5]{2,1,0:T(8,128)S(1)} %copy-done.2, f32[5,5]{1,0:T(8,128)S(1)} %copy-done.3, f32[8,2,5,2,8,256]{5,4,3,2,1,0:T(8,128)S(1)} %bitcast.8, f32[5,16,64,256]{3,2,1,0:T(8,128)} %stator_stencil.1.stator_ref, ...), custom_call_target="tpu_custom_call", output_to_operand_aliasing={{0}: (3, {}), {1}: (4, {})} | custom-call | flops 9830400 | bytes 3932160 | tf_op jit(solution)/shard_map/interface/pallas_call | solution.py:472
  (5 shorter events, 0.1 us)
Async XLA Ops:
  2.8 39.7 %all-to-all-start = ((f32[8,2,80,256]{3,2,1,0:T(8,128)}), f32[8,2,80,256]{3,2,1,0:T(8,128)S(1)}, u32[]{:S(2)}, u32[]{:S(2)}) async-start(f32[8,2,80,256]{3,2,1,0:T(8,128)} %bitcast.9), calls=%async_computation | async-start | bytes 2621440 | tf_op jit(solution)/shard_map/all_to_all | solution.py:501
  10.1 15.4 %copy-start.4 = (f32[5,2048]{1,0:T(8,128)S(1)}, f32[5,2048]{1,0:T(8,128)}, u32[]{:S(2)}) copy-start(f32[5,2048]{1,0:T(8,128)} %param.18) | copy-start | bytes 122884
  10.1 18.1 %copy-start.6 = (s32[16]{0:T(128)S(1)}, s32[16]{0:T(128)}, u32[]{:S(2)}) copy-start(s32[16]{0:T(128)} %constant.23) | copy-start | bytes 196
  10.1 32.4 %copy-start = (bf16[8,256,256]{2,1,0:T(8,128)(2,1)S(1)}, bf16[8,256,256]{2,1,0:T(8,128)(2,1)}, u32[]{:S(2)}) copy-start(bf16[8,256,256]{2,1,0:T(8,128)(2,1)} %constant.19.clone.low_ref) | copy-start | bytes 3145732
  10.1 32.4 %copy-start.1 = (bf16[8,256,256]{2,1,0:T(8,128)(2,1)S(1)}, bf16[8,256,256]{2,1,0:T(8,128)(2,1)}, u32[]{:S(2)}) copy-start(bf16[8,256,256]{2,1,0:T(8,128)(2,1)} %constant.18.clone.high_ref) | copy-start | bytes 3145732
  17.3 32.5 %copy-start.5 = (f32[3,5,5]{2,0,1:T(4,128)S(1)}, f32[3,5,5]{2,0,1:T(4,128)}, u32[]{:S(2)}) copy-start(f32[3,5,5]{2,0,1:T(4,128)} %param.16) | copy-start | bytes 904
  17.4 21.2 %collective-permute-start.2 = (f32[3,64,128]{2,1,0:T(8,128)}, f32[3,64,128]{2,1,0:T(8,128)}, u32[]{:S(2)}, u32[]{:S(2)}) collective-permute-start(f32[3,64,128]{2,1,0:T(8,128)} %get-tuple-element.19), channel_id=1, source_target_pairs={{0,4},{4,8},{8,12},{12,16},{16,20},{20,24},{24,28},{28,0},{1,5},{5... | collective-permute-start | bytes 294920 | tf_op jit(solution)/shard_map/ppermute | solution.py:505
  19.4 19.1 %collective-permute-start.3 = (f32[3,64,128]{2,1,0:T(8,128)}, f32[3,64,128]{2,1,0:T(8,128)}, u32[]{:S(2)}, u32[]{:S(2)}) collective-permute-start(f32[3,64,128]{2,1,0:T(8,128)} %get-tuple-element.20), channel_id=1, source_target_pairs={{4,0},{8,4},{12,8},{16,12},{20,16},{24,20},{28,24},{0,28},{5,1},{9... | collective-permute-start | bytes 294920 | tf_op jit(solution)/shard_map/ppermute | solution.py:506
  22.2 16.4 %collective-permute-start = (f32[2,16,5,2,256]{4,3,2,1,0:T(2,128)}, f32[2,16,5,2,256]{4,3,2,1,0:T(2,128)}, u32[]{:S(2)}, u32[]{:S(2)}) collective-permute-start(f32[2,16,5,2,256]{4,3,2,1,0:T(2,128)} %get-tuple-element.17), channel_id=1, source_target_pairs={{0,1},{1,2},{2,3},{4,5},{5,6},{6,7},{8,9},{9,10},{10,11},{12,13},{... | collective-permute-start | bytes 983048 | tf_op jit(solution)/shard_map/ppermute | solution.py:507
  24.2 14.4 %collective-permute-start.1 = (f32[2,16,5,2,256]{4,3,2,1,0:T(2,128)}, f32[2,16,5,2,256]{4,3,2,1,0:T(2,128)}, u32[]{:S(2)}, u32[]{:S(2)}) collective-permute-start(f32[2,16,5,2,256]{4,3,2,1,0:T(2,128)} %get-tuple-element.18), channel_id=1, source_target_pairs={{1,0},{2,1},{3,2},{5,4},{6,5},{7,6},{9,8},{10,9},{11,10},{13,12},{... | collective-permute-start | bytes 983048 | tf_op jit(solution)/shard_map/ppermute | solution.py:508
  45.9 36.8 %all-to-all-start.1 = ((f32[8,2,80,256]{3,2,1,0:T(8,128)}), f32[8,2,80,256]{3,2,1,0:T(8,128)S(1)}, u32[]{:S(2)}, u32[]{:S(2)}) async-start(f32[8,2,80,256]{3,2,1,0:T(8,128)} %modes.1), calls=%async_computation.1 | async-start | bytes 2621440 | tf_op jit(solution)/shard_map/all_to_all | solution.py:516
  66.5 16.2 %copy-start.2 = (f32[3,5,5]{2,1,0:T(8,128)S(1)}, f32[3,5,5]{2,1,0:T(8,128)}, u32[]{:S(2)}) copy-start(f32[3,5,5]{2,1,0:T(8,128)} %copy.26.jac_ref) | copy-start | bytes 904
  66.6 16.2 %copy-start.3 = (f32[5,5]{1,0:T(8,128)S(1)}, f32[5,5]{1,0:T(8,128)}, u32[]{:S(2)}) copy-start(f32[5,5]{1,0:T(8,128)} %mix_ref.5) | copy-start | bytes 304

commit v6 on v5

--- a/solution.py
+++ b/solution.py
@@ -106,11 +106,12 @@
             work[m, span, :LANES] = modes[pairs[m, 0]]
             work[m, span, LANES:] = modes[pairs[m, 1]]
     for m in range(PAIRS):
-        got = split_dot(work[m], high_ref[m], low_ref[m], ((1,), (0,)))
+        got = split_dot(work[m], high_ref[m], low_ref[m], ((1,), (0,))) * (1.0 / NP)
         per_field = rows // fields
         got = jnp.concatenate(
             [
-                got[f * per_field : (f + 1) * per_field] * blend_ref[m, f : f + 1, :]
+                got[f * per_field : (f + 1) * per_field]
+                * jnp.concatenate([blend_ref[k, f : f + 1, :] for k in pairs[m]], axis=1)
                 for f in range(fields)
             ],
             axis=0,
@@ -156,13 +157,13 @@
     )(offset, received, blend, jnp.asarray(high), jnp.asarray(low))
 
 
-def planes_kernel(stator, rotor, out):
-    count, _, _, _, step, _ = out.shape
+def planes_kernel(stator, rotor, *outs):
+    count, _, _, step, _ = outs[0].shape
     for q in range(count):
         span = slice(q * step, (q + 1) * step)
-        for ghost in range(2):
-            out[q, 0, :, ghost] = stator[:, 1 - ghost, span, :]
-            out[q, 1, :, ghost] = rotor[:, ghost, span, :]
+        for ghost, out in enumerate(outs):
+            out[q, 0] = stator[:, 1 - ghost, span, :]
+            out[q, 1] = rotor[:, ghost, span, :]
 
 
 def interface_planes(stator, rotor, count):
@@ -173,12 +174,12 @@
     return pl.pallas_call(
         planes_kernel,
         grid=(count // group,),
-        out_shape=jax.ShapeDtypeStruct((count, 2, fields, 2, step, cols), jnp.float32),
+        out_shape=(jax.ShapeDtypeStruct((count, 2, fields, step, cols), jnp.float32),) * 2,
         in_specs=[
             pl.BlockSpec(block, lambda q: (0, layers // 2 - 1, q, 0)),
             pl.BlockSpec(block, lambda q: (0, 0, q, 0)),
         ],
-        out_specs=pl.BlockSpec((group, 2, fields, 2, step, cols), lambda q: (q, 0, 0, 0, 0, 0)),
+        out_specs=(pl.BlockSpec((group, 2, fields, step, cols), lambda q: (q, 0, 0, 0, 0)),) * 2,
         compiler_params=pltpu.CompilerParams(vmem_limit_bytes=WIDE),
         name="planes",
     )(stator, rotor)
@@ -430,10 +431,9 @@
     )(weights, mix, state, low, high, left, right, jnp.asarray(along_rows), jnp.asarray(along_cols))
 
 
-def close_kernel(jac_ref, mix_ref, modes_ref, stator_ref, rotor_ref, stator_out, rotor_out):
+def close_kernel(jac_ref, mix_ref, first_ref, second_ref, stator_ref, rotor_ref, stator_out, rotor_out):
     fields = stator_ref.shape[0]
-    count = modes_ref.shape[0]
-    step = modes_ref.shape[4]
+    count, _, _, step, _ = first_ref.shape
     scale = time_step * damping
 
     def combine(row, sources):
@@ -448,8 +448,8 @@
         for q in range(count):
             span = slice(q * step, (q + 1) * step)
             ghosts = []
-            for ghost in range(2):
-                planes = [modes_ref[q, side, g, ghost] for g in range(fields)]
+            for modes_ref in (first_ref, second_ref):
+                planes = [modes_ref[q, side, g] for g in range(fields)]
                 ghosts.append([combine(lambda g: mix_ref[f, g], planes) for f in range(fields)])
             first, second = ghosts
             for f in range(fields):
@@ -459,9 +459,9 @@
                 out[f, far, span, :] = ref[f, far, span, :] - first[f] * (sign * scale)
 
 
-def close(modes, stator, rotor, jacobians, field_mix):
+def close(first, second, stator, rotor, jacobians, field_mix):
     fields, layers, rows, cols = stator.shape
-    count, _, _, _, step, _ = modes.shape
+    count = first.shape[0]
     group = max(1, count // 4)
     block = (fields, 2, rows // count * group, cols)
     specs = (
@@ -476,17 +476,18 @@
         in_specs=[
             pl.BlockSpec(memory_space=pltpu.SMEM),
             pl.BlockSpec(memory_space=pltpu.SMEM),
-            pl.BlockSpec((group,) + modes.shape[1:], lambda q: (q, 0, 0, 0, 0, 0)),
+            pl.BlockSpec((group,) + first.shape[1:], lambda q: (q, 0, 0, 0, 0)),
+            pl.BlockSpec((group,) + first.shape[1:], lambda q: (q, 0, 0, 0, 0)),
             *specs,
         ],
         out_specs=specs,
-        input_output_aliases={3: 0, 4: 1},
+        input_output_aliases={4: 0, 5: 1},
         compiler_params=pltpu.CompilerParams(vmem_limit_bytes=NARROW),
         cost_estimate=pl.CostEstimate(
-            flops=30 * modes.size, bytes_accessed=12 * modes.size, transcendentals=0
+            flops=60 * first.size, bytes_accessed=24 * first.size, transcendentals=0
         ),
         name="interface",
-    )(jacobians, field_mix, modes, stator, rotor)
+    )(jacobians, field_mix, first, second, stator, rotor)
 
 
 def shards(stator, rotor, jacobians, field_mix, mode_blend, rotor_offset):
@@ -495,10 +496,14 @@
     spans = lax.axis_size("span")
     step = rows // count
 
-    planes = interface_planes(stator, rotor, count).reshape(count, 2, fields * 2 * step, cols)
-
-    planes, *states = lax.optimization_barrier((planes, stator, rotor))
-    received = lax.all_to_all(planes, "pitch", 0, 0, tiled=True)
+    def exchange(block):
+        return lax.all_to_all(block.reshape(count, 2, fields * step, cols), "pitch", 0, 0, tiled=True)
+
+    blend = jnp.moveaxis(mode_blend.reshape(fields, LANES, OUTER), 2, 0)
+
+    nearest, second = interface_planes(stator, rotor, count)
+    nearest, *states = lax.optimization_barrier((nearest, stator, rotor))
+    got = exchange(nearest)
     low, high, left, right = pack_edges(*states)
     ring = [(i, (i + 1) % count) for i in range(count)]
     line = [(i, i + 1) for i in range(spans - 1)]
@@ -506,18 +511,22 @@
     from_right = lax.ppermute(left, "pitch", [(b, a) for a, b in ring])
     from_below = lax.ppermute(high, "span", line)
     from_above = lax.ppermute(low, "span", [(b, a) for a, b in line])
-
+    got, second, from_left, from_right = lax.optimization_barrier((got, second, from_left, from_right))
+    got_second = exchange(second)
+    sent = transform(got, rotor_offset, blend, fields)
+    sent, from_left, from_right = lax.optimization_barrier((sent, from_left, from_right))
     edges = (from_below, from_above, from_left, from_right)
-    blend = mode_blend.reshape(fields, LANES, OUTER) * (1.0 / NP)
-    blend = jnp.moveaxis(blend, 2, 0)[outer_order().reshape(-1)]
-    blend = blend.reshape(PAIRS, 2, fields, LANES).transpose(0, 2, 1, 3).reshape(PAIRS, fields, 2 * LANES)
-    received, edges = lax.optimization_barrier((received, edges))
-    sent = transform(received, rotor_offset, blend, fields)
-    modes = lax.all_to_all(sent, "pitch", 0, 0, tiled=True)
-    modes = modes.reshape(count, 2, fields, 2, step, cols)
+    modes = exchange(sent)
     stator_mid = stencil(0, stator, *edges, jacobians, field_mix)
+    got_second, stator_mid = lax.optimization_barrier((got_second, stator_mid))
+    sent_second = transform(got_second, rotor_offset, blend, fields)
+    sent_second, rotor = lax.optimization_barrier((sent_second, rotor))
+    modes_second = exchange(sent_second)
     rotor_mid = stencil(1, rotor, *edges, jacobians, field_mix)
-    return close(modes, stator_mid, rotor_mid, jacobians, field_mix)
+    layout = (count, 2, fields, step, cols)
+    return close(
+        modes.reshape(layout), modes_second.reshape(layout), stator_mid, rotor_mid, jacobians, field_mix
+    )
 
 
 def solution(mesh):

time: 87.1 us -> 112 us (1.29)
  the two profiles are of different devices: /device:TPU:0 before, /device:TPU:1 now
where the time goes in v6:
time: 112 us; the launch traced here: 111 us
  Pallas kernels  49.6 us (44%)
  starting transfers between devices  32.6 us (29%)
  waiting for transfers between devices  22.1 us (20%)
  local copies, waits for them, and re-layouts  5.7 us (5%)
  between operations  1.45 us (1%)
    pallas_call x2, Pallas kernels, stencil(): pl.pallas_call(functools.partial(stencil_kernel, side, layers), grid=(ste...  32.1 us
    all_to_all x4, starting transfers between devices, exchange(): lax.all_to_all(block.reshape(count, 2, fields * step, cols), 'pitch', 0,...  22.6 us
    all_to_all x4, waiting for transfers between devices, exchange(): lax.all_to_all(block.reshape(count, 2, fields * step, cols), 'pitch', 0,...  10.7 us
    pallas_call x1, Pallas kernels, pack_edges(): pl.pallas_call(pack_kernel, grid=(steps,), out_shape=(edge, edge, side, s...  7.24 us
    ppermute x1, waiting for transfers between devices, shards(): from_left = lax.ppermute(right, 'pitch', ring)  5.03 us
    ppermute x1, waiting for transfers between devices, shards(): from_above = lax.ppermute(low, 'span', [(b, a) for a, b in line])  4.58 us
    pallas_call x2, Pallas kernels, transform(): pl.pallas_call(functools.partial(transform_kernel, fields), out_shape=jax...  4.05 us
    pallas_call x1, Pallas kernels, close(): pl.pallas_call(close_kernel, grid=(count // group,), out_shape=(shape, sh...  3.94 us
  transfers between devices with their start and end apart: 8, of which 4 were waited for; matrix products, arithmetic and copies ran while one was open for 2% of the time, Pallas kernels for 39%

profile of v6, /device:TPU:1, one launch (start us, length us, event | category | flops | bytes accessed | tf_op | source)
XLA Modules:
  0.0 111.5 jit_solution(2147156507406933708)
XLA Ops:
  0.6 2.2 %planes.1 = (f32[8,2,5,8,256]{4,3,2,1,0:T(8,128)}, f32[8,2,5,8,256]{4,3,2,1,0:T(8,128)}) custom-call(f32[5,16,64,256]{3,2,1,0:T(8,128)} %source.1, f32[5,16,64,256]{3,2,1,0:T(8,128)} %source.2), custom_call_target="tpu_custom_call" | custom-call | tf_op jit(solution)/shard_map/planes/pallas_call | solution.py:174
  2.8 6.4 %all-to-all-start = ((f32[8,2,40,256]{3,2,1,0:T(8,128)}), f32[8,2,40,256]{3,2,1,0:T(8,128)S(1)}, u32[]{:S(2)}, u32[]{:S(2)}) async-start(f32[8,2,40,256]{3,2,1,0:T(8,128)} %bitcast.10), calls=%async_computation | async-start | bytes 1310720 | tf_op jit(solution)/shard_map/all_to_all | solution.py:500
  9.2 0.0 copy-start.9
  9.2 0.0 copy-start
  9.2 0.0 copy-start.1
  9.2 7.2 %edges.1 = (f32[2,16,5,2,256]{4,3,2,1,0:T(2,128)}, f32[2,16,5,2,256]{4,3,2,1,0:T(2,128)}, f32[3,64,128]{2,1,0:T(8,128)}, f32[3,64,128]{2,1,0:T(8,128)}) custom-call(f32[5,16,64,256]{3,2,1,0:T(8,128)} %source.1, f32[5,16,64,256]{3,2,1,0:T(8,128)} %source.2), custom_call_target="tpu_custom_call" | custom-call | bytes 10485760 | tf_op jit(solution)/shard_map/edges/pallas_call | solution.py:224
  16.4 0.0 copy-start.10
  16.5 1.5 %collective-permute-start = (f32[3,64,128]{2,1,0:T(8,128)}, f32[3,64,128]{2,1,0:T(8,128)S(1)}, u32[]{:S(2)}, u32[]{:S(2)}) collective-permute-start(f32[3,64,128]{2,1,0:T(8,128)} %get-tuple-element.27), channel_id=1, source_target_pairs={{0,4},{4,8},{8,12},{12,16},{16,20},{20,24},{24,28},{28,0},{1,5},{5... | collective-permute-start | bytes 294920 | tf_op jit(solution)/shard_map/ppermute | solution.py:510
  18.0 2.8 %collective-permute-start.1 = (f32[3,64,128]{2,1,0:T(8,128)}, f32[3,64,128]{2,1,0:T(8,128)}, u32[]{:S(2)}, u32[]{:S(2)}) collective-permute-start(f32[3,64,128]{2,1,0:T(8,128)} %get-tuple-element.28), channel_id=1, source_target_pairs={{4,0},{8,4},{12,8},{16,12},{20,16},{24,20},{28,24},{0,28},{5,1},{9... | collective-permute-start | bytes 294920 | tf_op jit(solution)/shard_map/ppermute | solution.py:511
  20.7 5.0 %collective-permute-done.left_ref = f32[3,64,128]{2,1,0:T(8,128)S(1)} collective-permute-done((f32[3,64,128]{2,1,0:T(8,128)}, f32[3,64,128]{2,1,0:T(8,128)S(1)}, u32[]{:S(2)}, u32[]{:S(2)}) %collective-permute-start) | collective-permute-done | bytes 98336 | tf_op jit(solution)/shard_map/ppermute | solution.py:510
  25.8 0.0 copy-start.8
  25.8 0.6 copy-done.8
  26.4 0.0 collective-permute-done.1.right_ref
  26.4 0.0 all-to-all-done.got_ref
  26.4 5.7 %all-to-all-start.2 = ((f32[8,2,40,256]{3,2,1,0:T(8,128)}), f32[8,2,40,256]{3,2,1,0:T(8,128)S(1)}, u32[]{:S(2)}, u32[]{:S(2)}) async-start(f32[8,2,40,256]{3,2,1,0:T(8,128)} %bitcast.9), calls=%async_computation.2 | async-start | bytes 1310720 | tf_op jit(solution)/shard_map/all_to_all | solution.py:500
  32.8 0.0 copy-done.9
  32.8 0.9 reshape.20
  33.7 1.1 %copy.21 = f32[5,128,16]{1,0,2:T(8,128)S(1)} copy(f32[5,128,16]{2,1,0:T(8,128)} %reshape.20) | data formatting | bytes 81920 | tf_op jit(solution)/shard_map/reshape | solution.py:502
  34.8 0.0 copy-done
  34.8 0.0 copy-done.1
  34.8 2.0 %modes.2 = f32[8,2,40,256]{3,2,1,0:T(8,128)S(1)} custom-call(s32[1]{0:T(128)S(6)} %copy.27.offset_ref, f32[8,2,40,256]{3,2,1,0:T(8,128)S(1)} %all-to-all-done.got_ref, f32[16,5,128]{2,1,0:T(8,128)S(1)} %bitcast.7, bf16[8,256,256]{2,1,0:T(8,128)(2,1)S(1)} %copy-done.1, bf16[8,256,256]{2,1,0:T(8,128)(2,1)S(1)} %copy-done), custom_call_target="tpu_custom_call" | custom-call | flops 251658240 | bytes 5000000 | tf_op jit(solution)/shard_map/modes/pallas_call | solution.py:143
  36.9 0.0 copy-start.2
  36.9 0.8 copy-done.2
  37.7 10.7 %all-to-all-done.2.got_ref = f32[8,2,40,256]{3,2,1,0:T(8,128)S(1)} async-done(((f32[8,2,40,256]{3,2,1,0:T(8,128)}), f32[8,2,40,256]{3,2,1,0:T(8,128)S(1)}, u32[]{:S(2)}, u32[]{:S(2)}) %all-to-all-start.2) | async-done | bytes 655392 | tf_op jit(solution)/shard_map/all_to_all | solution.py:500
  48.4 4.8 %all-to-all-start.1 = ((f32[8,2,40,256]{3,2,1,0:T(8,128)}), f32[8,2,40,256]{3,2,1,0:T(8,128)S(1)}, u32[]{:S(2)}, u32[]{:S(2)}) async-start(f32[8,2,40,256]{3,2,1,0:T(8,128)} %copy-done.2), calls=%async_computation.1 | async-start | bytes 1310720 | tf_op jit(solution)/shard_map/all_to_all | solution.py:500
  53.2 3.8 %collective-permute-start.2 = (f32[2,16,5,2,256]{4,3,2,1,0:T(2,128)}, f32[2,16,5,2,256]{4,3,2,1,0:T(2,128)S(1)}, u32[]{:S(2)}, u32[]{:S(2)}) collective-permute-start(f32[2,16,5,2,256]{4,3,2,1,0:T(2,128)} %get-tuple-element.34), channel_id=1, source_target_pairs={{0,1},{1,2},{2,3},{4,5},{5,6},{6,7},{8,9},{9,10},{10,11},{12,13},{... | collective-permute-start | bytes 983048 | tf_op jit(solution)/shard_map/ppermute | solution.py:512
  57.1 1.9 %collective-permute-start.3 = (f32[2,16,5,2,256]{4,3,2,1,0:T(2,128)}, f32[2,16,5,2,256]{4,3,2,1,0:T(2,128)S(1)}, u32[]{:S(2)}, u32[]{:S(2)}) collective-permute-start(f32[2,16,5,2,256]{4,3,2,1,0:T(2,128)} %get-tuple-element.35), channel_id=1, source_target_pairs={{1,0},{2,1},{3,2},{5,4},{6,5},{7,6},{9,8},{10,9},{11,10},{13,12},{... | collective-permute-start | bytes 983048 | tf_op jit(solution)/shard_map/ppermute | solution.py:513
  59.0 0.0 copy-done.10
  59.0 0.6 copy.24.jac_ref
  59.6 1.8 %collective-permute-done.2.low_ref = f32[2,16,5,2,256]{4,3,2,1,0:T(2,128)S(1)} collective-permute-done((f32[2,16,5,2,256]{4,3,2,1,0:T(2,128)}, f32[2,16,5,2,256]{4,3,2,1,0:T(2,128)S(1)}, u32[]{:S(2)}, u32[]{:S(2)}) %collective-permute-start.2) | collective-permute-done | bytes 327712 | tf_op jit(solution)/shard_map/ppermute | solution.py:512
  61.4 0.0 copy-start.6
  61.4 4.6 %collective-permute-done.3.high_ref = f32[2,16,5,2,256]{4,3,2,1,0:T(2,128)S(1)} collective-permute-done((f32[2,16,5,2,256]{4,3,2,1,0:T(2,128)}, f32[2,16,5,2,256]{4,3,2,1,0:T(2,128)S(1)}, u32[]{:S(2)}, u32[]{:S(2)}) %collective-permute-start.3) | collective-permute-done | bytes 327712 | tf_op jit(solution)/shard_map/ppermute | solution.py:513
  66.0 0.0 copy-done.6
  66.0 0.0 copy-start.7
  66.0 0.7 copy-done.7
  66.7 16.1 %stator_stencil.1.stator_ref = f32[5,16,64,256]{3,2,1,0:T(8,128)} custom-call(f32[3,5,5]{2,1,0:T(8,128)} %copy.24.jac_ref, f32[5,5]{1,0:T(8,128)} %mix_ref.5, f32[5,16,64,256]{3,2,1,0:T(8,128)} %source.1, f32[2,16,5,2,256]{4,3,2,1,0:T(2,128)} %copy-done.6, f32[2,16,5,2,256]{4,3,2,1,0:T(2,128)} %copy-done.7, f32[3,64,128]{2,1,0:T(8,128)} %copy-done.8, ...), custom_call_target="tpu_custom_call" | custom-call | flops 78643200 | bytes 20971520 | tf_op jit(solution)/shard_map/stator_stencil/pallas_call | solution.py:409
  82.8 2.0 %modes.3 = f32[8,2,40,256]{3,2,1,0:T(8,128)S(1)} custom-call(s32[1]{0:T(128)S(6)} %copy.27.offset_ref, f32[8,2,40,256]{3,2,1,0:T(8,128)S(1)} %all-to-all-done.2.got_ref, f32[16,5,128]{2,1,0:T(8,128)S(1)} %bitcast.8, bf16[8,256,256]{2,1,0:T(8,128)(2,1)S(1)} %copy-done.1, bf16[8,256,256]{2,1,0:T(8,128)(2,1)S(1)} %copy-done), custom_call_target="tpu_custom_call" | custom-call | flops 251658240 | bytes 5000000 | tf_op jit(solution)/shard_map/modes/pallas_call | solution.py:143
  84.8 0.0 copy-start.3
  84.8 0.9 copy-done.3
  85.7 0.0 all-to-all-done.1
  85.7 5.7 %all-to-all-start.3 = ((f32[8,2,40,256]{3,2,1,0:T(8,128)}), f32[8,2,40,256]{3,2,1,0:T(8,128)S(1)}, u32[]{:S(2)}, u32[]{:S(2)}) async-start(f32[8,2,40,256]{3,2,1,0:T(8,128)} %copy-done.3), calls=%async_computation.3 | async-start | bytes 1310720 | tf_op jit(solution)/shard_map/all_to_all | solution.py:500
  91.4 0.0 copy-start.4
  91.4 0.0 copy-start.5
  91.4 16.1 %rotor_stencil.1.rotor_ref = f32[5,16,64,256]{3,2,1,0:T(8,128)} custom-call(f32[3,5,5]{2,1,0:T(8,128)} %copy.24.jac_ref, f32[5,5]{1,0:T(8,128)} %mix_ref.5, f32[5,16,64,256]{3,2,1,0:T(8,128)} %source.2, f32[2,16,5,2,256]{4,3,2,1,0:T(2,128)} %copy-done.6, f32[2,16,5,2,256]{4,3,2,1,0:T(2,128)} %copy-done.7, f32[3,64,128]{2,1,0:T(8,128)} %copy-done.8, ...), custom_call_target="tpu_custom_call" | custom-call | flops 78643200 | bytes 20971520 | tf_op jit(solution)/shard_map/rotor_stencil/pallas_call | solution.py:409
  107.5 0.0 all-to-all-done.3
  107.5 0.0 copy-done.4
  107.5 0.0 copy-done.5
  107.5 3.9 %interface.1 = (f32[5,16,64,256]{3,2,1,0:T(8,128)}, f32[5,16,64,256]{3,2,1,0:T(8,128)}) custom-call(f32[3,5,5]{2,1,0:T(8,128)S(1)} %copy-done.4, f32[5,5]{1,0:T(8,128)S(1)} %copy-done.5, f32[8,2,5,8,256]{4,3,2,1,0:T(8,128)S(1)} %bitcast.5, f32[8,2,5,8,256]{4,3,2,1,0:T(8,128)S(1)} %bitcast.6, ...), custom_call_target="tpu_custom_call", output_to_operand_aliasing={{0}: (4, {}), {1}: (5, {})} | custom-call | flops 9830400 | bytes 3932160 | tf_op jit(solution)/shard_map/interface/pallas_call | solution.py:472
Async XLA Ops:
  2.8 23.6 %all-to-all-start = ((f32[8,2,40,256]{3,2,1,0:T(8,128)}), f32[8,2,40,256]{3,2,1,0:T(8,128)S(1)}, u32[]{:S(2)}, u32[]{:S(2)}) async-start(f32[8,2,40,256]{3,2,1,0:T(8,128)} %bitcast.10), calls=%async_computation | async-start | bytes 1310720 | tf_op jit(solution)/shard_map/all_to_all | solution.py:500
  9.2 23.6 %copy-start.9 = (f32[5,2048]{1,0:T(8,128)S(1)}, f32[5,2048]{1,0:T(8,128)}, u32[]{:S(2)}) copy-start(f32[5,2048]{1,0:T(8,128)} %param.18) | copy-start | bytes 122884
  9.2 25.6 %copy-start = (bf16[8,256,256]{2,1,0:T(8,128)(2,1)S(1)}, bf16[8,256,256]{2,1,0:T(8,128)(2,1)}, u32[]{:S(2)}) copy-start(bf16[8,256,256]{2,1,0:T(8,128)(2,1)} %constant.9.clone.low_ref) | copy-start | bytes 3145732
  9.2 25.6 %copy-start.1 = (bf16[8,256,256]{2,1,0:T(8,128)(2,1)S(1)}, bf16[8,256,256]{2,1,0:T(8,128)(2,1)}, u32[]{:S(2)}) copy-start(bf16[8,256,256]{2,1,0:T(8,128)(2,1)} %constant.8.clone.high_ref) | copy-start | bytes 3145732
  16.4 42.5 %copy-start.10 = (f32[3,5,5]{2,0,1:T(4,128)S(1)}, f32[3,5,5]{2,0,1:T(4,128)}, u32[]{:S(2)}) copy-start(f32[3,5,5]{2,0,1:T(4,128)} %param.16) | copy-start | bytes 904
  16.5 9.3 %collective-permute-start = (f32[3,64,128]{2,1,0:T(8,128)}, f32[3,64,128]{2,1,0:T(8,128)S(1)}, u32[]{:S(2)}, u32[]{:S(2)}) collective-permute-start(f32[3,64,128]{2,1,0:T(8,128)} %get-tuple-element.27), channel_id=1, source_target_pairs={{0,4},{4,8},{8,12},{12,16},{16,20},{20,24},{24,28},{28,0},{1,5},{5... | collective-permute-start | bytes 294920 | tf_op jit(solution)/shard_map/ppermute | solution.py:510
  18.0 8.4 %collective-permute-start.1 = (f32[3,64,128]{2,1,0:T(8,128)}, f32[3,64,128]{2,1,0:T(8,128)}, u32[]{:S(2)}, u32[]{:S(2)}) collective-permute-start(f32[3,64,128]{2,1,0:T(8,128)} %get-tuple-element.28), channel_id=1, source_target_pairs={{4,0},{8,4},{12,8},{16,12},{20,16},{24,20},{28,24},{0,28},{5,1},{9... | collective-permute-start | bytes 294920 | tf_op jit(solution)/shard_map/ppermute | solution.py:511
  25.8 0.6 copy-start.8
  26.4 22.0 %all-to-all-start.2 = ((f32[8,2,40,256]{3,2,1,0:T(8,128)}), f32[8,2,40,256]{3,2,1,0:T(8,128)S(1)}, u32[]{:S(2)}, u32[]{:S(2)}) async-start(f32[8,2,40,256]{3,2,1,0:T(8,128)} %bitcast.9), calls=%async_computation.2 | async-start | bytes 1310720 | tf_op jit(solution)/shard_map/all_to_all | solution.py:500
  36.9 0.8 copy-start.2
  48.4 37.2 %all-to-all-start.1 = ((f32[8,2,40,256]{3,2,1,0:T(8,128)}), f32[8,2,40,256]{3,2,1,0:T(8,128)S(1)}, u32[]{:S(2)}, u32[]{:S(2)}) async-start(f32[8,2,40,256]{3,2,1,0:T(8,128)} %copy-done.2), calls=%async_computation.1 | async-start | bytes 1310720 | tf_op jit(solution)/shard_map/all_to_all | solution.py:500
  53.2 8.1 %collective-permute-start.2 = (f32[2,16,5,2,256]{4,3,2,1,0:T(2,128)}, f32[2,16,5,2,256]{4,3,2,1,0:T(2,128)S(1)}, u32[]{:S(2)}, u32[]{:S(2)}) collective-permute-start(f32[2,16,5,2,256]{4,3,2,1,0:T(2,128)} %get-tuple-element.34), channel_id=1, source_target_pairs={{0,1},{1,2},{2,3},{4,5},{5,6},{6,7},{8,9},{9,10},{10,11},{12,13},{... | collective-permute-start | bytes 983048 | tf_op jit(solution)/shard_map/ppermute | solution.py:512
  57.1 8.9 %collective-permute-start.3 = (f32[2,16,5,2,256]{4,3,2,1,0:T(2,128)}, f32[2,16,5,2,256]{4,3,2,1,0:T(2,128)S(1)}, u32[]{:S(2)}, u32[]{:S(2)}) collective-permute-start(f32[2,16,5,2,256]{4,3,2,1,0:T(2,128)} %get-tuple-element.35), channel_id=1, source_target_pairs={{1,0},{2,1},{3,2},{5,4},{6,5},{7,6},{9,8},{10,9},{11,10},{13,12},{... | collective-permute-start | bytes 983048 | tf_op jit(solution)/shard_map/ppermute | solution.py:513
  61.4 4.6 %copy-start.6 = (f32[2,16,5,2,256]{4,3,2,1,0:T(2,128)}, f32[2,16,5,2,256]{4,3,2,1,0:T(2,128)S(1)}, u32[]{:S(2)}) copy-start(f32[2,16,5,2,256]{4,3,2,1,0:T(2,128)S(1)} %collective-permute-done.2.low_ref) | copy-start | bytes 983044
  66.0 0.7 copy-start.7
  84.8 0.9 copy-start.3
  85.7 21.8 %all-to-all-start.3 = ((f32[8,2,40,256]{3,2,1,0:T(8,128)}), f32[8,2,40,256]{3,2,1,0:T(8,128)S(1)}, u32[]{:S(2)}, u32[]{:S(2)}) async-start(f32[8,2,40,256]{3,2,1,0:T(8,128)} %copy-done.3), calls=%async_computation.3 | async-start | bytes 1310720 | tf_op jit(solution)/shard_map/all_to_all | solution.py:500
  91.4 16.1 %copy-start.4 = (f32[3,5,5]{2,1,0:T(8,128)S(1)}, f32[3,5,5]{2,1,0:T(8,128)}, u32[]{:S(2)}) copy-start(f32[3,5,5]{2,1,0:T(8,128)} %copy.24.jac_ref) | copy-start | bytes 904
  91.4 16.1 %copy-start.5 = (f32[5,5]{1,0:T(8,128)S(1)}, f32[5,5]{1,0:T(8,128)}, u32[]{:S(2)}) copy-start(f32[5,5]{1,0:T(8,128)} %mix_ref.5) | copy-start | bytes 304

commit v7 on v5

--- a/solution.py
+++ b/solution.py
@@ -292,7 +292,7 @@
             rim = jnp.where((before >= at) & (before < at + 2), from_left, from_right)
             rim = pltpu.roll(rim, (LANES - at) % LANES, 1)
             rim = jnp.where((lane < 2) | (lane >= LANES - 2), rim, 0.0)
-            span = slice(f * rows, (f + 1) * rows)
+            span = slice((slot * fields + f) * rows, (slot * fields + f + 1) * rows)
             x_high, x_low = halves(state[f, t + 2])
             rim_high, rim_low = halves(rim)
             parts[span, :cols] = x_high
@@ -309,7 +309,6 @@
                 jnp.concatenate([x_high, x_low, halo], axis=0),
                 preferred_element_type=jnp.float32,
             )
-        pitch[slot] = jnp.dot(parts[...], cols_ref[...], preferred_element_type=jnp.float32)
 
     def advance(t, slot):
         here = t + 2
@@ -323,7 +322,7 @@
                     (state[f, here, span, :] * (1.0 - 6.0 * scale) + (near * 4.0 - far) * scale)
                     + (
                         radial[slot, f, rows + at : rows + at + chunk, :]
-                        + pitch[slot, f * rows + at : f * rows + at + chunk, cols:]
+                        + pitch[pl.ds((slot * fields + f) * rows + at, chunk), cols:]
                     )
                 )
             place = at // chunk
@@ -332,18 +331,18 @@
                     (
                         state[g, here + 1, span, :] - state[g, here - 1, span, :],
                         radial[slot, g, span, :],
-                        pitch[slot, g * rows + at : g * rows + at + chunk, :cols],
+                        pitch[pl.ds((slot * fields + g) * rows + at, chunk), :cols],
                     )
                 ):
                     first = (d * fields + g) * chunk
                     high, low = halves(slope)
-                    slopes[slot, place, first : first + chunk, :] = high
-                    slopes[slot, place, wide + first : wide + first + chunk, :] = low
-            mixed = jnp.dot(
-                mixer[:, : 2 * wide], slopes[slot, place], preferred_element_type=jnp.float32
-            ) + jnp.dot(
-                mixer[:, 2 * wide :], slopes[slot, place, :wide, :], preferred_element_type=jnp.float32
+                    slopes[slot, place, 0, first : first + chunk, :] = high
+                    slopes[slot, place, 1, first : first + chunk, :] = low
+            both = jnp.dot(mixer[...], slopes[slot, place, 0], preferred_element_type=jnp.float32)
+            fine = jnp.dot(
+                mixer[: fields * chunk, :], slopes[slot, place, 1], preferred_element_type=jnp.float32
             )
+            mixed = both[: fields * chunk] + (both[fields * chunk :] + fine)
             for f in range(fields):
                 out[f, slot if side == 0 else 1 - slot, span, :] = (
                     totals[f] + mixed[f * chunk : (f + 1) * chunk]
@@ -360,17 +359,13 @@
             entries = jnp.zeros((chunk, wide), jnp.float32)
             for d in range(3):
                 for g in range(fields):
-                    entry = jnp.where(own & (spot // chunk == d * fields + g), jac_ref[d, f, g], 0.0)
+                    entry = jnp.where(own & (spot // chunk == d * fields + g), jac_ref[(d * fields + f) * fields + g], 0.0)
                     entries = entries + (entry * axial if d == 0 else entry)
             high, low = halves(entries)
-            band = slice(f * chunk, (f + 1) * chunk)
-            mixer[band, :wide] = high
-            mixer[band, wide : 2 * wide] = high
-            mixer[band, 2 * wide :] = low
+            mixer[f * chunk : (f + 1) * chunk, :] = high
+            mixer[(fields + f) * chunk : (fields + f + 1) * chunk, :] = low
         used = 3 * fields * chunk
-        blank = jnp.zeros((2, rows // chunk, wide - used, cols), jnp.bfloat16)
-        slopes[:, :, used:wide, :] = blank
-        slopes[:, :, wide + used :, :] = blank
+        slopes[:, :, :, used:, :] = jnp.zeros((2, rows // chunk, 2, wide - used, cols), jnp.bfloat16)
         load(0).wait()
         load(1).wait()
 
@@ -393,6 +388,7 @@
 
     for slot in range(2):
         products(2 * step + slot, slot)
+    pitch[...] = jnp.dot(parts[...], cols_ref[...], preferred_element_type=jnp.float32)
     for slot in range(2):
         advance(2 * step + slot, slot)
 
@@ -416,10 +412,10 @@
         scratch_shapes=[
             pltpu.VMEM((fields, layers + 4, rows, cols), jnp.float32),
             pltpu.VMEM((2, fields, 2 * rows, cols), jnp.float32),
-            pltpu.VMEM((2, fields * rows, 2 * cols), jnp.float32),
-            pltpu.VMEM((fields * rows, 2 * cols + 2 * LANES), jnp.bfloat16),
-            pltpu.VMEM((fields * 16, 6 * LANES), jnp.bfloat16),
-            pltpu.VMEM((2, rows // 16, 4 * LANES, cols), jnp.bfloat16),
+            pltpu.VMEM((2 * fields * rows, 2 * cols), jnp.float32),
+            pltpu.VMEM((2 * fields * rows, 2 * cols + 2 * LANES), jnp.bfloat16),
+            pltpu.VMEM((2 * fields * 16, 2 * LANES), jnp.bfloat16),
+            pltpu.VMEM((2, rows // 16, 2, 2 * LANES, cols), jnp.bfloat16),
             pltpu.SemaphoreType.DMA((layers,)),
         ],
         compiler_params=pltpu.CompilerParams(vmem_limit_bytes=WIDE),
@@ -453,7 +449,7 @@
                 ghosts.append([combine(lambda g: mix_ref[f, g], planes) for f in range(fields)])
             first, second = ghosts
             for f in range(fields):
-                slope = combine(lambda g: jac_ref[0, f, g], first) * (-0.5 * time_step)
+                slope = combine(lambda g: jac_ref[f * fields + g], first) * (-0.5 * time_step)
                 bend = first[f] * 4.0 - second[f]
                 out[f, near, span, :] = ref[f, near, span, :] + (slope + bend * (sign * scale))
                 out[f, far, span, :] = ref[f, far, span, :] - first[f] * (sign * scale)
@@ -511,13 +507,14 @@
     blend = mode_blend.reshape(fields, LANES, OUTER) * (1.0 / NP)
     blend = jnp.moveaxis(blend, 2, 0)[outer_order().reshape(-1)]
     blend = blend.reshape(PAIRS, 2, fields, LANES).transpose(0, 2, 1, 3).reshape(PAIRS, fields, 2 * LANES)
-    received, edges = lax.optimization_barrier((received, edges))
+    received, edges, flat = lax.optimization_barrier((received, edges, jacobians.reshape(-1)))
     sent = transform(received, rotor_offset, blend, fields)
+    sent, edges, flat = lax.optimization_barrier((sent, edges, flat))
     modes = lax.all_to_all(sent, "pitch", 0, 0, tiled=True)
     modes = modes.reshape(count, 2, fields, 2, step, cols)
-    stator_mid = stencil(0, stator, *edges, jacobians, field_mix)
-    rotor_mid = stencil(1, rotor, *edges, jacobians, field_mix)
-    return close(modes, stator_mid, rotor_mid, jacobians, field_mix)
+    stator_mid = stencil(0, stator, *edges, flat, field_mix)
+    rotor_mid = stencil(1, rotor, *edges, flat, field_mix)
+    return close(modes, stator_mid, rotor_mid, flat, field_mix)
 
 
 def solution(mesh):

time: 87.1 us -> 87.7 us (level)
  Pallas kernels: 48.9 us -> 50.1 us
    pallas_call x2, Pallas kernels: 32.2 us -> 33.4 us  [stencil(): pl.pallas_call(functools.partial(stencil_kernel, side, layers), grid=(ste...]
  transfers between devices with their start and end apart: 6 -> 6, of which waited for: 2 -> 2; matrix products, arithmetic and copies ran while one was open for 4% -> 4% of each run, Pallas kernels for 45% -> 46%
where the time goes in v7:
time: 87.7 us; the launch traced here: 87.3 us
  Pallas kernels  50.1 us (57%)
  starting transfers between devices  19.4 us (22%)
  waiting for transfers between devices  13 us (15%)
  local copies, waits for them, and re-layouts  3.35 us (4%)
  between operations  1.47 us (2%)
    pallas_call x2, Pallas kernels, stencil(): pl.pallas_call(functools.partial(stencil_kernel, side, layers), grid=(ste...  33.4 us
    ppermute x1, waiting for transfers between devices, shards(): from_left = lax.ppermute(right, 'pitch', ring)  9.01 us
    all_to_all x1, starting transfers between devices, shards(): received = lax.all_to_all(planes, 'pitch', 0, 0, tiled=True)  7.25 us
    pallas_call x1, Pallas kernels, pack_edges(): pl.pallas_call(pack_kernel, grid=(steps,), out_shape=(edge, edge, side, s...  7.22 us
    all_to_all x1, starting transfers between devices, shards(): modes = lax.all_to_all(sent, 'pitch', 0, 0, tiled=True)  3.98 us
    all_to_all x1, waiting for transfers between devices, shards(): received = lax.all_to_all(planes, 'pitch', 0, 0, tiled=True)  3.95 us
    pallas_call x1, Pallas kernels, close(): pl.pallas_call(close_kernel, grid=(count // group,), out_shape=(shape, sh...  3.94 us
    pallas_call x1, Pallas kernels, transform(): pl.pallas_call(functools.partial(transform_kernel, fields), out_shape=jax...  3.38 us
  transfers between devices with their start and end apart: 6, of which 2 were waited for; matrix products, arithmetic and copies ran while one was open for 4% of the time, Pallas kernels for 46%

profile of v7, /device:TPU:0, one launch (start us, length us, event | category | flops | bytes accessed | tf_op | source)
XLA Modules:
  0.0 87.3 jit_solution(2305410119292269420)
XLA Ops:
  0.6 2.2 %planes.1 = f32[8,2,5,2,8,256]{5,4,3,2,1,0:T(8,128)} custom-call(f32[5,16,64,256]{3,2,1,0:T(8,128)} %source.2, f32[5,16,64,256]{3,2,1,0:T(8,128)} %source.3), custom_call_target="tpu_custom_call" | custom-call | tf_op jit(solution)/shard_map/planes/pallas_call | solution.py:173
  2.8 7.3 %all-to-all-start = ((f32[8,2,80,256]{3,2,1,0:T(8,128)}), f32[8,2,80,256]{3,2,1,0:T(8,128)S(1)}, u32[]{:S(2)}, u32[]{:S(2)}) async-start(f32[8,2,80,256]{3,2,1,0:T(8,128)} %bitcast.9), calls=%async_computation | async-start | bytes 2621440 | tf_op jit(solution)/shard_map/all_to_all | solution.py:497
  10.1 0.0 copy-start.4
  10.1 0.0 copy-start.5
  10.1 0.0 copy-start.6
  10.1 0.0 copy-start
  10.1 0.0 copy-start.1
  10.1 7.2 %edges.1 = (f32[2,16,5,2,256]{4,3,2,1,0:T(2,128)}, f32[2,16,5,2,256]{4,3,2,1,0:T(2,128)}, f32[3,64,128]{2,1,0:T(8,128)}, f32[3,64,128]{2,1,0:T(8,128)}) custom-call(f32[5,16,64,256]{3,2,1,0:T(8,128)} %source.2, f32[5,16,64,256]{3,2,1,0:T(8,128)} %source.3), custom_call_target="tpu_custom_call" | custom-call | bytes 10485760 | tf_op jit(solution)/shard_map/edges/pallas_call | solution.py:223
  17.4 2.1 %collective-permute-start.2 = (f32[3,64,128]{2,1,0:T(8,128)}, f32[3,64,128]{2,1,0:T(8,128)}, u32[]{:S(2)}, u32[]{:S(2)}) collective-permute-start(f32[3,64,128]{2,1,0:T(8,128)} %get-tuple-element.26), channel_id=1, source_target_pairs={{0,4},{4,8},{8,12},{12,16},{16,20},{20,24},{24,28},{28,0},{1,5},{5... | collective-permute-start | bytes 294920 | tf_op jit(solution)/shard_map/ppermute | solution.py:501
  19.4 2.8 %collective-permute-start.3 = (f32[3,64,128]{2,1,0:T(8,128)}, f32[3,64,128]{2,1,0:T(8,128)}, u32[]{:S(2)}, u32[]{:S(2)}) collective-permute-start(f32[3,64,128]{2,1,0:T(8,128)} %get-tuple-element.27), channel_id=1, source_target_pairs={{4,0},{8,4},{12,8},{16,12},{20,16},{24,20},{28,24},{0,28},{5,1},{9... | collective-permute-start | bytes 294920 | tf_op jit(solution)/shard_map/ppermute | solution.py:502
  22.2 2.0 %collective-permute-start = (f32[2,16,5,2,256]{4,3,2,1,0:T(2,128)}, f32[2,16,5,2,256]{4,3,2,1,0:T(2,128)}, u32[]{:S(2)}, u32[]{:S(2)}) collective-permute-start(f32[2,16,5,2,256]{4,3,2,1,0:T(2,128)} %get-tuple-element.24), channel_id=1, source_target_pairs={{0,1},{1,2},{2,3},{4,5},{5,6},{6,7},{8,9},{9,10},{10,11},{12,13},{... | collective-permute-start | bytes 983048 | tf_op jit(solution)/shard_map/ppermute | solution.py:503
  24.2 1.3 %collective-permute-start.1 = (f32[2,16,5,2,256]{4,3,2,1,0:T(2,128)}, f32[2,16,5,2,256]{4,3,2,1,0:T(2,128)}, u32[]{:S(2)}, u32[]{:S(2)}) collective-permute-start(f32[2,16,5,2,256]{4,3,2,1,0:T(2,128)} %get-tuple-element.25), channel_id=1, source_target_pairs={{1,0},{2,1},{3,2},{5,4},{6,5},{7,6},{9,8},{10,9},{11,10},{13,12},{... | collective-permute-start | bytes 983048 | tf_op jit(solution)/shard_map/ppermute | solution.py:504
  25.5 0.0 copy-done.4
  26.2 0.0 copy-done.5
  26.2 0.7 reshape.23.jac_ref
  26.8 0.9 mul.11
  27.7 1.1 %copy.20 = f32[5,128,16]{1,0,2:T(8,128)S(1)} copy(f32[5,128,16]{2,1,0:T(8,128)} %mul.11) | data formatting | bytes 81920 | tf_op jit(solution)/shard_map/mul | solution.py:507
  28.9 0.0 copy-done.6
  28.9 0.6 gather_fusion
  29.5 9.0 %collective-permute-done.2.left_ref = f32[3,64,128]{2,1,0:T(8,128)} collective-permute-done((f32[3,64,128]{2,1,0:T(8,128)}, f32[3,64,128]{2,1,0:T(8,128)}, u32[]{:S(2)}, u32[]{:S(2)}) %collective-permute-start.2) | collective-permute-done | bytes 98336 | tf_op jit(solution)/shard_map/ppermute | solution.py:501
  38.6 0.0 collective-permute-done.3.right_ref
  38.6 0.0 collective-permute-done.low_ref
  38.6 0.0 collective-permute-done.1.high_ref
  38.6 3.9 %all-to-all-done.got_ref = f32[8,2,80,256]{3,2,1,0:T(8,128)S(1)} async-done(((f32[8,2,80,256]{3,2,1,0:T(8,128)}), f32[8,2,80,256]{3,2,1,0:T(8,128)S(1)}, u32[]{:S(2)}, u32[]{:S(2)}) %all-to-all-start) | async-done | bytes 1310752 | tf_op jit(solution)/shard_map/all_to_all | solution.py:497
  42.5 0.0 copy-done
  42.5 0.0 copy-done.1
  42.5 3.4 %modes.1 = f32[8,2,80,256]{3,2,1,0:T(8,128)} custom-call(s32[1]{0:T(128)S(6)} %copy.25.offset_ref, f32[8,2,80,256]{3,2,1,0:T(8,128)S(1)} %all-to-all-done.got_ref, f32[8,5,256]{2,1,0:T(8,128)S(1)} %copy.22.blend_ref, bf16[8,256,256]{2,1,0:T(8,128)(2,1)S(1)} %copy-done.1, bf16[8,256,256]{2,1,0:T(8,128)(2,1)S(1)} %copy-done), custom_call_target="tpu_custom_call" | custom-call | flops 503316480 | bytes 5000000 | tf_op jit(solution)/shard_map/modes/pallas_call | solution.py:142
  45.9 4.0 %all-to-all-start.1 = ((f32[8,2,80,256]{3,2,1,0:T(8,128)}), f32[8,2,80,256]{3,2,1,0:T(8,128)S(1)}, u32[]{:S(2)}, u32[]{:S(2)}) async-start(f32[8,2,80,256]{3,2,1,0:T(8,128)} %modes.1), calls=%async_computation.1 | async-start | bytes 2621440 | tf_op jit(solution)/shard_map/all_to_all | solution.py:513
  49.9 16.7 %rotor_stencil.1.rotor_ref = f32[5,16,64,256]{3,2,1,0:T(8,128)} custom-call(f32[75]{0:T(128)} %reshape.23.jac_ref, f32[5,5]{1,0:T(8,128)} %mix_ref.5, f32[5,16,64,256]{3,2,1,0:T(8,128)} %source.3, f32[2,16,5,2,256]{4,3,2,1,0:T(2,128)} %collective-permute-done.low_ref, f32[2,16,5,2,256]{4,3,2,1,0:T(2,128)} %collective-permute-done.1.high_ref, ...), custom_call_target="tpu_custom_call" | custom-call | flops 78643200 | bytes 20971520 | tf_op jit(solution)/shard_map/rotor_stencil/pallas_call | solution.py:404
  66.6 0.0 copy-start.2
  66.6 0.0 copy-start.3
  66.6 16.7 %stator_stencil.1.stator_ref = f32[5,16,64,256]{3,2,1,0:T(8,128)} custom-call(f32[75]{0:T(128)} %reshape.23.jac_ref, f32[5,5]{1,0:T(8,128)} %mix_ref.5, f32[5,16,64,256]{3,2,1,0:T(8,128)} %source.2, f32[2,16,5,2,256]{4,3,2,1,0:T(2,128)} %collective-permute-done.low_ref, f32[2,16,5,2,256]{4,3,2,1,0:T(2,128)} %collective-permute-done.1.high_ref, ...), custom_call_target="tpu_custom_call" | custom-call | flops 78643200 | bytes 20971520 | tf_op jit(solution)/shard_map/stator_stencil/pallas_call | solution.py:404
  83.3 0.0 all-to-all-done.1
  83.3 0.0 copy-done.2
  83.3 0.0 copy-done.3
  83.3 3.9 %interface.1 = (f32[5,16,64,256]{3,2,1,0:T(8,128)}, f32[5,16,64,256]{3,2,1,0:T(8,128)}) custom-call(f32[75]{0:T(128)S(1)} %copy-done.3, f32[5,5]{1,0:T(8,128)S(1)} %copy-done.2, f32[8,2,5,2,8,256]{5,4,3,2,1,0:T(8,128)S(1)} %bitcast.8, f32[5,16,64,256]{3,2,1,0:T(8,128)} %stator_stencil.1.stator_ref, ...), custom_call_target="tpu_custom_call", output_to_operand_aliasing={{0}: (3, {}), {1}: (4, {})} | custom-call | flops 9830400 | bytes 3932160 | tf_op jit(solution)/shard_map/interface/pallas_call | solution.py:468
  (6 shorter events, 0.1 us)
Async XLA Ops:
  2.8 39.7 %all-to-all-start = ((f32[8,2,80,256]{3,2,1,0:T(8,128)}), f32[8,2,80,256]{3,2,1,0:T(8,128)S(1)}, u32[]{:S(2)}, u32[]{:S(2)}) async-start(f32[8,2,80,256]{3,2,1,0:T(8,128)} %bitcast.9), calls=%async_computation | async-start | bytes 2621440 | tf_op jit(solution)/shard_map/all_to_all | solution.py:497
  10.1 15.4 %copy-start.4 = (f32[5,2048]{1,0:T(8,128)S(1)}, f32[5,2048]{1,0:T(8,128)}, u32[]{:S(2)}) copy-start(f32[5,2048]{1,0:T(8,128)} %param.18) | copy-start | bytes 122884
  10.1 16.1 %copy-start.5 = (f32[3,5,5]{2,0,1:T(4,128)S(1)}, f32[3,5,5]{2,0,1:T(4,128)}, u32[]{:S(2)}) copy-start(f32[3,5,5]{2,0,1:T(4,128)} %param.16) | copy-start | bytes 904
  10.1 18.8 %copy-start.6 = (s32[16]{0:T(128)S(1)}, s32[16]{0:T(128)}, u32[]{:S(2)}) copy-start(s32[16]{0:T(128)} %constant.23) | copy-start | bytes 196
  10.1 32.4 %copy-start = (bf16[8,256,256]{2,1,0:T(8,128)(2,1)S(1)}, bf16[8,256,256]{2,1,0:T(8,128)(2,1)}, u32[]{:S(2)}) copy-start(bf16[8,256,256]{2,1,0:T(8,128)(2,1)} %constant.19.clone.low_ref) | copy-start | bytes 3145732
  10.1 32.4 %copy-start.1 = (bf16[8,256,256]{2,1,0:T(8,128)(2,1)S(1)}, bf16[8,256,256]{2,1,0:T(8,128)(2,1)}, u32[]{:S(2)}) copy-start(bf16[8,256,256]{2,1,0:T(8,128)(2,1)} %constant.18.clone.high_ref) | copy-start | bytes 3145732
  17.4 21.2 %collective-permute-start.2 = (f32[3,64,128]{2,1,0:T(8,128)}, f32[3,64,128]{2,1,0:T(8,128)}, u32[]{:S(2)}, u32[]{:S(2)}) collective-permute-start(f32[3,64,128]{2,1,0:T(8,128)} %get-tuple-element.26), channel_id=1, source_target_pairs={{0,4},{4,8},{8,12},{12,16},{16,20},{20,24},{24,28},{28,0},{1,5},{5... | collective-permute-start | bytes 294920 | tf_op jit(solution)/shard_map/ppermute | solution.py:501
  19.4 19.1 %collective-permute-start.3 = (f32[3,64,128]{2,1,0:T(8,128)}, f32[3,64,128]{2,1,0:T(8,128)}, u32[]{:S(2)}, u32[]{:S(2)}) collective-permute-start(f32[3,64,128]{2,1,0:T(8,128)} %get-tuple-element.27), channel_id=1, source_target_pairs={{4,0},{8,4},{12,8},{16,12},{20,16},{24,20},{28,24},{0,28},{5,1},{9... | collective-permute-start | bytes 294920 | tf_op jit(solution)/shard_map/ppermute | solution.py:502
  22.2 16.4 %collective-permute-start = (f32[2,16,5,2,256]{4,3,2,1,0:T(2,128)}, f32[2,16,5,2,256]{4,3,2,1,0:T(2,128)}, u32[]{:S(2)}, u32[]{:S(2)}) collective-permute-start(f32[2,16,5,2,256]{4,3,2,1,0:T(2,128)} %get-tuple-element.24), channel_id=1, source_target_pairs={{0,1},{1,2},{2,3},{4,5},{5,6},{6,7},{8,9},{9,10},{10,11},{12,13},{... | collective-permute-start | bytes 983048 | tf_op jit(solution)/shard_map/ppermute | solution.py:503
  24.2 14.4 %collective-permute-start.1 = (f32[2,16,5,2,256]{4,3,2,1,0:T(2,128)}, f32[2,16,5,2,256]{4,3,2,1,0:T(2,128)}, u32[]{:S(2)}, u32[]{:S(2)}) collective-permute-start(f32[2,16,5,2,256]{4,3,2,1,0:T(2,128)} %get-tuple-element.25), channel_id=1, source_target_pairs={{1,0},{2,1},{3,2},{5,4},{6,5},{7,6},{9,8},{10,9},{11,10},{13,12},{... | collective-permute-start | bytes 983048 | tf_op jit(solution)/shard_map/ppermute | solution.py:504
  45.9 37.4 %all-to-all-start.1 = ((f32[8,2,80,256]{3,2,1,0:T(8,128)}), f32[8,2,80,256]{3,2,1,0:T(8,128)S(1)}, u32[]{:S(2)}, u32[]{:S(2)}) async-start(f32[8,2,80,256]{3,2,1,0:T(8,128)} %modes.1), calls=%async_computation.1 | async-start | bytes 2621440 | tf_op jit(solution)/shard_map/all_to_all | solution.py:513
  66.6 16.7 %copy-start.2 = (f32[5,5]{1,0:T(8,128)S(1)}, f32[5,5]{1,0:T(8,128)}, u32[]{:S(2)}) copy-start(f32[5,5]{1,0:T(8,128)} %mix_ref.5) | copy-start | bytes 304
  66.6 16.7 %copy-start.3 = (f32[75]{0:T(128)S(1)}, f32[75]{0:T(128)}, u32[]{:S(2)}) copy-start(f32[75]{0:T(128)} %reshape.23.jac_ref) | copy-start | bytes 904

commit v8 on v5

--- a/solution.py
+++ b/solution.py
@@ -268,19 +268,70 @@
 
 
 def stencil_kernel(
-    side, layers, jac_ref, mix_ref, source, low_ref, high_ref, left_ref, right_ref, rows_ref, cols_ref,
-    out, state, radial, pitch, parts, mixer, slopes, sems,
+    layers, jac_ref, mix_ref, stator_hbm, rotor_hbm, low_ref, high_ref, left_ref, right_ref, rows_ref,
+    cols_ref, stator_out, rotor_out, state, radial, pitch, parts, mixer, slopes, sems,
 ):
+    fields, _, rows, cols = stator_out.shape
+    chunk, wide = 16, 2 * LANES
+    steps = layers // 2
     step = pl.program_id(0)
+    sources = (stator_hbm, rotor_hbm)
+
+    def load(side, layer):
+        taken = layer if side == 0 else layers - 1 - layer
+        return pltpu.make_async_copy(
+            sources[side].at[:, taken], state.at[side, :, layer + 2], sems.at[side, layer]
+        )
+
+    @pl.when(step == 0)
+    def _():
+        for side in range(2):
+            for layer in range(layers):
+                load(side, layer).start()
+        state[:, :, 0:2] = jnp.zeros((2, fields, 2, rows, cols), jnp.float32)
+        spot = lax.broadcasted_iota(jnp.int32, (chunk, wide), 1)
+        own = spot % chunk == lax.broadcasted_iota(jnp.int32, (chunk, wide), 0)
+        for f in range(fields):
+            axial = jnp.zeros((chunk, wide), jnp.float32)
+            others = jnp.zeros((chunk, wide), jnp.float32)
+            for d in range(3):
+                for g in range(fields):
+                    here = own & (spot // chunk == d * fields + g)
+                    entry = jnp.where(here, jac_ref[(d * fields + f) * fields + g], 0.0)
+                    if d == 0:
+                        axial = axial + entry
+                    else:
+                        others = others + entry
+            band = slice(f * chunk, (f + 1) * chunk)
+            for side in range(2):
+                high, low = halves(others + axial * ((0.5 if side else -0.5) * time_step))
+                mixer[side, band, :wide] = high
+                mixer[side, band, wide : 2 * wide] = high
+                mixer[side, band, 2 * wide :] = low
+        used = 3 * fields * chunk
+        blank = jnp.zeros((2, rows // chunk, wide - used, cols), jnp.bfloat16)
+        slopes[:, :, used:wide, :] = blank
+        slopes[:, :, wide + used :, :] = blank
+
+    for side, out in enumerate((stator_out, rotor_out)):
+
+        @pl.when(step // steps == side)
+        def _():
+            stencil_step(
+                side, step - side * steps, layers, functools.partial(load, side), mix_ref, low_ref.at[side],
+                high_ref.at[side], left_ref, right_ref, rows_ref, cols_ref, out, state.at[side], radial,
+                pitch, parts, mixer.at[side], slopes,
+            )
+
+
+def stencil_step(
+    side, step, layers, load, mix_ref, low_ref, high_ref, left_ref, right_ref, rows_ref, cols_ref,
+    out, state, radial, pitch, parts, mixer, slopes,
+):
     fields, _, rows, cols = out.shape
     chunk, wide = 16, 2 * LANES
     scale = time_step * damping
-    axial = (0.5 if side else -0.5) * time_step
     lane = lax.broadcasted_iota(jnp.int32, (rows, LANES), 1)
-
-    def load(layer):
-        taken = layer if side == 0 else layers - 1 - layer
-        return pltpu.make_async_copy(source.at[:, taken], state.at[:, layer + 2], sems.at[layer])
 
     def products(t, slot):
         unit = 2 * t + side
@@ -300,7 +351,7 @@
             parts[span, 2 * cols : 2 * cols + LANES] = rim_high
             parts[span, 2 * cols + LANES :] = rim_low
             halo = jnp.concatenate(
-                [low_ref[0, t, f], high_ref[0, t, f], jnp.zeros((4, cols), jnp.float32)], axis=0
+                [low_ref[t, f], high_ref[t, f], jnp.zeros((4, cols), jnp.float32)], axis=0
             )
             halo_high = halo.astype(jnp.bfloat16).astype(jnp.float32)
             halo = jnp.concatenate([halo_high, halo - halo_high], axis=0).astype(jnp.bfloat16)
@@ -351,26 +402,6 @@
 
     @pl.when(step == 0)
     def _():
-        for layer in range(layers):
-            load(layer).start()
-        state[:, 0:2] = jnp.zeros((fields, 2, rows, cols), jnp.float32)
-        spot = lax.broadcasted_iota(jnp.int32, (chunk, wide), 1)
-        own = spot % chunk == lax.broadcasted_iota(jnp.int32, (chunk, wide), 0)
-        for f in range(fields):
-            entries = jnp.zeros((chunk, wide), jnp.float32)
-            for d in range(3):
-                for g in range(fields):
-                    entry = jnp.where(own & (spot // chunk == d * fields + g), jac_ref[d, f, g], 0.0)
-                    entries = entries + (entry * axial if d == 0 else entry)
-            high, low = halves(entries)
-            band = slice(f * chunk, (f + 1) * chunk)
-            mixer[band, :wide] = high
-            mixer[band, wide : 2 * wide] = high
-            mixer[band, 2 * wide :] = low
-        used = 3 * fields * chunk
-        blank = jnp.zeros((2, rows // chunk, wide - used, cols), jnp.bfloat16)
-        slopes[:, :, used:wide, :] = blank
-        slopes[:, :, wide + used :, :] = blank
         load(0).wait()
         load(1).wait()
 
@@ -397,44 +428,61 @@
         advance(2 * step + slot, slot)
 
 
-def stencil(side, state, low, high, left, right, weights, mix):
-    fields, layers, rows, cols = state.shape
+def stencil(stator, rotor, low, high, left, right, jacobians, mix):
+    fields, layers, rows, cols = stator.shape
     along_rows, along_cols = difference_tables(rows, cols)
+    steps = layers // 2
+    block = (fields, 2, rows, cols)
     smem = pl.BlockSpec(memory_space=pltpu.SMEM)
     vmem = pl.BlockSpec(memory_space=pltpu.VMEM)
-    edge_spec = pl.BlockSpec((1, layers, fields, 2, cols), lambda t: (side, 0, 0, 0, 0))
-    side_spec = pl.BlockSpec(left.shape, lambda t: (0, 0, 0))
-    steps = layers // 2
+    hbm = pl.BlockSpec(memory_space=pl.ANY)
+    shape = jax.ShapeDtypeStruct(stator.shape, jnp.float32)
     return pl.pallas_call(
-        functools.partial(stencil_kernel, side, layers),
-        grid=(steps,),
-        out_shape=jax.ShapeDtypeStruct(state.shape, jnp.float32),
-        in_specs=[smem, smem, pl.BlockSpec(memory_space=pl.ANY), edge_spec, edge_spec, side_spec, side_spec, vmem, vmem],
-        out_specs=pl.BlockSpec(
-            (fields, 2, rows, cols), lambda t: (0, t if side == 0 else steps - 1 - t, 0, 0)
+        functools.partial(stencil_kernel, layers),
+        grid=(2 * steps,),
+        out_shape=(shape, shape),
+        in_specs=[smem, smem, hbm, hbm] + [vmem] * 6,
+        out_specs=(
+            pl.BlockSpec(block, lambda t: (0, jnp.minimum(t, steps - 1), 0, 0)),
+            pl.BlockSpec(block, lambda t: (0, steps - 1 - jnp.maximum(t - steps, 0), 0, 0)),
         ),
         scratch_shapes=[
-            pltpu.VMEM((fields, layers + 4, rows, cols), jnp.float32),
+            pltpu.VMEM((2, fields, layers + 4, rows, cols), jnp.float32),
             pltpu.VMEM((2, fields, 2 * rows, cols), jnp.float32),
             pltpu.VMEM((2, fields * rows, 2 * cols), jnp.float32),
             pltpu.VMEM((fields * rows, 2 * cols + 2 * LANES), jnp.bfloat16),
-            pltpu.VMEM((fields * 16, 6 * LANES), jnp.bfloat16),
+            pltpu.VMEM((2, fields * 16, 6 * LANES), jnp.bfloat16),
             pltpu.VMEM((2, rows // 16, 4 * LANES, cols), jnp.bfloat16),
-            pltpu.SemaphoreType.DMA((layers,)),
+            pltpu.SemaphoreType.DMA((2, layers)),
         ],
         compiler_params=pltpu.CompilerParams(vmem_limit_bytes=WIDE),
         cost_estimate=pl.CostEstimate(
-            flops=60 * state.size, bytes_accessed=16 * state.size, transcendentals=0
+            flops=120 * stator.size, bytes_accessed=32 * stator.size, transcendentals=0
         ),
-        name=("stator_stencil", "rotor_stencil")[side],
-    )(weights, mix, state, low, high, left, right, jnp.asarray(along_rows), jnp.asarray(along_cols))
-
-
-def close_kernel(jac_ref, mix_ref, modes_ref, stator_ref, rotor_ref, stator_out, rotor_out):
-    fields = stator_ref.shape[0]
-    count = modes_ref.shape[0]
-    step = modes_ref.shape[4]
+        name="stencil",
+    )(jacobians, mix, stator, rotor, low, high, left, right, jnp.asarray(along_rows), jnp.asarray(along_cols))
+
+
+def close_kernel(
+    jac_ref, mix_ref, modes_ref, stator_ref, rotor_ref, stator_out, rotor_out, before, after, sems
+):
+    count, _, fields, _, step, cols = modes_ref.shape
+    layers = stator_ref.shape[1]
+    pieces, _, _, _, height, _ = before.shape
+    group = height // step
     scale = time_step * damping
+    refs = ((stator_ref, stator_out, layers - 2), (rotor_ref, rotor_out, 0))
+
+    def spot(side, piece):
+        return slice(None), pl.ds(refs[side][2], 2), pl.ds(piece * height, height)
+
+    def fetch(side, piece):
+        given = refs[side][0].at[spot(side, piece)]
+        return pltpu.make_async_copy(given, before.at[piece, side], sems.at[0, piece, side])
+
+    def store(side, piece):
+        out = refs[side][1].at[spot(side, piece)]
+        return pltpu.make_async_copy(after.at[piece, side], out, sems.at[1, piece, side])
 
     def combine(row, sources):
         total = row(0) * sources[0]
@@ -442,44 +490,47 @@
             total = total + row(g) * sources[g]
         return total
 
-    for side, (ref, out) in enumerate(((stator_ref, stator_out), (rotor_ref, rotor_out))):
+    order = [(side, piece) for piece in range(pieces) for side in range(2)]
+    for side, piece in order:
+        fetch(side, piece).start()
+    for side, piece in order:
         near, far = (1, 0) if side == 0 else (0, 1)
         sign = -1.0 if side else 1.0
-        for q in range(count):
+        fetch(side, piece).wait()
+        for q in range(group):
             span = slice(q * step, (q + 1) * step)
             ghosts = []
             for ghost in range(2):
-                planes = [modes_ref[q, side, g, ghost] for g in range(fields)]
+                planes = [modes_ref[piece * group + q, side, g, ghost] for g in range(fields)]
                 ghosts.append([combine(lambda g: mix_ref[f, g], planes) for f in range(fields)])
             first, second = ghosts
             for f in range(fields):
-                slope = combine(lambda g: jac_ref[0, f, g], first) * (-0.5 * time_step)
+                slope = combine(lambda g: jac_ref[f * fields + g], first) * (-0.5 * time_step)
                 bend = first[f] * 4.0 - second[f]
-                out[f, near, span, :] = ref[f, near, span, :] + (slope + bend * (sign * scale))
-                out[f, far, span, :] = ref[f, far, span, :] - first[f] * (sign * scale)
+                after[piece, side, f, near, span, :] = before[piece, side, f, near, span, :] + (
+                    slope + bend * (sign * scale)
+                )
+                after[piece, side, f, far, span, :] = before[piece, side, f, far, span, :] - first[f] * (
+                    sign * scale
+                )
+        store(side, piece).start()
+    for side, piece in order:
+        store(side, piece).wait()
 
 
 def close(modes, stator, rotor, jacobians, field_mix):
     fields, layers, rows, cols = stator.shape
-    count, _, _, _, step, _ = modes.shape
-    group = max(1, count // 4)
-    block = (fields, 2, rows // count * group, cols)
-    specs = (
-        pl.BlockSpec(block, lambda q: (0, layers // 2 - 1, q, 0)),
-        pl.BlockSpec(block, lambda q: (0, 0, q, 0)),
-    )
+    pieces = max(n for n in (4, 2, 1) if rows % (8 * n) == 0 and modes.shape[0] % n == 0)
+    smem = pl.BlockSpec(memory_space=pltpu.SMEM)
+    hbm = pl.BlockSpec(memory_space=pl.ANY)
     shape = jax.ShapeDtypeStruct(stator.shape, jnp.float32)
+    buffer = pltpu.VMEM((pieces, 2, fields, 2, rows // pieces, cols), jnp.float32)
     return pl.pallas_call(
         close_kernel,
-        grid=(count // group,),
         out_shape=(shape, shape),
-        in_specs=[
-            pl.BlockSpec(memory_space=pltpu.SMEM),
-            pl.BlockSpec(memory_space=pltpu.SMEM),
-            pl.BlockSpec((group,) + modes.shape[1:], lambda q: (q, 0, 0, 0, 0, 0)),
-            *specs,
-        ],
-        out_specs=specs,
+        in_specs=[smem, smem, pl.BlockSpec(memory_space=pltpu.VMEM), hbm, hbm],
+        out_specs=(hbm, hbm),
+        scratch_shapes=[buffer, buffer, pltpu.SemaphoreType.DMA((2, pieces, 2))],
         input_output_aliases={3: 0, 4: 1},
         compiler_params=pltpu.CompilerParams(vmem_limit_bytes=NARROW),
         cost_estimate=pl.CostEstimate(
@@ -511,13 +562,13 @@
     blend = mode_blend.reshape(fields, LANES, OUTER) * (1.0 / NP)
     blend = jnp.moveaxis(blend, 2, 0)[outer_order().reshape(-1)]
     blend = blend.reshape(PAIRS, 2, fields, LANES).transpose(0, 2, 1, 3).reshape(PAIRS, fields, 2 * LANES)
-    received, edges = lax.optimization_barrier((received, edges))
+    received, edges, flat = lax.optimization_barrier((received, edges, jacobians.reshape(-1)))
     sent = transform(received, rotor_offset, blend, fields)
+    sent, edges, flat = lax.optimization_barrier((sent, edges, flat))
     modes = lax.all_to_all(sent, "pitch", 0, 0, tiled=True)
     modes = modes.reshape(count, 2, fields, 2, step, cols)
-    stator_mid = stencil(0, stator, *edges, jacobians, field_mix)
-    rotor_mid = stencil(1, rotor, *edges, jacobians, field_mix)
-    return close(modes, stator_mid, rotor_mid, jacobians, field_mix)
+    stator_mid, rotor_mid = stencil(stator, rotor, *edges, flat, field_mix)
+    return close(modes, stator_mid, rotor_mid, flat, field_mix)
 
 
 def solution(mesh):

time: 87.1 us -> 85.1 us (0.977)
  Pallas kernels: 48.9 us -> 45.4 us
  waiting for transfers between devices: 13.7 us -> 15.2 us
    pallas_call x3 -> x2, Pallas kernels: 36.1 us -> 32.6 us  [the longest x1 29.4 us: stencil(): pl.pallas_call(functools.partial(stencil_kernel, layers), grid=(2 * steps...]
    all_to_all x1, waiting for transfers between devices: 0.01 us -> 2.13 us  [shards(): modes = lax.all_to_all(sent, 'pitch', 0, 0, tiled=True)]
  transfers between devices with their start and end apart: 6 -> 6, of which waited for: 2 -> 3; matrix products, arithmetic and copies ran while one was open for 4% -> 4% of each run, Pallas kernels for 45% -> 43%
where the time goes in v8:
time: 85.1 us; the launch traced here: 84.6 us
  Pallas kernels  45.4 us (53%)
  starting transfers between devices  19.3 us (23%)
  waiting for transfers between devices  15.2 us (18%)
  local copies, waits for them, and re-layouts  3.27 us (4%)
  between operations  1.43 us (2%)
    pallas_call x1, Pallas kernels, stencil(): pl.pallas_call(functools.partial(stencil_kernel, layers), grid=(2 * steps...  29.4 us
    ppermute x1, waiting for transfers between devices, shards(): from_left = lax.ppermute(right, 'pitch', ring)  9.1 us
    all_to_all x1, starting transfers between devices, shards(): received = lax.all_to_all(planes, 'pitch', 0, 0, tiled=True)  7.25 us
    pallas_call x1, Pallas kernels, pack_edges(): pl.pallas_call(pack_kernel, grid=(steps,), out_shape=(edge, edge, side, s...  7.21 us
    all_to_all x1, starting transfers between devices, shards(): modes = lax.all_to_all(sent, 'pitch', 0, 0, tiled=True)  3.98 us
    all_to_all x1, waiting for transfers between devices, shards(): received = lax.all_to_all(planes, 'pitch', 0, 0, tiled=True)  3.95 us
    pallas_call x1, Pallas kernels, transform(): pl.pallas_call(functools.partial(transform_kernel, fields), out_shape=jax...  3.37 us
    pallas_call x1, Pallas kernels, close(): pl.pallas_call(close_kernel, out_shape=(shape, shape), in_specs=[smem, sm...  3.2 us
  transfers between devices with their start and end apart: 6, of which 3 were waited for; matrix products, arithmetic and copies ran while one was open for 4% of the time, Pallas kernels for 43%

profile of v8, /device:TPU:0, one launch (start us, length us, event | category | flops | bytes accessed | tf_op | source)
XLA Modules:
  0.0 84.6 jit_solution(15662525933422186838)
XLA Ops:
  0.6 2.2 %planes.1 = f32[8,2,5,2,8,256]{5,4,3,2,1,0:T(8,128)} custom-call(f32[5,16,64,256]{3,2,1,0:T(8,128)} %stator_hbm.1, f32[5,16,64,256]{3,2,1,0:T(8,128)} %rotor_hbm.1), custom_call_target="tpu_custom_call" | custom-call | tf_op jit(solution)/shard_map/planes/pallas_call | solution.py:173
  2.8 7.3 %all-to-all-start = ((f32[8,2,80,256]{3,2,1,0:T(8,128)}), f32[8,2,80,256]{3,2,1,0:T(8,128)S(1)}, u32[]{:S(2)}, u32[]{:S(2)}) async-start(f32[8,2,80,256]{3,2,1,0:T(8,128)} %bitcast.9), calls=%async_computation | async-start | bytes 2621440 | tf_op jit(solution)/shard_map/all_to_all | solution.py:552
  10.1 0.0 copy-start.4
  10.1 0.0 copy-start.5
  10.1 0.0 copy-start.6
  10.1 0.0 copy-start
  10.1 0.0 copy-start.1
  10.1 7.2 %edges.1 = (f32[2,16,5,2,256]{4,3,2,1,0:T(2,128)}, f32[2,16,5,2,256]{4,3,2,1,0:T(2,128)}, f32[3,64,128]{2,1,0:T(8,128)}, f32[3,64,128]{2,1,0:T(8,128)}) custom-call(f32[5,16,64,256]{3,2,1,0:T(8,128)} %stator_hbm.1, f32[5,16,64,256]{3,2,1,0:T(8,128)} %rotor_hbm.1), custom_call_target="tpu_custom_call" | custom-call | bytes 10485760 | tf_op jit(solution)/shard_map/edges/pallas_call | solution.py:223
  17.3 2.1 %collective-permute-start.2 = (f32[3,64,128]{2,1,0:T(8,128)}, f32[3,64,128]{2,1,0:T(8,128)}, u32[]{:S(2)}, u32[]{:S(2)}) collective-permute-start(f32[3,64,128]{2,1,0:T(8,128)} %get-tuple-element.28), channel_id=1, source_target_pairs={{0,4},{4,8},{8,12},{12,16},{16,20},{20,24},{24,28},{28,0},{1,5},{5... | collective-permute-start | bytes 294920 | tf_op jit(solution)/shard_map/ppermute | solution.py:556
  19.4 2.8 %collective-permute-start.3 = (f32[3,64,128]{2,1,0:T(8,128)}, f32[3,64,128]{2,1,0:T(8,128)}, u32[]{:S(2)}, u32[]{:S(2)}) collective-permute-start(f32[3,64,128]{2,1,0:T(8,128)} %get-tuple-element.29), channel_id=1, source_target_pairs={{4,0},{8,4},{12,8},{16,12},{20,16},{24,20},{28,24},{0,28},{5,1},{9... | collective-permute-start | bytes 294920 | tf_op jit(solution)/shard_map/ppermute | solution.py:557
  22.2 2.0 %collective-permute-start = (f32[2,16,5,2,256]{4,3,2,1,0:T(2,128)}, f32[2,16,5,2,256]{4,3,2,1,0:T(2,128)}, u32[]{:S(2)}, u32[]{:S(2)}) collective-permute-start(f32[2,16,5,2,256]{4,3,2,1,0:T(2,128)} %get-tuple-element.26), channel_id=1, source_target_pairs={{0,1},{1,2},{2,3},{4,5},{5,6},{6,7},{8,9},{9,10},{10,11},{12,13},{... | collective-permute-start | bytes 983048 | tf_op jit(solution)/shard_map/ppermute | solution.py:558
  24.2 1.3 %collective-permute-start.1 = (f32[2,16,5,2,256]{4,3,2,1,0:T(2,128)}, f32[2,16,5,2,256]{4,3,2,1,0:T(2,128)}, u32[]{:S(2)}, u32[]{:S(2)}) collective-permute-start(f32[2,16,5,2,256]{4,3,2,1,0:T(2,128)} %get-tuple-element.27), channel_id=1, source_target_pairs={{1,0},{2,1},{3,2},{5,4},{6,5},{7,6},{9,8},{10,9},{11,10},{13,12},{... | collective-permute-start | bytes 983048 | tf_op jit(solution)/shard_map/ppermute | solution.py:559
  25.5 0.0 copy-done.4
  26.1 0.0 copy-done.5
  26.2 0.6 reshape.23.jac_ref
  26.8 0.9 %mul.11 = f32[5,128,16]{2,1,0:T(8,128)} reshape(f32[5,2048]{1,0:T(8,128)S(1)} %broadcast_multiply_fusion) | data formatting | bytes 81920 | tf_op jit(solution)/shard_map/mul | solution.py:562
  27.6 1.1 %copy.18 = f32[5,128,16]{1,0,2:T(8,128)S(1)} copy(f32[5,128,16]{2,1,0:T(8,128)} %mul.11) | data formatting | bytes 81920 | tf_op jit(solution)/shard_map/mul | solution.py:562
  28.8 0.0 copy-done.6
  28.8 0.6 gather_fusion
  29.4 9.1 %collective-permute-done.2.left_ref = f32[3,64,128]{2,1,0:T(8,128)} collective-permute-done((f32[3,64,128]{2,1,0:T(8,128)}, f32[3,64,128]{2,1,0:T(8,128)}, u32[]{:S(2)}, u32[]{:S(2)}) %collective-permute-start.2) | collective-permute-done | bytes 98336 | tf_op jit(solution)/shard_map/ppermute | solution.py:556
  38.6 0.0 collective-permute-done.3.right_ref
  38.6 0.0 collective-permute-done.low_ref
  38.6 0.0 collective-permute-done.1.high_ref
  38.6 3.9 %all-to-all-done.got_ref = f32[8,2,80,256]{3,2,1,0:T(8,128)S(1)} async-done(((f32[8,2,80,256]{3,2,1,0:T(8,128)}), f32[8,2,80,256]{3,2,1,0:T(8,128)S(1)}, u32[]{:S(2)}, u32[]{:S(2)}) %all-to-all-start) | async-done | bytes 1310752 | tf_op jit(solution)/shard_map/all_to_all | solution.py:552
  42.5 0.0 copy-done
  42.5 0.0 copy-done.1
  42.5 3.4 %modes.1 = f32[8,2,80,256]{3,2,1,0:T(8,128)} custom-call(s32[1]{0:T(128)S(6)} %copy.23.offset_ref, f32[8,2,80,256]{3,2,1,0:T(8,128)S(1)} %all-to-all-done.got_ref, f32[8,5,256]{2,1,0:T(8,128)S(1)} %copy.20.blend_ref, bf16[8,256,256]{2,1,0:T(8,128)(2,1)S(1)} %copy-done.1, bf16[8,256,256]{2,1,0:T(8,128)(2,1)S(1)} %copy-done), custom_call_target="tpu_custom_call" | custom-call | flops 503316480 | bytes 5000000 | tf_op jit(solution)/shard_map/modes/pallas_call | solution.py:142
  45.9 4.0 %all-to-all-start.1 = ((f32[8,2,80,256]{3,2,1,0:T(8,128)}), f32[8,2,80,256]{3,2,1,0:T(8,128)S(1)}, u32[]{:S(2)}, u32[]{:S(2)}) async-start(f32[8,2,80,256]{3,2,1,0:T(8,128)} %modes.1), calls=%async_computation.1 | async-start | bytes 2621440 | tf_op jit(solution)/shard_map/all_to_all | solution.py:568
  49.9 0.0 copy-start.2
  49.9 0.0 copy-start.3
  49.9 29.4 %stencil.1 = (f32[5,16,64,256]{3,2,1,0:T(8,128)}, f32[5,16,64,256]{3,2,1,0:T(8,128)}) custom-call(f32[75]{0:T(128)} %reshape.23.jac_ref, f32[5,5]{1,0:T(8,128)} %mix_ref.3, f32[5,16,64,256]{3,2,1,0:T(8,128)} %stator_hbm.1, f32[5,16,64,256]{3,2,1,0:T(8,128)} %rotor_hbm.1, f32[2,16,5,2,256]{4,3,2,1,0:T(2,128)} %collective-permute-done.low_ref, ...), custom_call_target="tpu_custom_call" | custom-call | flops 157286400 | bytes 41943040 | tf_op jit(solution)/shard_map/stencil/pallas_call | solution.py:440
  79.3 2.1 %all-to-all-done.1 = f32[8,2,80,256]{3,2,1,0:T(8,128)S(1)} async-done(((f32[8,2,80,256]{3,2,1,0:T(8,128)}), f32[8,2,80,256]{3,2,1,0:T(8,128)S(1)}, u32[]{:S(2)}, u32[]{:S(2)}) %all-to-all-start.1) | async-done | bytes 1310752 | tf_op jit(solution)/shard_map/all_to_all | solution.py:568
  81.4 0.0 copy-done.2
  81.4 0.0 copy-done.3
  81.4 3.2 %interface.1 = (f32[5,16,64,256]{3,2,1,0:T(8,128)}, f32[5,16,64,256]{3,2,1,0:T(8,128)}) custom-call(f32[75]{0:T(128)S(1)} %copy-done.3, f32[5,5]{1,0:T(8,128)S(1)} %copy-done.2, f32[8,2,5,2,8,256]{5,4,3,2,1,0:T(8,128)S(1)} %bitcast.8, f32[5,16,64,256]{3,2,1,0:T(8,128)} %get-tuple-element.42.stator_ref, ...), custom_call_target="tpu_custom_call", output_to_operand_aliasing={{0}: (3, {}), {1}: (4, {})} | custom-call | flops 9830400 | bytes 3932160 | tf_op jit(solution)/shard_map/interface/pallas_call | solution.py:528
  (6 shorter events, 0.1 us)
Async XLA Ops:
  2.8 39.7 %all-to-all-start = ((f32[8,2,80,256]{3,2,1,0:T(8,128)}), f32[8,2,80,256]{3,2,1,0:T(8,128)S(1)}, u32[]{:S(2)}, u32[]{:S(2)}) async-start(f32[8,2,80,256]{3,2,1,0:T(8,128)} %bitcast.9), calls=%async_computation | async-start | bytes 2621440 | tf_op jit(solution)/shard_map/all_to_all | solution.py:552
  10.1 15.4 %copy-start.4 = (f32[5,2048]{1,0:T(8,128)S(1)}, f32[5,2048]{1,0:T(8,128)}, u32[]{:S(2)}) copy-start(f32[5,2048]{1,0:T(8,128)} %param.16) | copy-start | bytes 122884
  10.1 16.1 %copy-start.5 = (f32[3,5,5]{2,0,1:T(4,128)S(1)}, f32[3,5,5]{2,0,1:T(4,128)}, u32[]{:S(2)}) copy-start(f32[3,5,5]{2,0,1:T(4,128)} %param.14) | copy-start | bytes 904
  10.1 18.7 %copy-start.6 = (s32[16]{0:T(128)S(1)}, s32[16]{0:T(128)}, u32[]{:S(2)}) copy-start(s32[16]{0:T(128)} %constant.23) | copy-start | bytes 196
  10.1 32.4 %copy-start = (bf16[8,256,256]{2,1,0:T(8,128)(2,1)S(1)}, bf16[8,256,256]{2,1,0:T(8,128)(2,1)}, u32[]{:S(2)}) copy-start(bf16[8,256,256]{2,1,0:T(8,128)(2,1)} %constant.19.clone.low_ref) | copy-start | bytes 3145732
  10.1 32.4 %copy-start.1 = (bf16[8,256,256]{2,1,0:T(8,128)(2,1)S(1)}, bf16[8,256,256]{2,1,0:T(8,128)(2,1)}, u32[]{:S(2)}) copy-start(bf16[8,256,256]{2,1,0:T(8,128)(2,1)} %constant.18.clone.high_ref) | copy-start | bytes 3145732
  17.3 21.2 %collective-permute-start.2 = (f32[3,64,128]{2,1,0:T(8,128)}, f32[3,64,128]{2,1,0:T(8,128)}, u32[]{:S(2)}, u32[]{:S(2)}) collective-permute-start(f32[3,64,128]{2,1,0:T(8,128)} %get-tuple-element.28), channel_id=1, source_target_pairs={{0,4},{4,8},{8,12},{12,16},{16,20},{20,24},{24,28},{28,0},{1,5},{5... | collective-permute-start | bytes 294920 | tf_op jit(solution)/shard_map/ppermute | solution.py:556
  19.4 19.1 %collective-permute-start.3 = (f32[3,64,128]{2,1,0:T(8,128)}, f32[3,64,128]{2,1,0:T(8,128)}, u32[]{:S(2)}, u32[]{:S(2)}) collective-permute-start(f32[3,64,128]{2,1,0:T(8,128)} %get-tuple-element.29), channel_id=1, source_target_pairs={{4,0},{8,4},{12,8},{16,12},{20,16},{24,20},{28,24},{0,28},{5,1},{9... | collective-permute-start | bytes 294920 | tf_op jit(solution)/shard_map/ppermute | solution.py:557
  22.2 16.4 %collective-permute-start = (f32[2,16,5,2,256]{4,3,2,1,0:T(2,128)}, f32[2,16,5,2,256]{4,3,2,1,0:T(2,128)}, u32[]{:S(2)}, u32[]{:S(2)}) collective-permute-start(f32[2,16,5,2,256]{4,3,2,1,0:T(2,128)} %get-tuple-element.26), channel_id=1, source_target_pairs={{0,1},{1,2},{2,3},{4,5},{5,6},{6,7},{8,9},{9,10},{10,11},{12,13},{... | collective-permute-start | bytes 983048 | tf_op jit(solution)/shard_map/ppermute | solution.py:558
  24.2 14.4 %collective-permute-start.1 = (f32[2,16,5,2,256]{4,3,2,1,0:T(2,128)}, f32[2,16,5,2,256]{4,3,2,1,0:T(2,128)}, u32[]{:S(2)}, u32[]{:S(2)}) collective-permute-start(f32[2,16,5,2,256]{4,3,2,1,0:T(2,128)} %get-tuple-element.27), channel_id=1, source_target_pairs={{1,0},{2,1},{3,2},{5,4},{6,5},{7,6},{9,8},{10,9},{11,10},{13,12},{... | collective-permute-start | bytes 983048 | tf_op jit(solution)/shard_map/ppermute | solution.py:559
  45.9 35.5 %all-to-all-start.1 = ((f32[8,2,80,256]{3,2,1,0:T(8,128)}), f32[8,2,80,256]{3,2,1,0:T(8,128)S(1)}, u32[]{:S(2)}, u32[]{:S(2)}) async-start(f32[8,2,80,256]{3,2,1,0:T(8,128)} %modes.1), calls=%async_computation.1 | async-start | bytes 2621440 | tf_op jit(solution)/shard_map/all_to_all | solution.py:568
  49.9 31.6 %copy-start.2 = (f32[5,5]{1,0:T(8,128)S(1)}, f32[5,5]{1,0:T(8,128)}, u32[]{:S(2)}) copy-start(f32[5,5]{1,0:T(8,128)} %mix_ref.3) | copy-start | bytes 304
  49.9 31.6 %copy-start.3 = (f32[75]{0:T(128)S(1)}, f32[75]{0:T(128)}, u32[]{:S(2)}) copy-start(f32[75]{0:T(128)} %reshape.23.jac_ref) | copy-start | bytes 904

commit v9 on v8

--- a/solution.py
+++ b/solution.py
@@ -75,7 +75,9 @@
     dot = functools.partial(
         lax.dot_general, dimension_numbers=(dims, ((), ())), preferred_element_type=jnp.float32
     )
-    return dot(x_high, high) + (dot(x_low, high) + dot(x_high, low))
+    rows = x.shape[0]
+    both = dot(jnp.concatenate([x_high, x_low], axis=0), high)
+    return both[:rows] + (both[rows:] + dot(x_high, low))
 
 
 def transform_kernel(fields, offset_ref, got_ref, blend_ref, high_ref, low_ref, out_ref, turn, work):
@@ -496,23 +498,20 @@
     for side, piece in order:
         near, far = (1, 0) if side == 0 else (0, 1)
         sign = -1.0 if side else 1.0
+
+        def plane(g, ghost):
+            return modes_ref[piece * group : (piece + 1) * group, side, g, ghost].reshape(height, cols)
+
+        planes = [plane(g, 0) for g in range(fields)]
+        first = [combine(lambda g: mix_ref[f, g], planes) for f in range(fields)]
         fetch(side, piece).wait()
-        for q in range(group):
-            span = slice(q * step, (q + 1) * step)
-            ghosts = []
-            for ghost in range(2):
-                planes = [modes_ref[piece * group + q, side, g, ghost] for g in range(fields)]
-                ghosts.append([combine(lambda g: mix_ref[f, g], planes) for f in range(fields)])
-            first, second = ghosts
-            for f in range(fields):
-                slope = combine(lambda g: jac_ref[f * fields + g], first) * (-0.5 * time_step)
-                bend = first[f] * 4.0 - second[f]
-                after[piece, side, f, near, span, :] = before[piece, side, f, near, span, :] + (
-                    slope + bend * (sign * scale)
-                )
-                after[piece, side, f, far, span, :] = before[piece, side, f, far, span, :] - first[f] * (
-                    sign * scale
-                )
+        planes = [plane(g, 1) for g in range(fields)]
+        for f in range(fields):
+            second = combine(lambda g: mix_ref[f, g], planes)
+            slope = combine(lambda g: jac_ref[f * fields + g], first) * (-0.5 * time_step)
+            bend = first[f] * 4.0 - second
+            after[piece, side, f, near] = before[piece, side, f, near] + (slope + bend * (sign * scale))
+            after[piece, side, f, far] = before[piece, side, f, far] - first[f] * (sign * scale)
         store(side, piece).start()
     for side, piece in order:
         store(side, piece).wait()

time: 85.1 us -> 84.9 us (level)
  no operation moved by 1% of the time
where the time goes in v9:
time: 84.9 us; the launch traced here: 84.4 us
  Pallas kernels  45.2 us (53%)
  starting transfers between devices  19.4 us (23%)
  waiting for transfers between devices  15.2 us (18%)
  local copies, waits for them, and re-layouts  3.27 us (4%)
  between operations  1.43 us (2%)
    pallas_call x1, Pallas kernels, stencil(): pl.pallas_call(functools.partial(stencil_kernel, layers), grid=(2 * steps...  29.4 us
    ppermute x1, waiting for transfers between devices, shards(): from_left = lax.ppermute(right, 'pitch', ring)  9.1 us
    all_to_all x1, starting transfers between devices, shards(): received = lax.all_to_all(planes, 'pitch', 0, 0, tiled=True)  7.25 us
    pallas_call x1, Pallas kernels, pack_edges(): pl.pallas_call(pack_kernel, grid=(steps,), out_shape=(edge, edge, side, s...  7.21 us
    all_to_all x1, starting transfers between devices, shards(): modes = lax.all_to_all(sent, 'pitch', 0, 0, tiled=True)  3.99 us
    all_to_all x1, waiting for transfers between devices, shards(): received = lax.all_to_all(planes, 'pitch', 0, 0, tiled=True)  3.95 us
    pallas_call x1, Pallas kernels, close(): pl.pallas_call(close_kernel, out_shape=(shape, shape), in_specs=[smem, sm...  3.23 us
    pallas_call x1, Pallas kernels, transform(): pl.pallas_call(functools.partial(transform_kernel, fields), out_shape=jax...  3.12 us
  transfers between devices with their start and end apart: 6, of which 3 were waited for; matrix products, arithmetic and copies ran while one was open for 4% of the time, Pallas kernels for 43%

profile of v9, /device:TPU:0, one launch (start us, length us, event | category | flops | bytes accessed | tf_op | source)
XLA Modules:
  0.0 84.4 jit_solution(1328362895112654755)
XLA Ops:
  0.6 2.2 %planes.1 = f32[8,2,5,2,8,256]{5,4,3,2,1,0:T(8,128)} custom-call(f32[5,16,64,256]{3,2,1,0:T(8,128)} %stator_hbm.1, f32[5,16,64,256]{3,2,1,0:T(8,128)} %rotor_hbm.1), custom_call_target="tpu_custom_call" | custom-call | tf_op jit(solution)/shard_map/planes/pallas_call | solution.py:175
  2.8 7.3 %all-to-all-start = ((f32[8,2,80,256]{3,2,1,0:T(8,128)}), f32[8,2,80,256]{3,2,1,0:T(8,128)S(1)}, u32[]{:S(2)}, u32[]{:S(2)}) async-start(f32[8,2,80,256]{3,2,1,0:T(8,128)} %bitcast.9), calls=%async_computation | async-start | bytes 2621440 | tf_op jit(solution)/shard_map/all_to_all | solution.py:551
  10.1 0.0 copy-start.4
  10.1 0.0 copy-start.5
  10.1 0.0 copy-start.6
  10.1 0.0 copy-start
  10.1 0.0 copy-start.1
  10.1 7.2 %edges.1 = (f32[2,16,5,2,256]{4,3,2,1,0:T(2,128)}, f32[2,16,5,2,256]{4,3,2,1,0:T(2,128)}, f32[3,64,128]{2,1,0:T(8,128)}, f32[3,64,128]{2,1,0:T(8,128)}) custom-call(f32[5,16,64,256]{3,2,1,0:T(8,128)} %stator_hbm.1, f32[5,16,64,256]{3,2,1,0:T(8,128)} %rotor_hbm.1), custom_call_target="tpu_custom_call" | custom-call | bytes 10485760 | tf_op jit(solution)/shard_map/edges/pallas_call | solution.py:225
  17.3 2.1 %collective-permute-start.2 = (f32[3,64,128]{2,1,0:T(8,128)}, f32[3,64,128]{2,1,0:T(8,128)}, u32[]{:S(2)}, u32[]{:S(2)}) collective-permute-start(f32[3,64,128]{2,1,0:T(8,128)} %get-tuple-element.28), channel_id=1, source_target_pairs={{0,4},{4,8},{8,12},{12,16},{16,20},{20,24},{24,28},{28,0},{1,5},{5... | collective-permute-start | bytes 294920 | tf_op jit(solution)/shard_map/ppermute | solution.py:555
  19.4 2.8 %collective-permute-start.3 = (f32[3,64,128]{2,1,0:T(8,128)}, f32[3,64,128]{2,1,0:T(8,128)}, u32[]{:S(2)}, u32[]{:S(2)}) collective-permute-start(f32[3,64,128]{2,1,0:T(8,128)} %get-tuple-element.29), channel_id=1, source_target_pairs={{4,0},{8,4},{12,8},{16,12},{20,16},{24,20},{28,24},{0,28},{5,1},{9... | collective-permute-start | bytes 294920 | tf_op jit(solution)/shard_map/ppermute | solution.py:556
  22.2 2.0 %collective-permute-start = (f32[2,16,5,2,256]{4,3,2,1,0:T(2,128)}, f32[2,16,5,2,256]{4,3,2,1,0:T(2,128)}, u32[]{:S(2)}, u32[]{:S(2)}) collective-permute-start(f32[2,16,5,2,256]{4,3,2,1,0:T(2,128)} %get-tuple-element.26), channel_id=1, source_target_pairs={{0,1},{1,2},{2,3},{4,5},{5,6},{6,7},{8,9},{9,10},{10,11},{12,13},{... | collective-permute-start | bytes 983048 | tf_op jit(solution)/shard_map/ppermute | solution.py:557
  24.2 1.3 %collective-permute-start.1 = (f32[2,16,5,2,256]{4,3,2,1,0:T(2,128)}, f32[2,16,5,2,256]{4,3,2,1,0:T(2,128)}, u32[]{:S(2)}, u32[]{:S(2)}) collective-permute-start(f32[2,16,5,2,256]{4,3,2,1,0:T(2,128)} %get-tuple-element.27), channel_id=1, source_target_pairs={{1,0},{2,1},{3,2},{5,4},{6,5},{7,6},{9,8},{10,9},{11,10},{13,12},{... | collective-permute-start | bytes 983048 | tf_op jit(solution)/shard_map/ppermute | solution.py:558
  25.5 0.0 copy-done.4
  26.1 0.0 copy-done.5
  26.2 0.6 reshape.23.jac_ref
  26.8 0.9 %mul.11 = f32[5,128,16]{2,1,0:T(8,128)} reshape(f32[5,2048]{1,0:T(8,128)S(1)} %broadcast_multiply_fusion) | data formatting | bytes 81920 | tf_op jit(solution)/shard_map/mul | solution.py:561
  27.6 1.1 %copy.18 = f32[5,128,16]{1,0,2:T(8,128)S(1)} copy(f32[5,128,16]{2,1,0:T(8,128)} %mul.11) | data formatting | bytes 81920 | tf_op jit(solution)/shard_map/mul | solution.py:561
  28.8 0.0 copy-done.6
  28.8 0.6 gather_fusion
  29.4 9.1 %collective-permute-done.2.left_ref = f32[3,64,128]{2,1,0:T(8,128)} collective-permute-done((f32[3,64,128]{2,1,0:T(8,128)}, f32[3,64,128]{2,1,0:T(8,128)}, u32[]{:S(2)}, u32[]{:S(2)}) %collective-permute-start.2) | collective-permute-done | bytes 98336 | tf_op jit(solution)/shard_map/ppermute | solution.py:555
  38.6 0.0 collective-permute-done.3.right_ref
  38.6 0.0 collective-permute-done.low_ref
  38.6 0.0 collective-permute-done.1.high_ref
  38.6 3.9 %all-to-all-done.got_ref = f32[8,2,80,256]{3,2,1,0:T(8,128)S(1)} async-done(((f32[8,2,80,256]{3,2,1,0:T(8,128)}), f32[8,2,80,256]{3,2,1,0:T(8,128)S(1)}, u32[]{:S(2)}, u32[]{:S(2)}) %all-to-all-start) | async-done | bytes 1310752 | tf_op jit(solution)/shard_map/all_to_all | solution.py:551
  42.5 0.0 copy-done
  42.5 0.0 copy-done.1
  42.5 3.1 %modes.1 = f32[8,2,80,256]{3,2,1,0:T(8,128)} custom-call(s32[1]{0:T(128)S(6)} %copy.23.offset_ref, f32[8,2,80,256]{3,2,1,0:T(8,128)S(1)} %all-to-all-done.got_ref, f32[8,5,256]{2,1,0:T(8,128)S(1)} %copy.20.blend_ref, bf16[8,256,256]{2,1,0:T(8,128)(2,1)S(1)} %copy-done.1, bf16[8,256,256]{2,1,0:T(8,128)(2,1)S(1)} %copy-done), custom_call_target="tpu_custom_call" | custom-call | flops 503316480 | bytes 5000000 | tf_op jit(solution)/shard_map/modes/pallas_call | solution.py:144
  45.6 4.0 %all-to-all-start.1 = ((f32[8,2,80,256]{3,2,1,0:T(8,128)}), f32[8,2,80,256]{3,2,1,0:T(8,128)S(1)}, u32[]{:S(2)}, u32[]{:S(2)}) async-start(f32[8,2,80,256]{3,2,1,0:T(8,128)} %modes.1), calls=%async_computation.1 | async-start | bytes 2621440 | tf_op jit(solution)/shard_map/all_to_all | solution.py:567
  49.6 0.0 copy-start.2
  49.6 0.0 copy-start.3
  49.6 29.4 %stencil.1 = (f32[5,16,64,256]{3,2,1,0:T(8,128)}, f32[5,16,64,256]{3,2,1,0:T(8,128)}) custom-call(f32[75]{0:T(128)} %reshape.23.jac_ref, f32[5,5]{1,0:T(8,128)} %mix_ref.3, f32[5,16,64,256]{3,2,1,0:T(8,128)} %stator_hbm.1, f32[5,16,64,256]{3,2,1,0:T(8,128)} %rotor_hbm.1, f32[2,16,5,2,256]{4,3,2,1,0:T(2,128)} %collective-permute-done.low_ref, ...), custom_call_target="tpu_custom_call" | custom-call | flops 157286400 | bytes 41943040 | tf_op jit(solution)/shard_map/stencil/pallas_call | solution.py:442
  79.1 2.1 %all-to-all-done.1 = f32[8,2,80,256]{3,2,1,0:T(8,128)S(1)} async-done(((f32[8,2,80,256]{3,2,1,0:T(8,128)}), f32[8,2,80,256]{3,2,1,0:T(8,128)S(1)}, u32[]{:S(2)}, u32[]{:S(2)}) %all-to-all-start.1) | async-done | bytes 1310752 | tf_op jit(solution)/shard_map/all_to_all | solution.py:567
  81.2 0.0 copy-done.2
  81.2 0.0 copy-done.3
  81.2 3.2 %interface.1 = (f32[5,16,64,256]{3,2,1,0:T(8,128)}, f32[5,16,64,256]{3,2,1,0:T(8,128)}) custom-call(f32[75]{0:T(128)S(1)} %copy-done.3, f32[5,5]{1,0:T(8,128)S(1)} %copy-done.2, f32[8,2,5,2,8,256]{5,4,3,2,1,0:T(8,128)S(1)} %bitcast.8, f32[5,16,64,256]{3,2,1,0:T(8,128)} %get-tuple-element.42.stator_ref, ...), custom_call_target="tpu_custom_call", output_to_operand_aliasing={{0}: (3, {}), {1}: (4, {})} | custom-call | flops 9830400 | bytes 3932160 | tf_op jit(solution)/shard_map/interface/pallas_call | solution.py:527
  (6 shorter events, 0.1 us)
Async XLA Ops:
  2.8 39.7 %all-to-all-start = ((f32[8,2,80,256]{3,2,1,0:T(8,128)}), f32[8,2,80,256]{3,2,1,0:T(8,128)S(1)}, u32[]{:S(2)}, u32[]{:S(2)}) async-start(f32[8,2,80,256]{3,2,1,0:T(8,128)} %bitcast.9), calls=%async_computation | async-start | bytes 2621440 | tf_op jit(solution)/shard_map/all_to_all | solution.py:551
  10.1 15.4 %copy-start.4 = (f32[5,2048]{1,0:T(8,128)S(1)}, f32[5,2048]{1,0:T(8,128)}, u32[]{:S(2)}) copy-start(f32[5,2048]{1,0:T(8,128)} %param.16) | copy-start | bytes 122884
  10.1 16.1 %copy-start.5 = (f32[3,5,5]{2,0,1:T(4,128)S(1)}, f32[3,5,5]{2,0,1:T(4,128)}, u32[]{:S(2)}) copy-start(f32[3,5,5]{2,0,1:T(4,128)} %param.14) | copy-start | bytes 904
  10.1 18.7 %copy-start.6 = (s32[16]{0:T(128)S(1)}, s32[16]{0:T(128)}, u32[]{:S(2)}) copy-start(s32[16]{0:T(128)} %constant.23) | copy-start | bytes 196
  10.1 32.4 %copy-start = (bf16[8,256,256]{2,1,0:T(8,128)(2,1)S(1)}, bf16[8,256,256]{2,1,0:T(8,128)(2,1)}, u32[]{:S(2)}) copy-start(bf16[8,256,256]{2,1,0:T(8,128)(2,1)} %constant.19.clone.low_ref) | copy-start | bytes 3145732
  10.1 32.4 %copy-start.1 = (bf16[8,256,256]{2,1,0:T(8,128)(2,1)S(1)}, bf16[8,256,256]{2,1,0:T(8,128)(2,1)}, u32[]{:S(2)}) copy-start(bf16[8,256,256]{2,1,0:T(8,128)(2,1)} %constant.18.clone.high_ref) | copy-start | bytes 3145732
  17.3 21.2 %collective-permute-start.2 = (f32[3,64,128]{2,1,0:T(8,128)}, f32[3,64,128]{2,1,0:T(8,128)}, u32[]{:S(2)}, u32[]{:S(2)}) collective-permute-start(f32[3,64,128]{2,1,0:T(8,128)} %get-tuple-element.28), channel_id=1, source_target_pairs={{0,4},{4,8},{8,12},{12,16},{16,20},{20,24},{24,28},{28,0},{1,5},{5... | collective-permute-start | bytes 294920 | tf_op jit(solution)/shard_map/ppermute | solution.py:555
  19.4 19.1 %collective-permute-start.3 = (f32[3,64,128]{2,1,0:T(8,128)}, f32[3,64,128]{2,1,0:T(8,128)}, u32[]{:S(2)}, u32[]{:S(2)}) collective-permute-start(f32[3,64,128]{2,1,0:T(8,128)} %get-tuple-element.29), channel_id=1, source_target_pairs={{4,0},{8,4},{12,8},{16,12},{20,16},{24,20},{28,24},{0,28},{5,1},{9... | collective-permute-start | bytes 294920 | tf_op jit(solution)/shard_map/ppermute | solution.py:556
  22.2 16.4 %collective-permute-start = (f32[2,16,5,2,256]{4,3,2,1,0:T(2,128)}, f32[2,16,5,2,256]{4,3,2,1,0:T(2,128)}, u32[]{:S(2)}, u32[]{:S(2)}) collective-permute-start(f32[2,16,5,2,256]{4,3,2,1,0:T(2,128)} %get-tuple-element.26), channel_id=1, source_target_pairs={{0,1},{1,2},{2,3},{4,5},{5,6},{6,7},{8,9},{9,10},{10,11},{12,13},{... | collective-permute-start | bytes 983048 | tf_op jit(solution)/shard_map/ppermute | solution.py:557
  24.2 14.4 %collective-permute-start.1 = (f32[2,16,5,2,256]{4,3,2,1,0:T(2,128)}, f32[2,16,5,2,256]{4,3,2,1,0:T(2,128)}, u32[]{:S(2)}, u32[]{:S(2)}) collective-permute-start(f32[2,16,5,2,256]{4,3,2,1,0:T(2,128)} %get-tuple-element.27), channel_id=1, source_target_pairs={{1,0},{2,1},{3,2},{5,4},{6,5},{7,6},{9,8},{10,9},{11,10},{13,12},{... | collective-permute-start | bytes 983048 | tf_op jit(solution)/shard_map/ppermute | solution.py:558
  45.6 35.5 %all-to-all-start.1 = ((f32[8,2,80,256]{3,2,1,0:T(8,128)}), f32[8,2,80,256]{3,2,1,0:T(8,128)S(1)}, u32[]{:S(2)}, u32[]{:S(2)}) async-start(f32[8,2,80,256]{3,2,1,0:T(8,128)} %modes.1), calls=%async_computation.1 | async-start | bytes 2621440 | tf_op jit(solution)/shard_map/all_to_all | solution.py:567
  49.6 31.6 %copy-start.2 = (f32[5,5]{1,0:T(8,128)S(1)}, f32[5,5]{1,0:T(8,128)}, u32[]{:S(2)}) copy-start(f32[5,5]{1,0:T(8,128)} %mix_ref.3) | copy-start | bytes 304
  49.6 31.6 %copy-start.3 = (f32[75]{0:T(128)S(1)}, f32[75]{0:T(128)}, u32[]{:S(2)}) copy-start(f32[75]{0:T(128)} %reshape.23.jac_ref) | copy-start | bytes 904

commit v10 on v9

--- a/solution.py
+++ b/solution.py
@@ -167,9 +167,48 @@
             out[q, 1, :, ghost] = rotor[:, ghost, span, :]
 
 
+def planes_copy_kernel(stator, rotor, out, held, sems, stores):
+    count, _, _, _, step, _ = out.shape
+    layers = stator.shape[1]
+
+    def load(side, ghost):
+        source = stator.at[:, layers - 1 - ghost] if side == 0 else rotor.at[:, ghost]
+        return pltpu.make_async_copy(source, held.at[side, ghost], sems.at[side, ghost])
+
+    def store(side, ghost, q):
+        source = held.at[side, ghost, :, pl.ds(q * step, step)]
+        return pltpu.make_async_copy(source, out.at[q, side, :, ghost], stores.at[side, ghost, q])
+
+    order = [(side, ghost) for side in range(2) for ghost in range(2)]
+    for plane in order:
+        load(*plane).start()
+    for plane in order:
+        load(*plane).wait()
+        for q in range(count):
+            store(*plane, q).start()
+    for plane in order:
+        for q in range(count):
+            store(*plane, q).wait()
+
+
 def interface_planes(stator, rotor, count):
     fields, layers, rows, cols = stator.shape
     step = rows // count
+    if step % 8 == 0:
+        hbm = pl.BlockSpec(memory_space=pl.ANY)
+        return pl.pallas_call(
+            planes_copy_kernel,
+            out_shape=jax.ShapeDtypeStruct((count, 2, fields, 2, step, cols), jnp.float32),
+            in_specs=[hbm, hbm],
+            out_specs=hbm,
+            scratch_shapes=[
+                pltpu.VMEM((2, 2, fields, rows, cols), jnp.float32),
+                pltpu.SemaphoreType.DMA((2, 2)),
+                pltpu.SemaphoreType.DMA((2, 2, count)),
+            ],
+            compiler_params=pltpu.CompilerParams(vmem_limit_bytes=WIDE),
+            name="planes",
+        )(stator, rotor)
     group = max(1, count // 2)
     block = (fields, 2, group * step, cols)
     return pl.pallas_call(

time: 84.9 us -> 85 us (level)
  no operation moved by 1% of the time
where the time goes in v10:
time: 85 us; the launch traced here: 84.6 us
  Pallas kernels  45.3 us (53%)
  starting transfers between devices  19.4 us (23%)
  waiting for transfers between devices  15.2 us (18%)
  local copies, waits for them, and re-layouts  3.27 us (4%)
  between operations  1.44 us (2%)
    pallas_call x1, Pallas kernels, stencil(): pl.pallas_call(functools.partial(stencil_kernel, layers), grid=(2 * steps...  29.4 us
    ppermute x1, waiting for transfers between devices, shards(): from_left = lax.ppermute(right, 'pitch', ring)  9.1 us
    all_to_all x1, starting transfers between devices, shards(): received = lax.all_to_all(planes, 'pitch', 0, 0, tiled=True)  7.26 us
    pallas_call x1, Pallas kernels, pack_edges(): pl.pallas_call(pack_kernel, grid=(steps,), out_shape=(edge, edge, side, s...  7.21 us
    all_to_all x1, starting transfers between devices, shards(): modes = lax.all_to_all(sent, 'pitch', 0, 0, tiled=True)  3.98 us
    all_to_all x1, waiting for transfers between devices, shards(): received = lax.all_to_all(planes, 'pitch', 0, 0, tiled=True)  3.95 us
    pallas_call x1, Pallas kernels, close(): pl.pallas_call(close_kernel, out_shape=(shape, shape), in_specs=[smem, sm...  3.23 us
    pallas_call x1, Pallas kernels, transform(): pl.pallas_call(functools.partial(transform_kernel, fields), out_shape=jax...  3.13 us
  transfers between devices with their start and end apart: 6, of which 3 were waited for; matrix products, arithmetic and copies ran while one was open for 4% of the time, Pallas kernels for 43%

profile of v10, /device:TPU:0, one launch (start us, length us, event | category | flops | bytes accessed | tf_op | source)
XLA Modules:
  0.0 84.6 jit_solution(4110851797486674831)
XLA Ops:
  0.6 2.3 %planes.1 = f32[8,2,5,2,8,256]{5,4,3,2,1,0:T(8,128)} custom-call(f32[5,16,64,256]{3,2,1,0:T(8,128)} %stator_hbm.1, f32[5,16,64,256]{3,2,1,0:T(8,128)} %rotor_hbm.1), custom_call_target="tpu_custom_call" | custom-call | tf_op jit(solution)/shard_map/planes/pallas_call | solution.py:199
  3.0 7.3 %all-to-all-start = ((f32[8,2,80,256]{3,2,1,0:T(8,128)}), f32[8,2,80,256]{3,2,1,0:T(8,128)S(1)}, u32[]{:S(2)}, u32[]{:S(2)}) async-start(f32[8,2,80,256]{3,2,1,0:T(8,128)} %bitcast.9), calls=%async_computation | async-start | bytes 2621440 | tf_op jit(solution)/shard_map/all_to_all | solution.py:590
  10.2 0.0 copy-start.4
  10.2 0.0 copy-start.5
  10.2 0.0 copy-start.6
  10.3 0.0 copy-start
  10.3 0.0 copy-start.1
  10.3 7.2 %edges.1 = (f32[2,16,5,2,256]{4,3,2,1,0:T(2,128)}, f32[2,16,5,2,256]{4,3,2,1,0:T(2,128)}, f32[3,64,128]{2,1,0:T(8,128)}, f32[3,64,128]{2,1,0:T(8,128)}) custom-call(f32[5,16,64,256]{3,2,1,0:T(8,128)} %stator_hbm.1, f32[5,16,64,256]{3,2,1,0:T(8,128)} %rotor_hbm.1), custom_call_target="tpu_custom_call" | custom-call | bytes 10485760 | tf_op jit(solution)/shard_map/edges/pallas_call | solution.py:264
  17.5 2.1 %collective-permute-start.2 = (f32[3,64,128]{2,1,0:T(8,128)}, f32[3,64,128]{2,1,0:T(8,128)}, u32[]{:S(2)}, u32[]{:S(2)}) collective-permute-start(f32[3,64,128]{2,1,0:T(8,128)} %get-tuple-element.28), channel_id=1, source_target_pairs={{0,4},{4,8},{8,12},{12,16},{16,20},{20,24},{24,28},{28,0},{1,5},{5... | collective-permute-start | bytes 294920 | tf_op jit(solution)/shard_map/ppermute | solution.py:594
  19.6 2.8 %collective-permute-start.3 = (f32[3,64,128]{2,1,0:T(8,128)}, f32[3,64,128]{2,1,0:T(8,128)}, u32[]{:S(2)}, u32[]{:S(2)}) collective-permute-start(f32[3,64,128]{2,1,0:T(8,128)} %get-tuple-element.29), channel_id=1, source_target_pairs={{4,0},{8,4},{12,8},{16,12},{20,16},{24,20},{28,24},{0,28},{5,1},{9... | collective-permute-start | bytes 294920 | tf_op jit(solution)/shard_map/ppermute | solution.py:595
  22.3 2.0 %collective-permute-start = (f32[2,16,5,2,256]{4,3,2,1,0:T(2,128)}, f32[2,16,5,2,256]{4,3,2,1,0:T(2,128)}, u32[]{:S(2)}, u32[]{:S(2)}) collective-permute-start(f32[2,16,5,2,256]{4,3,2,1,0:T(2,128)} %get-tuple-element.26), channel_id=1, source_target_pairs={{0,1},{1,2},{2,3},{4,5},{5,6},{6,7},{8,9},{9,10},{10,11},{12,13},{... | collective-permute-start | bytes 983048 | tf_op jit(solution)/shard_map/ppermute | solution.py:596
  24.3 1.3 %collective-permute-start.1 = (f32[2,16,5,2,256]{4,3,2,1,0:T(2,128)}, f32[2,16,5,2,256]{4,3,2,1,0:T(2,128)}, u32[]{:S(2)}, u32[]{:S(2)}) collective-permute-start(f32[2,16,5,2,256]{4,3,2,1,0:T(2,128)} %get-tuple-element.27), channel_id=1, source_target_pairs={{1,0},{2,1},{3,2},{5,4},{6,5},{7,6},{9,8},{10,9},{11,10},{13,12},{... | collective-permute-start | bytes 983048 | tf_op jit(solution)/shard_map/ppermute | solution.py:597
  25.6 0.0 copy-done.4
  26.3 0.0 copy-done.5
  26.3 0.6 reshape.23.jac_ref
  26.9 0.9 %mul.11 = f32[5,128,16]{2,1,0:T(8,128)} reshape(f32[5,2048]{1,0:T(8,128)S(1)} %broadcast_multiply_fusion) | data formatting | bytes 81920 | tf_op jit(solution)/shard_map/mul | solution.py:600
  27.8 1.1 %copy.18 = f32[5,128,16]{1,0,2:T(8,128)S(1)} copy(f32[5,128,16]{2,1,0:T(8,128)} %mul.11) | data formatting | bytes 81920 | tf_op jit(solution)/shard_map/mul | solution.py:600
  28.9 0.0 copy-done.6
  28.9 0.6 gather_fusion
  29.6 9.1 %collective-permute-done.2.left_ref = f32[3,64,128]{2,1,0:T(8,128)} collective-permute-done((f32[3,64,128]{2,1,0:T(8,128)}, f32[3,64,128]{2,1,0:T(8,128)}, u32[]{:S(2)}, u32[]{:S(2)}) %collective-permute-start.2) | collective-permute-done | bytes 98336 | tf_op jit(solution)/shard_map/ppermute | solution.py:594
  38.7 0.0 collective-permute-done.3.right_ref
  38.7 0.0 collective-permute-done.low_ref
  38.7 0.0 collective-permute-done.1.high_ref
  38.7 3.9 %all-to-all-done.got_ref = f32[8,2,80,256]{3,2,1,0:T(8,128)S(1)} async-done(((f32[8,2,80,256]{3,2,1,0:T(8,128)}), f32[8,2,80,256]{3,2,1,0:T(8,128)S(1)}, u32[]{:S(2)}, u32[]{:S(2)}) %all-to-all-start) | async-done | bytes 1310752 | tf_op jit(solution)/shard_map/all_to_all | solution.py:590
  42.7 0.0 copy-done
  42.7 0.0 copy-done.1
  42.7 3.1 %modes.1 = f32[8,2,80,256]{3,2,1,0:T(8,128)} custom-call(s32[1]{0:T(128)S(6)} %copy.23.offset_ref, f32[8,2,80,256]{3,2,1,0:T(8,128)S(1)} %all-to-all-done.got_ref, f32[8,5,256]{2,1,0:T(8,128)S(1)} %copy.20.blend_ref, bf16[8,256,256]{2,1,0:T(8,128)(2,1)S(1)} %copy-done.1, bf16[8,256,256]{2,1,0:T(8,128)(2,1)S(1)} %copy-done), custom_call_target="tpu_custom_call" | custom-call | flops 503316480 | bytes 5000000 | tf_op jit(solution)/shard_map/modes/pallas_call | solution.py:144
  45.8 4.0 %all-to-all-start.1 = ((f32[8,2,80,256]{3,2,1,0:T(8,128)}), f32[8,2,80,256]{3,2,1,0:T(8,128)S(1)}, u32[]{:S(2)}, u32[]{:S(2)}) async-start(f32[8,2,80,256]{3,2,1,0:T(8,128)} %modes.1), calls=%async_computation.1 | async-start | bytes 2621440 | tf_op jit(solution)/shard_map/all_to_all | solution.py:606
  49.8 0.0 copy-start.2
  49.8 0.0 copy-start.3
  49.8 29.4 %stencil.1 = (f32[5,16,64,256]{3,2,1,0:T(8,128)}, f32[5,16,64,256]{3,2,1,0:T(8,128)}) custom-call(f32[75]{0:T(128)} %reshape.23.jac_ref, f32[5,5]{1,0:T(8,128)} %mix_ref.3, f32[5,16,64,256]{3,2,1,0:T(8,128)} %stator_hbm.1, f32[5,16,64,256]{3,2,1,0:T(8,128)} %rotor_hbm.1, f32[2,16,5,2,256]{4,3,2,1,0:T(2,128)} %collective-permute-done.low_ref, ...), custom_call_target="tpu_custom_call" | custom-call | flops 157286400 | bytes 41943040 | tf_op jit(solution)/shard_map/stencil/pallas_call | solution.py:481
  79.2 2.1 %all-to-all-done.1 = f32[8,2,80,256]{3,2,1,0:T(8,128)S(1)} async-done(((f32[8,2,80,256]{3,2,1,0:T(8,128)}), f32[8,2,80,256]{3,2,1,0:T(8,128)S(1)}, u32[]{:S(2)}, u32[]{:S(2)}) %all-to-all-start.1) | async-done | bytes 1310752 | tf_op jit(solution)/shard_map/all_to_all | solution.py:606
  81.3 0.0 copy-done.2
  81.3 0.0 copy-done.3
  81.3 3.2 %interface.1 = (f32[5,16,64,256]{3,2,1,0:T(8,128)}, f32[5,16,64,256]{3,2,1,0:T(8,128)}) custom-call(f32[75]{0:T(128)S(1)} %copy-done.3, f32[5,5]{1,0:T(8,128)S(1)} %copy-done.2, f32[8,2,5,2,8,256]{5,4,3,2,1,0:T(8,128)S(1)} %bitcast.8, f32[5,16,64,256]{3,2,1,0:T(8,128)} %get-tuple-element.42.stator_ref, ...), custom_call_target="tpu_custom_call", output_to_operand_aliasing={{0}: (3, {}), {1}: (4, {})} | custom-call | flops 9830400 | bytes 3932160 | tf_op jit(solution)/shard_map/interface/pallas_call | solution.py:566
  (6 shorter events, 0.1 us)
Async XLA Ops:
  3.0 39.7 %all-to-all-start = ((f32[8,2,80,256]{3,2,1,0:T(8,128)}), f32[8,2,80,256]{3,2,1,0:T(8,128)S(1)}, u32[]{:S(2)}, u32[]{:S(2)}) async-start(f32[8,2,80,256]{3,2,1,0:T(8,128)} %bitcast.9), calls=%async_computation | async-start | bytes 2621440 | tf_op jit(solution)/shard_map/all_to_all | solution.py:590
  10.2 15.4 %copy-start.4 = (f32[5,2048]{1,0:T(8,128)S(1)}, f32[5,2048]{1,0:T(8,128)}, u32[]{:S(2)}) copy-start(f32[5,2048]{1,0:T(8,128)} %param.16) | copy-start | bytes 122884
  10.2 16.1 %copy-start.5 = (f32[3,5,5]{2,0,1:T(4,128)S(1)}, f32[3,5,5]{2,0,1:T(4,128)}, u32[]{:S(2)}) copy-start(f32[3,5,5]{2,0,1:T(4,128)} %param.14) | copy-start | bytes 904
  10.2 18.7 %copy-start.6 = (s32[16]{0:T(128)S(1)}, s32[16]{0:T(128)}, u32[]{:S(2)}) copy-start(s32[16]{0:T(128)} %constant.23) | copy-start | bytes 196
  10.3 32.4 %copy-start = (bf16[8,256,256]{2,1,0:T(8,128)(2,1)S(1)}, bf16[8,256,256]{2,1,0:T(8,128)(2,1)}, u32[]{:S(2)}) copy-start(bf16[8,256,256]{2,1,0:T(8,128)(2,1)} %constant.19.clone.low_ref) | copy-start | bytes 3145732
  10.3 32.4 %copy-start.1 = (bf16[8,256,256]{2,1,0:T(8,128)(2,1)S(1)}, bf16[8,256,256]{2,1,0:T(8,128)(2,1)}, u32[]{:S(2)}) copy-start(bf16[8,256,256]{2,1,0:T(8,128)(2,1)} %constant.18.clone.high_ref) | copy-start | bytes 3145732
  17.5 21.2 %collective-permute-start.2 = (f32[3,64,128]{2,1,0:T(8,128)}, f32[3,64,128]{2,1,0:T(8,128)}, u32[]{:S(2)}, u32[]{:S(2)}) collective-permute-start(f32[3,64,128]{2,1,0:T(8,128)} %get-tuple-element.28), channel_id=1, source_target_pairs={{0,4},{4,8},{8,12},{12,16},{16,20},{20,24},{24,28},{28,0},{1,5},{5... | collective-permute-start | bytes 294920 | tf_op jit(solution)/shard_map/ppermute | solution.py:594
  19.6 19.1 %collective-permute-start.3 = (f32[3,64,128]{2,1,0:T(8,128)}, f32[3,64,128]{2,1,0:T(8,128)}, u32[]{:S(2)}, u32[]{:S(2)}) collective-permute-start(f32[3,64,128]{2,1,0:T(8,128)} %get-tuple-element.29), channel_id=1, source_target_pairs={{4,0},{8,4},{12,8},{16,12},{20,16},{24,20},{28,24},{0,28},{5,1},{9... | collective-permute-start | bytes 294920 | tf_op jit(solution)/shard_map/ppermute | solution.py:595
  22.3 16.4 %collective-permute-start = (f32[2,16,5,2,256]{4,3,2,1,0:T(2,128)}, f32[2,16,5,2,256]{4,3,2,1,0:T(2,128)}, u32[]{:S(2)}, u32[]{:S(2)}) collective-permute-start(f32[2,16,5,2,256]{4,3,2,1,0:T(2,128)} %get-tuple-element.26), channel_id=1, source_target_pairs={{0,1},{1,2},{2,3},{4,5},{5,6},{6,7},{8,9},{9,10},{10,11},{12,13},{... | collective-permute-start | bytes 983048 | tf_op jit(solution)/shard_map/ppermute | solution.py:596
  24.3 14.4 %collective-permute-start.1 = (f32[2,16,5,2,256]{4,3,2,1,0:T(2,128)}, f32[2,16,5,2,256]{4,3,2,1,0:T(2,128)}, u32[]{:S(2)}, u32[]{:S(2)}) collective-permute-start(f32[2,16,5,2,256]{4,3,2,1,0:T(2,128)} %get-tuple-element.27), channel_id=1, source_target_pairs={{1,0},{2,1},{3,2},{5,4},{6,5},{7,6},{9,8},{10,9},{11,10},{13,12},{... | collective-permute-start | bytes 983048 | tf_op jit(solution)/shard_map/ppermute | solution.py:597
  45.8 35.5 %all-to-all-start.1 = ((f32[8,2,80,256]{3,2,1,0:T(8,128)}), f32[8,2,80,256]{3,2,1,0:T(8,128)S(1)}, u32[]{:S(2)}, u32[]{:S(2)}) async-start(f32[8,2,80,256]{3,2,1,0:T(8,128)} %modes.1), calls=%async_computation.1 | async-start | bytes 2621440 | tf_op jit(solution)/shard_map/all_to_all | solution.py:606
  49.8 31.6 %copy-start.2 = (f32[5,5]{1,0:T(8,128)S(1)}, f32[5,5]{1,0:T(8,128)}, u32[]{:S(2)}) copy-start(f32[5,5]{1,0:T(8,128)} %mix_ref.3) | copy-start | bytes 304
  49.8 31.6 %copy-start.3 = (f32[75]{0:T(128)S(1)}, f32[75]{0:T(128)}, u32[]{:S(2)}) copy-start(f32[75]{0:T(128)} %reshape.23.jac_ref) | copy-start | bytes 904
